TPU v7x, 32 devices: a whole 2x2x4 slice. The times are simulated.
32 devices in a mesh: dp: 4 (over y, x), ctx: 4 (over z), tensor: 2 (over core).
Axes of the slice: x: 2, y: 2, z: 4, core: 2. Of those that a mesh axis runs over, the one named last changes fastest.
Arguments:
- layer_input: bfloat16 [4096, 2048], P(('dp', 'ctx', 'tensor')), may hold values from -6 to 6
- segments: int32 [4096], P(('dp', 'ctx')), may hold values from 0 to 3, as said below
- attn_gain: bfloat16 [2048], P(('dp', 'ctx')), may hold values from 0.5 to 1.5
- query_weight: bfloat16 [2048, 2048], P(('dp', 'ctx'), 'tensor'), may hold values from -0.015625 to 0.015625
- key_weight: bfloat16 [2048, 2048], P(('dp', 'ctx'), 'tensor'), may hold values from -0.125 to 0.125
- value_weight: bfloat16 [2048, 2048], P(('dp', 'ctx'), 'tensor'), may hold values from -0.125 to 0.125
- output_weight: bfloat16 [2048, 2048], P('tensor', ('dp', 'ctx')), may hold values from -2 to 2
- bias_table: float32 [32, 32], P(None, 'tensor'), may hold values from -4 to 4
- ff_gain: bfloat16 [2048], P(('dp', 'ctx')), may hold values from 0.5 to 1.5
- gate_weight: bfloat16 [2048, 5120], P(('dp', 'ctx'), 'tensor'), may hold values from -0.125 to 0.125
- up_weight: bfloat16 [2048, 5120], P(('dp', 'ctx'), 'tensor'), may hold values from -0.125 to 0.125
- down_weight: bfloat16 [5120, 2048], P('tensor', ('dp', 'ctx')), may hold values from -0.078125 to 0.078125
- cotangent: bfloat16 [4096, 2048], P(('dp', 'ctx', 'tensor')), may hold values from -6 to 6
Outputs:
- block_output: bfloat16 [4096, 2048], P(('dp', 'ctx', 'tensor'))
- input_grads: bfloat16 [4096, 2048], P(('dp', 'ctx', 'tensor'))
- attn_gain_grads: float32 [2048], replicated
- query_grads: float32 [2048, 2048], P(('dp', 'ctx'), 'tensor')
- key_grads: float32 [2048, 2048], P(('dp', 'ctx'), 'tensor')
- value_grads: float32 [2048, 2048], P(('dp', 'ctx'), 'tensor')
- output_grads: float32 [2048, 2048], P('tensor', ('dp', 'ctx'))
- bias_grads: float32 [32, 32], replicated
- ff_gain_grads: float32 [2048], replicated
- gate_grads: float32 [2048, 5120], P(('dp', 'ctx'), 'tensor')
- up_grads: float32 [2048, 5120], P(('dp', 'ctx'), 'tensor')
- down_grads: float32 [5120, 2048], P('tensor', ('dp', 'ctx'))
- rms_stats: float32 [2], replicated
Inputs may be any that keep to these rules, and one draw needn't show every extreme that they name: `segments`: each sequence of 1024 tokens holds document 1, then document 2, then document 3, then padding 0; document 1 lies within the first 256 tokens, document 2 ends within the last 256 tokens, and every sequence ends with at least one padding token.
All inputs are finite; a program needn't handle non-finite values.
Results may differ from a plain program's by a relative error of at most 0.018.
Values may be sent and summed in bfloat16 or wider, within the bound.
No kernel may reach another device: no remote copies, remote signals or barrier semaphores. Data moves between devices by JAX's collectives and lax.ppermute only.
A program may use at most 256 MiB of HBM per device.

v0:
```python
import jax
import jax.numpy as jnp
from jax import lax
from jax.sharding import PartitionSpec as P

NB = 32


edge_list = (12, 16, 23, 32, 46, 64, 91)
exact_span = 8
eps = 1e-06
highest = lax.Precision.HIGHEST


def bucket_of(relative):
    distance = jnp.abs(relative)
    coarse = jnp.full_like(distance, exact_span)
    for edge in edge_list:
        coarse = coarse + (distance >= edge).astype(jnp.int32)
    nearby = jnp.where(distance < exact_span, distance, coarse)
    return nearby + jnp.where(relative > 0, NB // 2, 0)


def spread_bias(vector, stretch, width, seq_len):
    tiled = jnp.broadcast_to(vector, (stretch, width + 1)).reshape(-1)[: stretch * width]
    return tiled.reshape(stretch, width)[:, :seq_len]


def fold_diagonals(matrix, stretch, width):
    padded = jnp.pad(matrix, ((0, 0), (stretch, 0)))
    flat = jnp.pad(padded.reshape(-1), (0, stretch))
    return jnp.sum(flat.reshape(stretch, width + 1), axis=0)


def split_heads(matrix, heads):
    return jnp.transpose(matrix.reshape(matrix.shape[0], heads, -1), (1, 0, 2))


def merge_heads(stack):
    return jnp.transpose(stack, (1, 0, 2)).reshape(stack.shape[1], -1)


def root_mean_square_backward(grad, normalized, scale, gain):
    scaled = grad * gain
    return scale * (scaled - normalized * jnp.mean(scaled * normalized, axis=-1, keepdims=True))


def bucket_onehot(relative):
    return (bucket_of(relative)[:, None] == jnp.arange(NB, dtype=jnp.int32)[None, :]).astype(
        jnp.float32
    )


def shards(
    layer_input,
    segments,
    attn_gain,
    query_weight,
    key_weight,
    value_weight,
    output_weight,
    bias_table,
    ff_gain,
    gate_weight,
    up_weight,
    down_weight,
    cotangent,
):
    parts = lax.axis_size("tensor")
    part_index = lax.axis_index("tensor")
    stretch = segments.shape[0]
    rows = layer_input.shape[0]
    seq_len = stretch * lax.axis_size("ctx")
    query_start = lax.axis_index("ctx") * stretch
    width = seq_len + stretch
    local_heads = bias_table.shape[1]
    sharded = (
        attn_gain,
        query_weight,
        key_weight,
        value_weight,
        output_weight,
        ff_gain,
        gate_weight,
        up_weight,
        down_weight,
    )
    gathered = (
        lax.all_gather(sharded[0], ("dp", "ctx"), axis=0, tiled=True),
        lax.all_gather(sharded[1], ("dp", "ctx"), axis=0, tiled=True),
        lax.all_gather(sharded[2], ("dp", "ctx"), axis=0, tiled=True),
        lax.all_gather(sharded[3], ("dp", "ctx"), axis=0, tiled=True),
        lax.all_gather(sharded[4], ("dp", "ctx"), axis=1, tiled=True),
        lax.all_gather(sharded[5], ("dp", "ctx"), axis=0, tiled=True),
        lax.all_gather(sharded[6], ("dp", "ctx"), axis=0, tiled=True),
        lax.all_gather(sharded[7], ("dp", "ctx"), axis=0, tiled=True),
        lax.all_gather(sharded[8], ("dp", "ctx"), axis=1, tiled=True),
    )
    (
        attention_gain_complete,
        full_query,
        full_key,
        full_value,
        full_output,
        feedforward_gain_complete,
        full_gate,
        full_up,
        full_down,
    ) = gathered
    own_segments = lax.dynamic_slice_in_dim(segments, part_index * rows, rows)
    sublayer_input_rows = layer_input.astype(jnp.float32)
    first_inverse_scale = lax.rsqrt(
        jnp.mean(sublayer_input_rows * sublayer_input_rows, axis=1, keepdims=True) + eps
    )
    first_unit_input = sublayer_input_rows * first_inverse_scale
    first_normalized_input = (
        first_unit_input * attention_gain_complete.astype(jnp.float32)
    ).astype(jnp.bfloat16)
    normed_stretch = lax.all_gather(first_normalized_input, "tensor", axis=0, tiled=True)
    query = jnp.dot(normed_stretch, full_query, preferred_element_type=jnp.float32).astype(
        jnp.bfloat16
    )
    key_local = jnp.dot(normed_stretch, full_key, preferred_element_type=jnp.float32).astype(
        jnp.bfloat16
    )
    value_local = jnp.dot(normed_stretch, full_value, preferred_element_type=jnp.float32).astype(
        jnp.bfloat16
    )
    all_keys, all_values, all_segments = (
        lax.all_gather(key_local, "ctx", axis=0, tiled=True),
        lax.all_gather(value_local, "ctx", axis=0, tiled=True),
        lax.all_gather(segments, "ctx", axis=0, tiled=True),
    )
    allowed = segments[:, None] == all_segments[None, :]
    column = jnp.arange(width + 1, dtype=jnp.int32)
    local_offset = jnp.where(column < seq_len, column, column - (width + 1))
    bias_vectors = jnp.dot(
        bucket_onehot(local_offset - query_start), bias_table, precision=highest
    ).T
    query_heads = split_heads(query, local_heads)
    key_heads = split_heads(all_keys, local_heads)
    value_heads = split_heads(all_values, local_heads)

    def head_scores(query_h, key_h, vector):
        bias = spread_bias(vector, stretch, width, seq_len)
        scores = jnp.einsum("qd,kd->qk", query_h, key_h, preferred_element_type=jnp.float32) + bias
        return jnp.where(allowed, scores, -1e30)

    def attend(items):
        query_h, key_h, value_h, vector = items
        scores = head_scores(query_h, key_h, vector)
        top = jnp.max(scores, axis=1, keepdims=True)
        expo = jnp.exp(scores - top)
        total = jnp.sum(expo, axis=1, keepdims=True)
        probs = (expo / total).astype(jnp.bfloat16)
        mixed_h = jnp.dot(probs, value_h, preferred_element_type=jnp.float32)
        return (mixed_h.astype(jnp.bfloat16), (top + jnp.log(total))[:, 0])

    head_mix, log_totals = lax.map(attend, (query_heads, key_heads, value_heads, bias_vectors))
    mixed = merge_heads(head_mix)
    attn_part = jnp.dot(mixed, full_output, preferred_element_type=jnp.float32)
    attn_own = lax.psum_scatter(
        attn_part.astype(jnp.bfloat16), "tensor", scatter_dimension=0, tiled=True
    ).astype(jnp.float32)
    first_hidden_state = sublayer_input_rows + attn_own
    second_inverse_scale = lax.rsqrt(
        jnp.mean(first_hidden_state * first_hidden_state, axis=1, keepdims=True) + eps
    )
    second_unit_input = first_hidden_state * second_inverse_scale
    second_normalized_input = (
        second_unit_input * feedforward_gain_complete.astype(jnp.float32)
    ).astype(jnp.bfloat16)
    normed_two_stretch = lax.all_gather(second_normalized_input, "tensor", axis=0, tiled=True)
    gate = jnp.dot(normed_two_stretch, full_gate, preferred_element_type=jnp.float32)
    upper = jnp.dot(normed_two_stretch, full_up, preferred_element_type=jnp.float32)
    inner = (jax.nn.gelu(gate, approximate=True) * upper).astype(jnp.bfloat16)
    ff_part = jnp.dot(inner, full_down, preferred_element_type=jnp.float32)
    ff_own = lax.psum_scatter(
        ff_part.astype(jnp.bfloat16), "tensor", scatter_dimension=0, tiled=True
    ).astype(jnp.float32)
    block_output = (first_hidden_state + ff_own).astype(jnp.bfloat16)
    back_weights = (
        lax.all_gather(sharded[0], ("dp", "ctx"), axis=0, tiled=True),
        lax.all_gather(sharded[1], ("dp", "ctx"), axis=0, tiled=True),
        lax.all_gather(sharded[2], ("dp", "ctx"), axis=0, tiled=True),
        lax.all_gather(sharded[3], ("dp", "ctx"), axis=0, tiled=True),
        lax.all_gather(sharded[4], ("dp", "ctx"), axis=1, tiled=True),
        lax.all_gather(sharded[5], ("dp", "ctx"), axis=0, tiled=True),
        lax.all_gather(sharded[6], ("dp", "ctx"), axis=0, tiled=True),
        lax.all_gather(sharded[7], ("dp", "ctx"), axis=0, tiled=True),
        lax.all_gather(sharded[8], ("dp", "ctx"), axis=1, tiled=True),
    )
    (
        attention_gain_backward,
        back_query,
        back_key,
        back_value,
        back_output,
        feedforward_gain_backward,
        back_gate,
        back_up,
        back_down,
    ) = back_weights
    grad_stretch = lax.all_gather(cotangent, "tensor", axis=0, tiled=True)
    inner_grad = jnp.dot(grad_stretch, back_down.T, preferred_element_type=jnp.float32)
    down_wgrad = jnp.dot(inner.T, grad_stretch, preferred_element_type=jnp.float32)
    _, gelu_pull = jax.vjp(
        lambda gate_in, upper_in: jax.nn.gelu(gate_in, approximate=True) * upper_in, gate, upper
    )
    gate_grad, upper_grad = gelu_pull(inner_grad)
    gate_grad = gate_grad.astype(jnp.bfloat16)
    upper_grad = upper_grad.astype(jnp.bfloat16)
    gate_wgrad = jnp.dot(normed_two_stretch.T, gate_grad, preferred_element_type=jnp.float32)
    up_wgrad = jnp.dot(normed_two_stretch.T, upper_grad, preferred_element_type=jnp.float32)
    normed_two_part = jnp.dot(gate_grad, back_gate.T, preferred_element_type=jnp.float32) + jnp.dot(
        upper_grad, back_up.T, preferred_element_type=jnp.float32
    )
    second_normalized_gradient = lax.psum_scatter(
        normed_two_part.astype(jnp.bfloat16), "tensor", scatter_dimension=0, tiled=True
    ).astype(jnp.float32)
    feedforward_gain_share = jnp.sum(second_normalized_gradient * second_unit_input, axis=0)
    hidden_grad = cotangent.astype(jnp.float32) + root_mean_square_backward(
        second_normalized_gradient,
        second_unit_input,
        second_inverse_scale,
        feedforward_gain_backward.astype(jnp.float32),
    )
    attn_step = hidden_grad.astype(jnp.bfloat16)
    attn_step_stretch = lax.all_gather(attn_step, "tensor", axis=0, tiled=True)
    mixed_grad = jnp.dot(
        attn_step_stretch, back_output.T, preferred_element_type=jnp.float32
    ).astype(jnp.bfloat16)
    output_wgrad = jnp.dot(mixed.T, attn_step_stretch, preferred_element_type=jnp.float32)

    def attend_back(items):
        query_h, key_h, value_h, vector, log_total, mixed_grad_h = items
        scores = head_scores(query_h, key_h, vector)
        probs = jnp.exp(scores - log_total[:, None])
        value_g = jnp.einsum(
            "qk,qd->kd",
            probs.astype(jnp.bfloat16),
            mixed_grad_h,
            preferred_element_type=jnp.float32,
        )
        prob_grad = jnp.einsum(
            "qd,kd->qk", mixed_grad_h, value_h, preferred_element_type=jnp.float32
        )
        centre = jnp.sum(probs * prob_grad, axis=1, keepdims=True)
        score_grad = (probs * (prob_grad - centre)).astype(jnp.bfloat16)
        query_g = jnp.dot(score_grad, key_h, preferred_element_type=jnp.float32)
        key_g = jnp.einsum("qk,qd->kd", score_grad, query_h, preferred_element_type=jnp.float32)
        diagonal = fold_diagonals(score_grad.astype(jnp.float32), stretch, width)
        return (query_g.astype(jnp.bfloat16), key_g, value_g, diagonal)

    back_items = (
        query_heads,
        key_heads,
        value_heads,
        bias_vectors,
        log_totals,
        split_heads(mixed_grad, local_heads),
    )
    query_step_heads, key_all_heads, value_all_heads, diagonals = lax.map(attend_back, back_items)
    query_step = merge_heads(query_step_heads)
    key_step, value_step = (
        lax.psum_scatter(
            merge_heads(key_all_heads).astype(jnp.bfloat16), "ctx", scatter_dimension=0, tiled=True
        ).astype(jnp.float32),
        lax.psum_scatter(
            merge_heads(value_all_heads).astype(jnp.bfloat16),
            "ctx",
            scatter_dimension=0,
            tiled=True,
        ).astype(jnp.float32),
    )
    key_step = key_step.astype(jnp.bfloat16)
    value_step = value_step.astype(jnp.bfloat16)
    local_bias_grad = jnp.dot(
        diagonals, bucket_onehot(column - stretch - query_start), precision=highest
    )
    bias_full = lax.dynamic_update_slice(
        jnp.zeros((NB, local_heads * parts), jnp.float32),
        local_bias_grad.T,
        (jnp.int32(0), part_index * local_heads),
    )
    query_wgrad = jnp.dot(normed_stretch.T, query_step, preferred_element_type=jnp.float32)
    key_wgrad = jnp.dot(normed_stretch.T, key_step, preferred_element_type=jnp.float32)
    value_wgrad = jnp.dot(normed_stretch.T, value_step, preferred_element_type=jnp.float32)
    normed_one_part = jnp.dot(query_step, back_query.T, preferred_element_type=jnp.float32)
    normed_one_part = normed_one_part + jnp.dot(
        key_step, back_key.T, preferred_element_type=jnp.float32
    )
    normed_one_part = normed_one_part + jnp.dot(
        value_step, back_value.T, preferred_element_type=jnp.float32
    )
    first_normalized_gradient = lax.psum_scatter(
        normed_one_part.astype(jnp.bfloat16), "tensor", scatter_dimension=0, tiled=True
    ).astype(jnp.float32)
    attention_gain_share = jnp.sum(first_normalized_gradient * first_unit_input, axis=0)
    input_grads = (
        hidden_grad
        + root_mean_square_backward(
            first_normalized_gradient,
            first_unit_input,
            first_inverse_scale,
            attention_gain_backward.astype(jnp.float32),
        )
    ).astype(jnp.bfloat16)
    weight_terms = (
        query_wgrad,
        key_wgrad,
        value_wgrad,
        output_wgrad,
        gate_wgrad,
        up_wgrad,
        down_wgrad,
    )
    query_out, key_out, value_out, output_out, gate_out, up_out, down_out = (
        lax.psum_scatter(weight_terms[0], ("dp", "ctx"), scatter_dimension=0, tiled=True),
        lax.psum_scatter(weight_terms[1], ("dp", "ctx"), scatter_dimension=0, tiled=True),
        lax.psum_scatter(weight_terms[2], ("dp", "ctx"), scatter_dimension=0, tiled=True),
        lax.psum_scatter(weight_terms[3], ("dp", "ctx"), scatter_dimension=1, tiled=True),
        lax.psum_scatter(weight_terms[4], ("dp", "ctx"), scatter_dimension=0, tiled=True),
        lax.psum_scatter(weight_terms[5], ("dp", "ctx"), scatter_dimension=0, tiled=True),
        lax.psum_scatter(weight_terms[6], ("dp", "ctx"), scatter_dimension=1, tiled=True),
    )
    valid = (own_segments != 0).astype(jnp.float32)
    out_values = block_output.astype(jnp.float32)
    grad_values = input_grads.astype(jnp.float32)
    local_sums = jnp.stack(
        [
            jnp.sum(valid * jnp.sum(out_values * out_values, axis=1)),
            jnp.sum(valid * jnp.sum(grad_values * grad_values, axis=1)),
            jnp.sum(valid),
        ]
    )
    gain_one_total, gain_two_total, bias_total, sums_total = lax.psum(
        (attention_gain_share, feedforward_gain_share, bias_full, local_sums),
        ("dp", "ctx", "tensor"),
    )
    rms_stats = jnp.sqrt(sums_total[:2] / (sums_total[2] * sublayer_input_rows.shape[1]))
    return (
        block_output,
        input_grads,
        gain_one_total,
        query_out,
        key_out,
        value_out,
        output_out,
        bias_total,
        gain_two_total,
        gate_out,
        up_out,
        down_out,
        rms_stats,
    )


def solution(mesh):
    return jax.shard_map(
        shards,
        mesh=mesh,
        in_specs=(
            P(("dp", "ctx", "tensor"), None),
            P(("dp", "ctx")),
            P(("dp", "ctx")),
            P(("dp", "ctx"), "tensor"),
            P(("dp", "ctx"), "tensor"),
            P(("dp", "ctx"), "tensor"),
            P("tensor", ("dp", "ctx")),
            P(None, "tensor"),
            P(("dp", "ctx")),
            P(("dp", "ctx"), "tensor"),
            P(("dp", "ctx"), "tensor"),
            P("tensor", ("dp", "ctx")),
            P(("dp", "ctx", "tensor"), None),
        ),
        out_specs=(
            P(("dp", "ctx", "tensor"), None),
            P(("dp", "ctx", "tensor"), None),
            P(),
            P(("dp", "ctx"), "tensor"),
            P(("dp", "ctx"), "tensor"),
            P(("dp", "ctx"), "tensor"),
            P("tensor", ("dp", "ctx")),
            P(),
            P(),
            P(("dp", "ctx"), "tensor"),
            P(("dp", "ctx"), "tensor"),
            P("tensor", ("dp", "ctx")),
            P(),
        ),
        check_vma=False,
    )
```

profile of v0, /device:TPU:0, one launch (start us, length us, event | category | flops | bytes accessed | tf_op | source)
XLA Modules:
  0.0 3525.5 jit_solution(717120642239859965)
XLA Ops:
  7.2 42.4 %all-gather = bf16[16,1,128]{2,1,0:T(2,128)(2,1)S(1)} all-gather(bf16[1,1,128]{2,1,0:T(2,128)(2,1)} %bitcast.193), channel_id=1, replica_groups=mesh['dp'=4,'ctx'=4,'tensor'=2] {'dp','ctx'}, dimensions={0}, use_global_device_ids=true | all-gather | bytes 4352 | tf_op jit(solution)/shard_map/all_gather | solution.py:89
  55.5 3.4 all-gather.17.cloned.1.call-done
  58.9 79.9 %all-gather.21.cloned.1.call-done = bf16[2048,1024]{1,0:T(8,128)(2,1)} async-done(((bf16[128,1024]{1,0:T(8,128)(2,1)}), bf16[2048,1024]{1,0:T(8,128)(2,1)}) %all-gather.21.cloned.1.call-update) | async-done | bytes 4194320 | tf_op jit(solution)/shard_map/all_gather | solution.py:91
  138.8 4.6 convolution_convert_fusion.6
  143.4 72.7 %all-gather.25.cloned.1.call-done = bf16[2048,1024]{1,0:T(8,128)(2,1)} async-done(((bf16[128,1024]{1,0:T(8,128)(2,1)}), bf16[2048,1024]{1,0:T(8,128)(2,1)}) %all-gather.25.cloned.1.call-update) | async-done | bytes 4194320 | tf_op jit(solution)/shard_map/all_gather | solution.py:92
  216.1 4.3 convolution_convert_fusion.5
  221.2 9.6 all-gather.1
  231.3 62.1 %all-gather.19.cloned.1.call-done = bf16[2048,1024]{1,0:T(8,128)(2,1)} async-done(((bf16[128,1024]{1,0:T(8,128)(2,1)}), bf16[2048,1024]{1,0:T(8,128)(2,1)}) %all-gather.19.cloned.1.call-update) | async-done | bytes 4194320 | tf_op jit(solution)/shard_map/all_gather | solution.py:90
  293.4 3.5 convolution_convert_fusion.7
  298.4 41.5 %all-gather.23.cloned.1.call-done = bf16[1024,1024]{1,0:T(8,128)(2,1)} async-done(((bf16[256,1024]{1,0:T(8,128)(2,1)}), bf16[1024,1024]{1,0:T(8,128)(2,1)}) %all-gather.23.cloned.1.call-update) | async-done | bytes 2097168 | tf_op jit(solution)/shard_map/all_gather | solution.py:130
  346.0 40.7 %all-gather.27.cloned.1.call-done = bf16[1024,1024]{1,0:T(8,128)(2,1)} async-done(((bf16[256,1024]{1,0:T(8,128)(2,1)}), bf16[1024,1024]{1,0:T(8,128)(2,1)}) %all-gather.27.cloned.1.call-update) | async-done | bytes 2097168 | tf_op jit(solution)/shard_map/all_gather | solution.py:131
  392.7 71.4 %while.32 = (s32[]{:T(128)}, bf16[16,256,64]{1,2,0:T(8,128)(2,1)S(1)}, f32[16,256]{1,0:T(8,128)S(1)}, bf16[16,256,64]{2,1,0:T(8,128)(2,1)}, bf16[16,1024,64]{2,1...) while((s32[]{:T(128)}, ...), condition=%wide.region_4.5_spmd.clone, body=%wide.region_1.4_spmd.clone.sunk | while | flops 69484288 | bytes 14027905 | solution.py:159
  464.1 13.2 all-gather.29.cloned.1.call-done
  477.3 4.5 convolution_convert_fusion.3
  481.9 37.6 %all-gather.2 = bf16[16,1,128]{2,1,0:T(2,128)(2,1)S(1)} all-gather(bf16[1,1,128]{2,1,0:T(2,128)(2,1)S(1)} %bitcast.194), channel_id=1, replica_groups=mesh['dp'=4,'ctx'=4,'tensor'=2] {'dp','ctx'}, dimensions={0}, use_global_device_ids=true | all-gather | bytes 4352 | tf_op jit(solution)/shard_map/all_gather | solution.py:94
  528.5 136.3 %all-gather.33.cloned.1.call-done = bf16[2048,2560]{1,0:T(8,128)(2,1)} async-done(((bf16[128,2560]{1,0:T(8,128)(2,1)}), bf16[2048,2560]{1,0:T(8,128)(2,1)}) %all-gather.33.cloned.1.call-update) | async-done | bytes 10485776 | tf_op jit(solution)/shard_map/all_gather | solution.py:95
  664.8 8.7 fusion.101
  673.5 124.8 %all-gather.35.cloned.1.call-done = bf16[2048,2560]{1,0:T(8,128)(2,1)} async-done(((bf16[128,2560]{1,0:T(8,128)(2,1)}), bf16[2048,2560]{1,0:T(8,128)(2,1)}) %all-gather.35.cloned.1.call-update) | async-done | bytes 10485776 | tf_op jit(solution)/shard_map/all_gather | solution.py:96
  798.4 8.3 fusion.102
  807.1 173.4 %all-gather.37.cloned.1.call-done = bf16[2560,2048]{1,0:T(8,128)(2,1)} async-done(((bf16[2560,128]{1,0:T(8,128)(2,1)}), bf16[2560,2048]{1,0:T(8,128)(2,1)}) %all-gather.37.cloned.1.call-update) | async-done | bytes 10485776 | tf_op jit(solution)/shard_map/all_gather | solution.py:97
  980.5 11.5 multiply_convert_fusion.1
  992.0 6.6 fusion.103
  998.6 8.0 fusion.52
  1006.8 6.7 reduce-scatter.18.cloned.1.call-done
  1017.5 10.3 all-gather.41.cloned.1.call-done
  1027.8 3.8 convolution_convert_fusion.4
  1033.4 327.1 %while.33 = (s32[]{:T(128)}, bf16[16,256,64]{1,2,0:T(8,128)(2,1)}, bf16[16,1024,64]{1,2,0:T(8,128)(2,1)}, bf16[16,1024,64]{1,2,0:T(8,128)(2,1)}, f32[16,1281]{1,...) while((s32[]{:T(128)}, bf16[16,256,64]{1,2,0:T(8,128)(2,1)}, ...), condition=%wide.region_13.14_spmd.clone, body=%wide.region_10.13_spmd.clone.sunk | while | flops 171064320 | bytes 29391080 | solution.py:263
  1043.4 3.6 reshape.245
  1063.9 3.6 reshape.245
  1084.4 3.6 reshape.245
  1104.8 3.6 reshape.245
  1125.3 3.6 reshape.245
  1145.7 3.6 reshape.245
  1166.1 3.6 reshape.245
  1186.6 3.6 reshape.245
  1207.0 3.6 reshape.245
  1227.4 3.6 reshape.245
  1247.9 3.6 reshape.245
  1268.3 3.6 reshape.245
  1288.8 3.6 reshape.245
  1309.2 3.6 reshape.245
  1329.6 3.6 reshape.245
  1350.1 3.6 reshape.245
  1361.5 3.5 fusion.104
  1365.1 40.6 %reduce-scatter.20.cloned.1.call-done = bf16[256,1024]{0,1:T(8,128)(2,1)} async-done(((bf16[1024,1024]{0,1:T(8,128)(2,1)}), bf16[256,1024]{0,1:T(8,128)(2,1)}) %reduce-scatter.20.cloned.1.call-update) | async-done | bytes 524304 | tf_op jit(solution)/shard_map/reduce_scatter | solution.py:266
  1405.7 5.0 convolution_add_fusion.3
  1410.8 40.4 %reduce-scatter.22.cloned.1.call-done = bf16[256,1024]{0,1:T(8,128)(2,1)} async-done(((bf16[1024,1024]{0,1:T(8,128)(2,1)}), bf16[256,1024]{0,1:T(8,128)(2,1)}) %reduce-scatter.22.cloned.1.call-update) | async-done | bytes 524304 | tf_op jit(solution)/shard_map/reduce_scatter | solution.py:269
  1451.2 5.3 fusion.51
  1456.8 7.9 convolution_convert_fusion.2
  1464.8 5.7 fusion.108
  1471.7 4.6 fusion.105
  1477.4 4.6 fusion.106
  1483.0 4.5 fusion.107
  1488.8 10.0 fusion.109
  1498.8 10.0 fusion.110
  1510.1 8.6 fusion.111
  1527.1 45.6 %all-reduce.2 = (f32[2048]{0:T(1024)}, f32[32,32]{1,0:T(8,128)}, f32[2048]{0:T(1024)}, f32[3]{0:T(128)S(1)}) all-reduce(f32[2048]{0:T(1024)S(1)} %get-tuple-element.312, f32[32,32]{1,0:T(8,128)S(1)} %dynamic_update_slice.37, f32[2048]{0:T(1024)S(1)} %get-tuple-element.310, ...), channel_id=1, replica_groups=mesh['dp'=4,'ctx'=4,'tensor'=2] {'dp','ctx','tensor'}, use_global_device_ids=true, to_apply=%region_19.20 | all-reduce | flops 5123 | bytes 40984 | tf_op jit(solution)/shard_map/psum | solution.py:337
  1574.5 89.3 %reduce-scatter.32.cloned.1.call-done = f32[1024,128]{1,0:T(8,128)} async-done(((f32[1024,2048]{1,0:T(8,128)}), f32[1024,128]{1,0:T(8,128)}) %reduce-scatter.32.cloned.1.call-update) | async-done | bytes 524304 | tf_op jit(solution)/shard_map/reduce_scatter | solution.py:322
  1663.8 182.7 %reduce-scatter.26.cloned.1.call-done = f32[128,1024]{1,0:T(8,128)} async-done(((f32[2048,1024]{1,0:T(8,128)}), f32[128,1024]{1,0:T(8,128)}) %reduce-scatter.26.cloned.1.call-update) | async-done | bytes 524304 | tf_op jit(solution)/shard_map/reduce_scatter | solution.py:319
  1846.6 182.7 %reduce-scatter.28.cloned.1.call-done = f32[128,1024]{1,0:T(8,128)} async-done(((f32[2048,1024]{1,0:T(8,128)}), f32[128,1024]{1,0:T(8,128)}) %reduce-scatter.28.cloned.1.call-update) | async-done | bytes 524304 | tf_op jit(solution)/shard_map/reduce_scatter | solution.py:320
  2029.3 182.7 %reduce-scatter.30.cloned.1.call-done = f32[128,1024]{1,0:T(8,128)} async-done(((f32[2048,1024]{1,0:T(8,128)}), f32[128,1024]{1,0:T(8,128)}) %reduce-scatter.30.cloned.1.call-update) | async-done | bytes 524304 | tf_op jit(solution)/shard_map/reduce_scatter | solution.py:321
  2212.0 434.1 %reduce-scatter.34.cloned.1.call-done = f32[128,2560]{1,0:T(8,128)} async-done(((f32[2048,2560]{1,0:T(8,128)}), f32[128,2560]{1,0:T(8,128)}) %reduce-scatter.34.cloned.1.call-update) | async-done | bytes 1310736 | tf_op jit(solution)/shard_map/reduce_scatter | solution.py:323
  2646.1 436.3 %reduce-scatter.36.cloned.1.call-done = f32[128,2560]{1,0:T(8,128)} async-done(((f32[2048,2560]{1,0:T(8,128)}), f32[128,2560]{1,0:T(8,128)}) %reduce-scatter.36.cloned.1.call-update) | async-done | bytes 1310736 | tf_op jit(solution)/shard_map/reduce_scatter | solution.py:324
  3082.4 436.2 %reduce-scatter.38.cloned.1.call-done = f32[2560,128]{1,0:T(8,128)} async-done(((f32[2560,2048]{1,0:T(8,128)}), f32[2560,128]{1,0:T(8,128)}) %reduce-scatter.38.cloned.1.call-update) | async-done | bytes 1310736 | tf_op jit(solution)/shard_map/reduce_scatter | solution.py:325
  (614 shorter events, 391.9 us)
Async XLA Ops:
  7.2 223.6 %copy-start = (f32[32,16]{0,1:T(8,128)S(1)}, f32[32,16]{0,1:T(8,128)}, u32[]{:S(2)}) copy-start(f32[32,16]{0,1:T(8,128)} %param.24) | copy-start | bytes 6148
  7.2 51.7 %all-gather.17.cloned.1.call-start = ((), (), s32[]{:S(2)}) async-start(), calls=%async_computation.13 | async-start | bytes 1572864 | tf_op jit(solution)/shard_map/all_gather | solution.py:119
  49.6 1.3 copy-start.23
  53.4 85.3 %all-gather.21.cloned.1.call-start = ((), (), s32[]{:S(2)}) async-start(), calls=%async_computation.15 | async-start | bytes 4456448 | tf_op jit(solution)/shard_map/all_gather | solution.py:91
  54.2 161.9 %all-gather.25.cloned.1.call-start = ((), (), s32[]{:S(2)}) async-start(), calls=%async_computation.17 | async-start | bytes 4456448 | tf_op jit(solution)/shard_map/all_gather | solution.py:92
  54.9 238.5 %all-gather.19.cloned.1.call-start = ((), (), s32[]{:S(2)}) async-start(), calls=%async_computation.14 | async-start | bytes 4456448 | tf_op jit(solution)/shard_map/all_gather | solution.py:90
  55.5 284.5 %all-gather.23.cloned.1.call-start = ((), (), s32[]{:S(2)}) async-start(), calls=%async_computation.16 | async-start | bytes 2621440 | tf_op jit(solution)/shard_map/all_gather | solution.py:130
  58.9 157.2 %copy-start.4 = (bf16[256,2048]{1,0:T(8,128)(2,1)S(1)}, bf16[256,2048]{1,0:T(8,128)(2,1)}, u32[]{:S(2)}) copy-start(bf16[256,2048]{1,0:T(8,128)(2,1)} %all-gather.17.cloned.1.call-done) | copy-start | bytes 3145732
  143.3 77.9 %copy-start.22 = (s32[256]{0:T(256)S(1)}, s32[256]{0:T(256)}, u32[]{:S(2)}) copy-start(s32[256]{0:T(256)} %param.18) | copy-start | bytes 3076
  143.4 243.3 %all-gather.27.cloned.1.call-start = ((), (), s32[]{:S(2)}) async-start(), calls=%async_computation.18 | async-start | bytes 2621440 | tf_op jit(solution)/shard_map/all_gather | solution.py:131
  220.4 257.0 %all-gather.29.cloned.1.call-start = ((), (), s32[]{:S(2)}) async-start(), calls=%async_computation.19 | async-start | bytes 4456448 | tf_op jit(solution)/shard_map/all_gather | solution.py:93
  221.1 298.4 %reduce-scatter.14.cloned.1.call-start = ((), (), s32[]{:S(2)}) async-start(), calls=%async_computation.20 | async-start | bytes 1572864 | tf_op jit(solution)/shard_map/reduce_scatter | solution.py:162
  464.1 17.7 copy-start.13
  477.3 4.6 copy-start.27
  477.3 42.2 %copy-start.2 = (bf16[128,2048]{1,0:T(8,128)(2,1)S(1)}, bf16[128,2048]{1,0:T(8,128)(2,1)}, u32[]{:S(2)}) copy-start(bf16[128,2048]{1,0:T(8,128)(2,1)} %param.17) | copy-start | bytes 1572868
  481.8 46.7 %all-gather.31.cloned.1.call-start = ((), (), s32[]{:S(2)}) async-start(), calls=%async_computation.21 | async-start | bytes 1572864 | tf_op jit(solution)/shard_map/all_gather | solution.py:173
  523.0 141.9 %all-gather.33.cloned.1.call-start = ((), (), s32[]{:S(2)}) async-start(), calls=%async_computation.22 | async-start | bytes 11141120 | tf_op jit(solution)/shard_map/all_gather | solution.py:95
  523.5 274.8 %all-gather.35.cloned.1.call-start = ((), (), s32[]{:S(2)}) async-start(), calls=%async_computation.23 | async-start | bytes 11141120 | tf_op jit(solution)/shard_map/all_gather | solution.py:96
  524.3 282.8 %all-gather.39.cloned.1.call-start = ((), (), s32[]{:S(2)}) async-start(), calls=%async_computation.26 | async-start | bytes 1572864 | tf_op jit(solution)/shard_map/all_gather | solution.py:204
  524.9 455.6 %all-gather.37.cloned.1.call-start = ((), (), s32[]{:S(2)}) async-start(), calls=%async_computation.24 | async-start | bytes 11141120 | tf_op jit(solution)/shard_map/all_gather | solution.py:97
  525.6 487.9 %reduce-scatter.18.cloned.1.call-start = ((), (), s32[]{:S(2)}) async-start(), calls=%async_computation.27 | async-start | bytes 1572864 | tf_op jit(solution)/shard_map/reduce_scatter | solution.py:218
  528.5 269.9 %copy-start.8 = (bf16[256,2048]{1,0:T(8,128)(2,1)S(1)}, bf16[256,2048]{1,0:T(8,128)(2,1)}, u32[]{:S(2)}) copy-start(bf16[256,2048]{1,0:T(8,128)(2,1)} %all-gather.31.cloned.1.call-done) | copy-start | bytes 3145732
  992.0 6.6 copy-start.19
  992.0 6.6 copy-start.18
  998.6 14.9 copy-start.6
  1006.6 8.5 copy-start.10
  1006.6 21.1 all-gather.41.cloned.1.call-start
  1017.4 388.3 %reduce-scatter.20.cloned.1.call-start = ((), (), s32[]{:S(2)}) async-start(), calls=%async_computation.29 | async-start | bytes 2621440 | tf_op jit(solution)/shard_map/reduce_scatter | solution.py:266
  1036.7 1.3 slice-start
  1057.2 1.3 slice-start
  1077.7 1.3 slice-start
  1098.1 1.3 slice-start
  1118.6 1.3 slice-start
  1139.0 1.3 slice-start
  1159.4 1.3 slice-start
  1179.9 1.3 slice-start
  1200.3 1.3 slice-start
  1220.8 1.3 slice-start
  1241.2 1.3 slice-start
  1261.6 1.3 slice-start
  1282.1 1.3 slice-start
  1302.5 1.3 slice-start
  1323.0 1.3 slice-start
  1343.4 1.3 slice-start
  1360.5 90.6 %reduce-scatter.22.cloned.1.call-start = ((), (), s32[]{:S(2)}) async-start(), calls=%async_computation.30 | async-start | bytes 2621440 | tf_op jit(solution)/shard_map/reduce_scatter | solution.py:269
  1361.1 158.7 %reduce-scatter.24.cloned.1.call-start = ((), (), s32[]{:S(2)}) async-start(), calls=%async_computation.31 | async-start | bytes 1572864 | tf_op jit(solution)/shard_map/reduce_scatter | solution.py:296
  1410.8 46.0 %copy-start.15 = (bf16[256,2560]{1,0:T(8,128)(2,1)S(1)}, bf16[256,2560]{1,0:T(8,128)(2,1)}, u32[]{:S(2)}) copy-start(bf16[256,2560]{1,0:T(8,128)(2,1)} %get-tuple-element.375) | copy-start | bytes 3932164
  1456.5 64.9 %reduce-scatter.16.cloned.1.call-start = ((), (), s32[]{:S(2)}) async-start(), calls=%async_computation.25 | async-start | bytes 1572864 | tf_op jit(solution)/shard_map/reduce_scatter | solution.py:178
  1456.8 8.0 copy-start.14
  1464.7 199.1 %reduce-scatter.32.cloned.1.call-start = ((), (), s32[]{:S(2)}) async-start(), calls=%async_computation.35 | async-start | bytes 8912896 | tf_op jit(solution)/shard_map/reduce_scatter | solution.py:322
  1470.5 1.2 copy-start.5
  1470.5 376.0 %reduce-scatter.26.cloned.1.call-start = ((), (), s32[]{:S(2)}) async-start(), calls=%async_computation.32 | async-start | bytes 8912896 | tf_op jit(solution)/shard_map/reduce_scatter | solution.py:319
  1476.4 552.9 %reduce-scatter.28.cloned.1.call-start = ((), (), s32[]{:S(2)}) async-start(), calls=%async_computation.33 | async-start | bytes 8912896 | tf_op jit(solution)/shard_map/reduce_scatter | solution.py:320
  1482.0 730.0 %reduce-scatter.30.cloned.1.call-start = ((), (), s32[]{:S(2)}) async-start(), calls=%async_computation.34 | async-start | bytes 8912896 | tf_op jit(solution)/shard_map/reduce_scatter | solution.py:321
  1487.6 1.2 copy-start.9
  1487.6 1158.5 %reduce-scatter.34.cloned.1.call-start = ((), (), s32[]{:S(2)}) async-start(), calls=%async_computation.36 | async-start | bytes 22282240 | tf_op jit(solution)/shard_map/reduce_scatter | solution.py:323
  1498.8 1583.6 %reduce-scatter.36.cloned.1.call-start = ((), (), s32[]{:S(2)}) async-start(), calls=%async_computation.37 | async-start | bytes 22282240 | tf_op jit(solution)/shard_map/reduce_scatter | solution.py:324
  1508.8 1.2 copy-start.20
  1508.8 2009.7 %reduce-scatter.38.cloned.1.call-start = ((), (), s32[]{:S(2)}) async-start(), calls=%async_computation.38 | async-start | bytes 22282240 | tf_op jit(solution)/shard_map/reduce_scatter | solution.py:325
  1518.7 1.1 copy-start.26
  1518.7 2.7 copy-start.7
  1518.7 2.7 copy-start.11
  1518.7 2.7 copy-start.12
  1519.5 1999.0 %copy-start.1 = (f32[32,16]{0,1:T(8,128)S(1)}, f32[32,16]{0,1:T(8,128)}, u32[]{:S(2)}) copy-start(f32[32,16]{0,1:T(8,128)} %param.24) | copy-start | bytes 6148
  (6 other events, 5.9 us)
Sparse Core Ops, SparseCore 0:
  53.6 5.3 all-gather.16
  61.7 77.0 all-gather.20
  141.5 74.4 all-gather.24
  218.7 74.6 all-gather.18
  295.4 44.5 all-gather.22
  342.0 44.6 all-gather.26
  389.4 87.9 all-gather.28
  482.0 6.7 reduce-scatter.13
  523.1 5.3 all-gather.30
  531.5 133.3 all-gather.32
  668.0 130.3 all-gather.34
  799.8 7.2 all-gather.38
  810.2 170.3 all-gather.36
  1006.7 6.7 reduce-scatter.17
  1017.5 10.1 all-gather.40
  1360.7 45.0 reduce-scatter.19
  1408.0 43.1 reduce-scatter.21
  1456.6 7.8 reduce-scatter.23
  1466.9 9.6 reduce-scatter.15
  1479.3 184.4 reduce-scatter.31
  1666.7 179.8 reduce-scatter.25
  1849.4 179.8 reduce-scatter.27
  2032.2 179.8 reduce-scatter.29
  2214.7 431.2 reduce-scatter.33
  2648.9 433.3 reduce-scatter.35
  3085.1 433.3 reduce-scatter.37
where the time goes:
time: 3540 us; the launch traced here: 3530 us
  waiting for transfers between devices  2800 us (79%)
  matrix products  314 us (9%)
  local copies, waits for them, and re-layouts  190 us (5%)
  blocking collectives  135 us (4%)
  other arithmetic  67.7 us (2%)
    reduce_scatter x1, waiting for transfers between devices, shards(): lax.psum_scatter(weight_terms[5], ('dp', 'ctx'), scatter_dimension=0, til...  436 us
    reduce_scatter x1, waiting for transfers between devices, shards(): lax.psum_scatter(weight_terms[6], ('dp', 'ctx'), scatter_dimension=1, til...  436 us
    reduce_scatter x1, waiting for transfers between devices, shards(): lax.psum_scatter(weight_terms[4], ('dp', 'ctx'), scatter_dimension=0, til...  434 us
    reduce_scatter x1, waiting for transfers between devices, shards(): lax.psum_scatter(weight_terms[0], ('dp', 'ctx'), scatter_dimension=0, til...  183 us
    reduce_scatter x1, waiting for transfers between devices, shards(): lax.psum_scatter(weight_terms[2], ('dp', 'ctx'), scatter_dimension=0, til...  183 us
    reduce_scatter x1, waiting for transfers between devices, shards(): lax.psum_scatter(weight_terms[1], ('dp', 'ctx'), scatter_dimension=0, til...  183 us
    all_gather x1, waiting for transfers between devices, shards(): lax.all_gather(sharded[8], ('dp', 'ctx'), axis=1, tiled=True)  173 us
    all_gather x1, waiting for transfers between devices, shards(): lax.all_gather(sharded[6], ('dp', 'ctx'), axis=0, tiled=True)  136 us
  transfers between devices with their start and end apart: 26, of which 23 were waited for; matrix products, arithmetic and copies ran while one was open for 5% of the time, Pallas kernels for 0%

commit v1 on v0

v1 whole, which is shorter than its diff:
```python
import functools

import jax
import jax.numpy as jnp
from jax import lax
from jax.experimental import pallas as pl
from jax.experimental.pallas import tpu as pltpu
from jax.sharding import PartitionSpec as P

NB = 32
DH = 64
edge_list = (12, 16, 23, 32, 46, 64, 91)
exact_span = 8
eps = 1e-06
highest = lax.Precision.HIGHEST
bf16 = jnp.bfloat16
f32 = jnp.float32

TQ = 256
REACH = 128
SPAN = TQ + 2 * REACH
WIDE = 1024


def bucket_of(relative):
    distance = jnp.abs(relative)
    coarse = jnp.full_like(distance, exact_span)
    for edge in edge_list:
        coarse = coarse + (distance >= edge).astype(jnp.int32)
    nearby = jnp.where(distance < exact_span, distance, coarse)
    return nearby + jnp.where(relative > 0, NB // 2, 0)


def lane_buckets():
    lane = jnp.arange(WIDE, dtype=jnp.int32)
    ahead = jnp.where(lane < TQ, lane, lane - WIDE)
    onehot = bucket_of(-ahead - REACH)[:, None] == jnp.arange(NB, dtype=jnp.int32)[None, :]
    return onehot.astype(f32)


def dot_nt(a, b):
    return lax.dot_general(a, b, (((1,), (1,)), ((), ())), preferred_element_type=f32)


def dot_nn(a, b):
    return lax.dot_general(a, b, (((1,), (0,)), ((), ())), preferred_element_type=f32)


def tile_range(tile, seq_len):
    start = tile * TQ
    low, high = max(0, start - REACH), min(seq_len, start + TQ + REACH)
    return start, low, high, low - (start - REACH), high - (start - REACH)


def tile_scores(key, query, strip_ref, far, seg_col, seg_row, tile, seq_len):
    start, low, high, strip_low, strip_high = tile_range(tile, seq_len)
    scores = dot_nt(key, query)
    parts = []
    if low > 0:
        parts.append(scores[:low] + far[0])
    parts.append(scores[low:high] + strip_ref[strip_low:strip_high])
    if high < seq_len:
        parts.append(scores[high:] + far[1])
    scores = jnp.concatenate(parts, axis=0) if len(parts) > 1 else parts[0]
    return jnp.where(seg_col == seg_row[:, start : start + TQ], scores, -1e30)


def make_strip(strip_ref, vector):
    tall = jnp.broadcast_to(vector, (SPAN, WIDE))
    strip_ref[...] = pltpu.roll(tall, 0, 1, stride=1, stride_axis=0)[:, :TQ]


def fold_diagonals(acc_ref):
    rest = jnp.zeros((8, WIDE - TQ), f32)
    groups = jnp.zeros((8, WIDE), f32)
    for at in range(0, SPAN, 8):
        wide = jnp.concatenate([acc_ref[at : at + 8, :], rest], axis=1)
        groups = groups + pltpu.roll(wide, (WIDE - at) % WIDE, 1)
    diagonals = groups[0:1]
    for row in range(1, 8):
        diagonals = diagonals + pltpu.roll(groups[row : row + 1], WIDE - row, 1)
    return diagonals


def attend_kernel(
    seq_len, q_ref, k_ref, v_ref, segc_ref, segr_ref, vec_ref, far_ref, mix_ref, lse_ref, strip_ref
):
    seg_col = segc_ref[...]
    seg_row = segr_ref[...]
    pair = pl.program_id(0)
    value_t = v_ref[...].T
    for half in range(2):
        make_strip(strip_ref, vec_ref[0, half : half + 1, :])
        far = (far_ref[2 * pair + half, 0], far_ref[2 * pair + half, 1])
        lanes = slice(half * DH, (half + 1) * DH)
        key = k_ref[:, lanes]
        for tile in range(seq_len // TQ):
            rows = slice(tile * TQ, (tile + 1) * TQ)
            query = q_ref[rows, lanes]
            scores = tile_scores(key, query, strip_ref, far, seg_col, seg_row, tile, seq_len)
            top = jnp.max(scores, axis=0, keepdims=True)
            expo = jnp.exp(scores - top)
            total = jnp.sum(expo, axis=0, keepdims=True)
            mixed_t = dot_nn(value_t[lanes, :], expo.astype(bf16)) * (1.0 / total)
            mix_ref[rows, lanes] = mixed_t.T.astype(bf16)
            lse_ref[0, half : half + 1, rows] = top + jnp.log(total)


def attend_back_kernel(
    seq_len,
    q_ref,
    k_ref,
    v_ref,
    do_ref,
    segc_ref,
    segr_ref,
    vec_ref,
    far_ref,
    lse_ref,
    dq_ref,
    dk_ref,
    dv_ref,
    diag_ref,
    farsum_ref,
    strip_ref,
    acc_ref,
    dk_acc,
    dv_acc,
):
    seg_col = segc_ref[...]
    seg_row = segr_ref[...]
    pair = pl.program_id(0)
    key_t = k_ref[...].T
    for half in range(2):
        make_strip(strip_ref, vec_ref[0, half : half + 1, :])
        far = (far_ref[2 * pair + half, 0], far_ref[2 * pair + half, 1])
        lanes = slice(half * DH, (half + 1) * DH)
        key = k_ref[:, lanes]
        value = v_ref[:, lanes]
        acc_ref[...] = jnp.zeros_like(acc_ref)
        far_before = jnp.zeros((1, TQ), f32)
        far_after = jnp.zeros((1, TQ), f32)
        for tile in range(seq_len // TQ):
            start, low, high, strip_low, strip_high = tile_range(tile, seq_len)
            rows = slice(start, start + TQ)
            query = q_ref[rows, lanes]
            mixed_grad = do_ref[rows, lanes]
            scores = tile_scores(key, query, strip_ref, far, seg_col, seg_row, tile, seq_len)
            probs = jnp.exp(scores - lse_ref[0, half : half + 1, rows])
            prob_grad = dot_nt(value, mixed_grad)
            centre = jnp.sum(probs * prob_grad, axis=0, keepdims=True)
            score_grad = probs * (prob_grad - centre)
            rounded = score_grad.astype(bf16)
            value_g = dot_nn(probs.astype(bf16), mixed_grad)
            key_g = dot_nn(rounded, query)
            if tile == 0:
                dv_acc[...] = value_g
                dk_acc[...] = key_g
            else:
                dv_acc[...] += value_g
                dk_acc[...] += key_g
            dq_ref[rows, lanes] = dot_nn(key_t[lanes, :], rounded).T.astype(bf16)
            acc_ref[strip_low:strip_high, :] += score_grad[low:high]
            if low > 0:
                far_before = far_before + jnp.sum(score_grad[:low], axis=0, keepdims=True)
            if high < seq_len:
                far_after = far_after + jnp.sum(score_grad[high:], axis=0, keepdims=True)
        dk_ref[:, lanes] = dk_acc[...].astype(bf16)
        dv_ref[:, lanes] = dv_acc[...].astype(bf16)
        diag_ref[0, half : half + 1, :] = fold_diagonals(acc_ref)
        farsum_ref[0, half : half + 1, 0:TQ] = far_before
        farsum_ref[0, half : half + 1, TQ : 2 * TQ] = far_after


def kernel_params():
    return pltpu.CompilerParams(vmem_limit_bytes=56 * 1024 * 1024)


def attention_specs(seq_len, pairs):
    wide = lambda at: pl.BlockSpec((seq_len, 2 * DH), lambda p, at=at: (0, at * pairs + p))
    seg_c = pl.BlockSpec((seq_len, 1), lambda p: (0, 0))
    seg_r = pl.BlockSpec((1, seq_len), lambda p: (0, 0))
    vec = pl.BlockSpec((1, 2, WIDE), lambda p: (p, 0, 0))
    far = pl.BlockSpec(memory_space=pltpu.SMEM)
    lse = pl.BlockSpec((1, 2, seq_len), lambda p: (p, 0, 0))
    return wide, seg_c, seg_r, vec, far, lse


def attend(qkv, segs, vectors, far):
    seq_len = qkv.shape[0]
    pairs = vectors.shape[0]
    wide, seg_c, seg_r, vec, far_spec, lse = attention_specs(seq_len, pairs)
    work = pairs * 2 * seq_len * seq_len
    return pl.pallas_call(
        functools.partial(attend_kernel, seq_len),
        grid=(pairs,),
        in_specs=[wide(0), wide(1), wide(2), seg_c, seg_r, vec, far_spec],
        out_specs=[wide(0), lse],
        out_shape=[
            jax.ShapeDtypeStruct((seq_len, pairs * 2 * DH), bf16),
            jax.ShapeDtypeStruct((pairs, 2, seq_len), f32),
        ],
        scratch_shapes=[pltpu.VMEM((SPAN, TQ), f32)],
        compiler_params=kernel_params(),
        cost_estimate=pl.CostEstimate(
            flops=16 * DH * work, bytes_accessed=8 * seq_len * pairs * DH, transcendentals=work
        ),
        name="attend",
    )(qkv, qkv, qkv, segs[:, None], segs[None, :], vectors, far)


def attend_back(qkv, mixed_grad, segs, vectors, far, lse_rows):
    seq_len = qkv.shape[0]
    pairs = vectors.shape[0]
    wide, seg_c, seg_r, vec, far_spec, lse = attention_specs(seq_len, pairs)
    work = pairs * 2 * seq_len * seq_len
    heads_shape = jax.ShapeDtypeStruct((seq_len, pairs * 2 * DH), bf16)
    return pl.pallas_call(
        functools.partial(attend_back_kernel, seq_len),
        grid=(pairs,),
        in_specs=[wide(0), wide(1), wide(2), wide(0), seg_c, seg_r, vec, far_spec, lse],
        out_specs=[
            wide(0),
            wide(0),
            wide(0),
            vec,
            pl.BlockSpec((1, 2, 2 * TQ), lambda p: (p, 0, 0)),
        ],
        out_shape=[
            heads_shape,
            heads_shape,
            heads_shape,
            jax.ShapeDtypeStruct((pairs, 2, WIDE), f32),
            jax.ShapeDtypeStruct((pairs, 2, 2 * TQ), f32),
        ],
        scratch_shapes=[
            pltpu.VMEM((SPAN, TQ), f32),
            pltpu.VMEM((SPAN, TQ), f32),
            pltpu.VMEM((seq_len, DH), f32),
            pltpu.VMEM((seq_len, DH), f32),
        ],
        compiler_params=kernel_params(),
        cost_estimate=pl.CostEstimate(
            flops=40 * DH * work, bytes_accessed=16 * seq_len * pairs * DH, transcendentals=work
        ),
        name="attend_back",
    )(qkv, qkv, qkv, mixed_grad, segs[:, None], segs[None, :], vectors, far, lse_rows)


def shift(value, axis, by):
    size = lax.axis_size(axis)
    return lax.ppermute(value, axis, [(i, (i + by) % size) for i in range(size)])


def block_at(stack, at):
    return lax.dynamic_index_in_dim(stack, at, 0, keepdims=False)


def place(stack, block, at):
    return lax.dynamic_update_slice(stack, block[None], (at,) + (jnp.int32(0),) * block.ndim)


def gather_axis(block, axis):
    size, me = lax.axis_size(axis), lax.axis_index(axis)
    stack = place(jnp.zeros((size,) + block.shape, block.dtype), block, me)
    for k in range(1, size):
        stack = place(stack, shift(block, axis, k), (me - k) % size)
    return stack


def exchange_axis(block_of, axis):
    size, me = lax.axis_size(axis), lax.axis_index(axis)
    own = block_of(me)
    stack = place(jnp.zeros((size,) + own.shape, own.dtype), own, me)
    for k in range(1, size):
        stack = place(stack, shift(block_of((me + k) % size), axis, k), (me - k) % size)
    return stack


def scatter_sum_axis(block_of, axis):
    size, me = lax.axis_size(axis), lax.axis_index(axis)
    arrived = [shift(block_of((me + k) % size).astype(bf16), axis, k) for k in range(1, size)]
    total = block_of(me).astype(f32)
    for block in arrived:
        total = total + block.astype(f32)
    return total


def gather_tokens(rows):
    parts, pieces = lax.axis_size("tensor"), lax.axis_size("ctx")
    t, z = lax.axis_index("tensor"), lax.axis_index("ctx")
    stack = jnp.zeros((pieces * parts,) + rows.shape, rows.dtype)
    for k in range(pieces):
        block = shift(rows, "ctx", k) if k else rows
        at = (z - k) % pieces
        stack = place(stack, block, at * parts + t)
        for j in range(1, parts):
            stack = place(stack, shift(block, "tensor", j), at * parts + (t - j) % parts)
    return stack.reshape(-1, rows.shape[1])


def scatter_tokens(partial):
    parts, pieces = lax.axis_size("tensor"), lax.axis_size("ctx")
    stack = partial.reshape(pieces, parts, -1, partial.shape[1])
    pieces_sum = scatter_sum_axis(
        lambda j: lax.dynamic_index_in_dim(stack, j, 1, keepdims=False), "tensor"
    )
    return scatter_sum_axis(lambda j: block_at(pieces_sum, j), "ctx")


def gather_weight(weights):
    pieces = lax.axis_size("ctx")

    def block_of(j):
        columns = [
            lax.dynamic_slice_in_dim(w, j * (w.shape[1] // pieces), w.shape[1] // pieces, 1)
            for w in weights
        ]
        return jnp.concatenate(columns, axis=1) if len(columns) > 1 else columns[0]

    stack = exchange_axis(block_of, "ctx")
    stack = stack.reshape(-1, stack.shape[-1])
    return gather_axis(stack, "dp").reshape(-1, stack.shape[-1])


def scatter_weight(grad, widths):
    dps, pieces = lax.axis_size("dp"), lax.axis_size("ctx")
    stack = grad.reshape(dps, -1, grad.shape[1])
    mine = scatter_sum_axis(lambda j: block_at(stack, j), "dp")
    mine = mine.reshape(pieces, -1, grad.shape[1])
    back = exchange_axis(lambda j: block_at(mine, j).astype(bf16), "ctx")
    outs, at = [], 0
    for width in widths:
        part = back[:, :, at : at + width].astype(f32)
        outs.append(jnp.transpose(part, (1, 0, 2)).reshape(part.shape[1], -1))
        at += width
    return outs


def root_mean_square_backward(grad, normalized, scale, gain):
    scaled = grad * gain
    return scale * (scaled - normalized * jnp.mean(scaled * normalized, axis=-1, keepdims=True))


def mm(a, b):
    return jnp.dot(a, b, preferred_element_type=f32)


def mm_nt(a, b):
    return dot_nt(a, b)


def mm_tn(a, b):
    return lax.dot_general(a, b, (((0,), (0,)), ((), ())), preferred_element_type=f32)


def inverse_scale(values):
    return lax.rsqrt(jnp.mean(values * values, axis=1, keepdims=True) + eps)


def shards(
    layer_input,
    segments,
    attn_gain,
    query_weight,
    key_weight,
    value_weight,
    output_weight,
    bias_table,
    ff_gain,
    gate_weight,
    up_weight,
    down_weight,
    cotangent,
):
    parts, pieces, dps = lax.axis_size("tensor"), lax.axis_size("ctx"), lax.axis_size("dp")
    t, z, s = lax.axis_index("tensor"), lax.axis_index("ctx"), lax.axis_index("dp")
    rows, width = layer_input.shape
    seq_len = rows * parts * pieces
    part_heads = bias_table.shape[1]
    heads = part_heads // pieces
    head_cols = heads * DH

    x_seq = gather_tokens(layer_input)
    gains = gather_axis(gather_axis(jnp.stack([attn_gain, ff_gain]), "ctx"), "dp")
    gains = jnp.transpose(gains, (2, 0, 1, 3)).reshape(2, width).astype(f32)
    gain_one, gain_two = gains[0:1], gains[1:2]
    w_qkv = gather_weight([query_weight, key_weight, value_weight])
    output_t = gather_axis(output_weight.T, "ctx")
    w_out = gather_axis(output_t, "dp").reshape(width, -1)
    w_gu = gather_weight([gate_weight, up_weight])
    w_down = gather_weight([down_weight.T])
    dy_seq = gather_tokens(cotangent)
    segs = gather_axis(segments, "ctx").reshape(seq_len)

    own_table = lax.dynamic_slice_in_dim(bias_table, z * heads, heads, 1)
    lanes_onehot = lane_buckets()
    vectors = jnp.dot(lanes_onehot, own_table, precision=highest).T.reshape(heads // 2, 2, WIDE)
    far = jnp.stack([own_table[NB // 2 - 1], own_table[NB - 1]], axis=1)

    x_wide = x_seq.astype(f32)
    normed_seq = (x_wide * inverse_scale(x_wide) * gain_one).astype(bf16)
    qkv = mm(normed_seq, w_qkv).astype(bf16)
    mixed_heads, lse_rows = attend(qkv, segs, vectors, far)
    mixed_stack = mixed_heads.reshape(pieces, -1, head_cols)
    mixed = exchange_axis(lambda j: block_at(mixed_stack, j), "ctx")
    mixed = jnp.transpose(mixed, (1, 0, 2)).reshape(rows * parts, -1)
    attn_part = mm_nt(mixed, w_out).reshape(parts, rows, width)
    attn_own = scatter_sum_axis(lambda j: block_at(attn_part, j), "tensor")

    x_own = layer_input.astype(f32)
    scale_one = inverse_scale(x_own)
    unit_one = x_own * scale_one
    hidden = x_own + attn_own
    scale_two = inverse_scale(hidden)
    unit_two = hidden * scale_two
    normed_two = (unit_two * gain_two).astype(bf16)

    normed_two_seq = gather_tokens(normed_two)
    units = w_down.shape[1]
    gate_up = mm(normed_two_seq, w_gu)
    gate, upper = gate_up[:, :units], gate_up[:, units:]
    inner_grad = mm(dy_seq, w_down)
    inner, gelu_pull = jax.vjp(lambda g, u: jax.nn.gelu(g, approximate=True) * u, gate, upper)
    inner = inner.astype(bf16)
    gate_grad, upper_grad = gelu_pull(inner_grad)
    gate_up_grad = jnp.concatenate([gate_grad.astype(bf16), upper_grad.astype(bf16)], axis=1)
    normed_two_part = mm_nt(gate_up_grad, w_gu).astype(bf16)
    normed_two_grad = scatter_tokens(normed_two_part)
    ff_part = mm_nt(inner, w_down).astype(bf16)
    ff_own = scatter_tokens(ff_part)
    block_output = (hidden + ff_own).astype(bf16)
    gate_out, up_out = scatter_weight(mm_tn(normed_two_seq, gate_up_grad), (units, units))
    (down_out,) = scatter_weight(mm_tn(dy_seq, inner), (units,))

    ff_gain_share = jnp.sum(normed_two_grad * unit_two, axis=0)
    hidden_grad = cotangent.astype(f32) + root_mean_square_backward(
        normed_two_grad, unit_two, scale_two, gain_two
    )
    attn_step = gather_axis(hidden_grad.astype(bf16), "tensor").reshape(rows * parts, width)
    mixed_grad = mm(attn_step, w_out).astype(bf16).reshape(rows * parts, pieces, head_cols)
    mixed_grad = exchange_axis(
        lambda j: lax.dynamic_index_in_dim(mixed_grad, j, 1, keepdims=False), "ctx"
    ).reshape(seq_len, head_cols)
    output_wgrad = mm_tn(attn_step, mixed)
    output_stack = output_wgrad.reshape(dps, -1, output_wgrad.shape[1])
    output_sum = scatter_sum_axis(lambda j: block_at(output_stack, j), "dp")
    output_sum = output_sum.reshape(pieces, -1, output_wgrad.shape[1])
    output_out = scatter_sum_axis(lambda j: block_at(output_sum, j), "ctx").T

    dq, dk, dv, diagonals, far_sums = attend_back(qkv, mixed_grad, segs, vectors, far, lse_rows)
    dqkv = jnp.concatenate([dq, dk, dv], axis=1)
    normed_one_part = mm_nt(dqkv, w_qkv).astype(bf16)
    normed_one_grad = scatter_tokens(normed_one_part)
    query_out, key_out, value_out = scatter_weight(
        mm_tn(normed_seq, dqkv), (head_cols, head_cols, head_cols)
    )
    attn_gain_share = jnp.sum(normed_one_grad * unit_one, axis=0)
    input_grads = (
        hidden_grad + root_mean_square_backward(normed_one_grad, unit_one, scale_one, gain_one)
    ).astype(bf16)

    far_total = jnp.sum(far_sums.reshape(heads, 2, TQ), axis=2)
    bias_own = jnp.dot(diagonals.reshape(heads, WIDE), lanes_onehot, precision=highest)
    bucket = jnp.arange(NB, dtype=jnp.int32)[None, :]
    bias_own = bias_own + jnp.where(bucket == NB // 2 - 1, far_total[:, 0:1], 0.0)
    bias_own = bias_own + jnp.where(bucket == NB - 1, far_total[:, 1:2], 0.0)
    bias_full = lax.dynamic_update_slice(
        jnp.zeros((NB, part_heads * parts), f32), bias_own.T, (jnp.int32(0), t * part_heads + z * heads)
    )
    own_segments = lax.dynamic_slice_in_dim(segments, t * rows, rows)
    valid = (own_segments != 0).astype(f32)
    out_values = block_output.astype(f32)
    grad_values = input_grads.astype(f32)
    local_sums = jnp.stack(
        [
            jnp.sum(valid * jnp.sum(out_values * out_values, axis=1)),
            jnp.sum(valid * jnp.sum(grad_values * grad_values, axis=1)),
            jnp.sum(valid),
        ]
    )
    gain_one_total, gain_two_total, bias_total, sums_total = lax.psum(
        (attn_gain_share, ff_gain_share, bias_full, local_sums), ("dp", "ctx", "tensor")
    )
    rms_stats = jnp.sqrt(sums_total[:2] / (sums_total[2] * width))
    return (
        block_output,
        input_grads,
        gain_one_total,
        query_out,
        key_out,
        value_out,
        output_out,
        bias_total,
        gain_two_total,
        gate_out,
        up_out,
        down_out.T,
        rms_stats,
    )


def solution(mesh):
    return jax.shard_map(
        shards,
        mesh=mesh,
        in_specs=(
            P(("dp", "ctx", "tensor"), None),
            P(("dp", "ctx")),
            P(("dp", "ctx")),
            P(("dp", "ctx"), "tensor"),
            P(("dp", "ctx"), "tensor"),
            P(("dp", "ctx"), "tensor"),
            P("tensor", ("dp", "ctx")),
            P(None, "tensor"),
            P(("dp", "ctx")),
            P(("dp", "ctx"), "tensor"),
            P(("dp", "ctx"), "tensor"),
            P("tensor", ("dp", "ctx")),
            P(("dp", "ctx", "tensor"), None),
        ),
        out_specs=(
            P(("dp", "ctx", "tensor"), None),
            P(("dp", "ctx", "tensor"), None),
            P(),
            P(("dp", "ctx"), "tensor"),
            P(("dp", "ctx"), "tensor"),
            P(("dp", "ctx"), "tensor"),
            P("tensor", ("dp", "ctx")),
            P(),
            P(),
            P(("dp", "ctx"), "tensor"),
            P(("dp", "ctx"), "tensor"),
            P("tensor", ("dp", "ctx")),
            P(),
        ),
        check_vma=False,
    )
```

time: 3540 us -> 1030 us (0.29)
  waiting for transfers between devices: 2800 us -> 430 us
  matrix products: 314 us -> 69.8 us
  starting transfers between devices: 2.15 us -> 214 us
  blocking collectives: 135 us -> 37.8 us
    reduce_scatter x13 -> x0, waiting for transfers between devices: 2030 us -> none  [the longest x1 436 us: shards(): lax.psum_scatter(weight_terms[5], ('dp', 'ctx'), scatter_dimension=0, til...]
    all_gather x13 -> x0, waiting for transfers between devices: 761 us -> none  [the longest x1 173 us: shards(): lax.all_gather(sharded[8], ('dp', 'ctx'), axis=1, tiled=True)]
    ppermute x0 -> x98, waiting for transfers between devices: none -> 430 us  [shift(): lax.ppermute(value, axis, [(i, (i + by) % size) for i in range(size)])]
    dot_general x135 -> x14, matrix products: 314 us -> 69.8 us  [the longest x4 23.9 us: mm(): return jnp.dot(a, b, preferred_element_type=f32)]
    ppermute x0 -> x98, starting transfers between devices: none -> 214 us  [shift(): lax.ppermute(value, axis, [(i, (i + by) % size) for i in range(size)])]
    reshape x96 -> x10, local copies, waits for them, and re-layouts: 138 us -> 15 us  [the longest x5 11.7 us: scatter_weight(): outs.append(jnp.transpose(part, (1, 0, 2)).reshape(part.shape[1], -1))]
    all_gather x3 -> x0, blocking collectives: 89.6 us -> none  [the longest x1 42.4 us: shards(): lax.all_gather(sharded[0], ('dp', 'ctx'), axis=0, tiled=True)]
    dynamic_update_slice x33 -> x82, local copies, waits for them, and re-layouts: 3.33 us -> 51.8 us  [the longest x81 51.6 us: place(): lax.dynamic_update_slice(stack, block[None], (at,) + (jnp.int32(0),) * bl...]
  transfers between devices with their start and end apart: 26 -> 98, of which waited for: 23 -> 35; matrix products, arithmetic and copies ran while one was open for 5% -> 22% of each run, Pallas kernels for 0% -> 1%
where the time goes in v1:
time: 1030 us; the launch traced here: 1020 us
  waiting for transfers between devices  430 us (42%)
  starting transfers between devices  214 us (21%)
  local copies, waits for them, and re-layouts  175 us (17%)
  matrix products  69.8 us (7%)
  other arithmetic  58 us (6%)
  blocking collectives  37.8 us (4%)
  Pallas kernels  32.4 us (3%)
    ppermute x98, waiting for transfers between devices, shift(): lax.ppermute(value, axis, [(i, (i + by) % size) for i in range(size)])  430 us
    ppermute x98, starting transfers between devices, shift(): lax.ppermute(value, axis, [(i, (i + by) % size) for i in range(size)])  214 us
    dynamic_update_slice x81, local copies, waits for them, and re-layouts, place(): lax.dynamic_update_slice(stack, block[None], (at,) + (jnp.int32(0),) * bl...  51.6 us
    psum x1, blocking collectives, shards(): lax.psum((attn_gain_share, ff_gain_share, bias_full, local_sums), ('dp',...  37.8 us
    unnamed x136, local copies, waits for them, and re-layouts  34.4 us
    dot_general x4, matrix products, mm(): return jnp.dot(a, b, preferred_element_type=f32)  23.9 us
    dot_general x4, matrix products, mm_tn(): lax.dot_general(a, b, (((0,), (0,)), ((), ())), preferred_element_type=f32)  23.4 us
    dot_general x4, matrix products, dot_nt(): lax.dot_general(a, b, (((1,), (1,)), ((), ())), preferred_element_type=f32)  21.7 us
  transfers between devices with their start and end apart: 98, of which 35 were waited for; matrix products, arithmetic and copies ran while one was open for 22% of the time, Pallas kernels for 1%

profile of v1, /device:TPU:0, one launch (start us, length us, event | category | flops | bytes accessed | tf_op | source)
XLA Modules:
  0.0 1019.8 jit_solution(13654191003852150372)
XLA Ops:
  53.8 21.4 %collective-permute-done.45 = bf16[128,640]{1,0:T(8,128)(2,1)S(1)} collective-permute-done((bf16[128,640]{1,0:T(8,128)(2,1)}, bf16[128,640]{1,0:T(8,128)(2,1)S(1)}, u32[]{:S(2)}, u32[]{:S(2)}) %collective-permute-start.45) | collective-permute-done | bytes 163872 | tf_op jit(solution)/shard_map/ppermute | solution.py:252
  75.2 11.8 %collective-permute-start.46 = (bf16[128,640]{1,0:T(8,128)(2,1)}, bf16[128,640]{1,0:T(8,128)(2,1)S(1)}, u32[]{:S(2)}, u32[]{:S(2)}) collective-permute-start(bf16[128,640]{1,0:T(8,128)(2,1)} %bitcast.524), channel_id=1, source_target_pairs={{0,4},{2,6},{4,0},{6,2},{1,5},{3,7},{5,1},{7,3},{8,12},{10,14},{12... | collective-permute-start | bytes 491528 | tf_op jit(solution)/shard_map/ppermute | solution.py:252
  87.7 5.7 collective-permute-done.46
  95.2 3.6 collective-permute-done.47
  101.2 3.9 collective-permute-start.15
  105.8 4.1 collective-permute-done.14
  112.6 3.3 collective-permute-start.26
  118.1 3.9 collective-permute-done.25
  123.3 8.4 collective-permute-done.26
  133.3 4.4 collective-permute-start.39
  138.5 7.0 collective-permute-done.39
  146.2 14.9 %collective-permute-done.40 = bf16[128,1280]{1,0:T(8,128)(2,1)S(1)} collective-permute-done((bf16[128,1280]{1,0:T(8,128)(2,1)S(1)}, bf16[128,1280]{1,0:T(8,128)(2,1)S(1)}, u32[]{:S(2)}, u32[]{:S(2)}) %collective-permute-start.40) | collective-permute-done | bytes 327712 | tf_op jit(solution)/shard_map/ppermute | solution.py:252
  164.6 6.5 collective-permute-done.41
  188.4 4.1 collective-permute-done.48
  194.2 12.5 %collective-permute-done.49 = bf16[512,640]{1,0:T(8,128)(2,1)S(1)} collective-permute-done((bf16[512,640]{1,0:T(8,128)(2,1)}, bf16[512,640]{1,0:T(8,128)(2,1)S(1)}, u32[]{:S(2)}, u32[]{:S(2)}) %collective-permute-start.49) | collective-permute-done | bytes 655392 | tf_op jit(solution)/shard_map/ppermute | solution.py:252
  206.7 4.0 collective-permute-start.18
  210.8 4.3 collective-permute-start.5
  215.2 8.3 collective-permute-done.16
  223.5 4.8 collective-permute-start.58
  228.4 9.7 collective-permute-done.17
  238.2 4.0 collective-permute-start.60
  242.4 4.3 collective-permute-start.28
  258.2 4.5 convolution_convert_fusion.3.q_ref.k_ref.v_ref
  262.7 5.3 fusion.1
  270.5 14.9 %attend.1 = (bf16[1024,256]{1,0:T(8,128)(2,1)}, f32[2,2,1024]{2,1,0:T(2,128)}) custom-call(bf16[1024,768]{1,0:T(8,128)(2,1)} %convolution_convert_fusion.3.q_ref.k_ref.v_ref, bf16[1024,768]{1,0:T(8,128)(2,1)} %convolution_convert_fusion.3.q_ref.k_ref.v_ref, bf16[1024,768]{1,0:T(8,128)(2,1)} %convolution_convert_fusion.3.q_ref.k_ref.v_ref, ...), custom_call_target="tpu_custom_call" | custom-call | flops 4294967296 | bytes 1048576 | tf_op jit(solution)/shard_map/attend/pallas_call | solution.py:194
  290.7 6.4 copy.187
  297.1 6.4 copy.201
  305.8 7.1 collective-permute-done.23
  331.3 3.6 fusion.107
  336.5 14.1 %collective-permute-done.43 = bf16[512,1280]{1,0:T(8,128)(2,1)} collective-permute-done((bf16[512,1280]{1,0:T(8,128)(2,1)}, bf16[512,1280]{1,0:T(8,128)(2,1)}, u32[]{:S(2)}, u32[]{:S(2)}) %collective-permute-start.43) | collective-permute-done | bytes 1310752 | tf_op jit(solution)/shard_map/ppermute | solution.py:252
  355.8 3.8 collective-permute-start.35
  359.8 12.7 %collective-permute-done.33 = bf16[128,2048]{1,0:T(8,128)(2,1)S(1)} collective-permute-done((bf16[128,2048]{1,0:T(8,128)(2,1)S(1)}, bf16[128,2048]{1,0:T(8,128)(2,1)S(1)}, u32[]{:S(2)}, u32[]{:S(2)}) %collective-permute-start.33) | collective-permute-done | bytes 524320 | tf_op jit(solution)/shard_map/ppermute | solution.py:252
  372.5 22.1 %collective-permute-done.35 = bf16[128,2048]{1,0:T(8,128)(2,1)S(1)} collective-permute-done((bf16[128,2048]{1,0:T(8,128)(2,1)S(1)}, bf16[128,2048]{1,0:T(8,128)(2,1)S(1)}, u32[]{:S(2)}, u32[]{:S(2)}) %collective-permute-start.35) | collective-permute-done | bytes 524320 | tf_op jit(solution)/shard_map/ppermute | solution.py:252
  401.0 6.4 copy.210
  407.4 9.0 fusion.108
  416.4 8.3 fusion.8
  424.7 9.5 convolution_convert_fusion
  434.3 9.1 fusion.11
  443.4 4.9 fusion.27
  449.5 30.1 %collective-permute-start.94 = (bf16[512,640]{1,0:T(8,128)(2,1)}, bf16[512,640]{1,0:T(8,128)(2,1)S(1)}, u32[]{:S(2)}, u32[]{:S(2)}) collective-permute-start(bf16[512,640]{1,0:T(8,128)(2,1)} %get-tuple-element.105), channel_id=1, source_target_pairs={{0,24},{8,0},{16,8},{24,16},{1,25},{9,1},{17,9},{25,17},{2,26},{10... | collective-permute-start | bytes 1966088 | tf_op jit(solution)/shard_map/ppermute | solution.py:252
  485.5 5.0 convolution_convert_fusion.1
  490.5 4.5 collective-permute-done.94
  499.1 69.3 %collective-permute-done.93 = bf16[512,640]{1,0:T(8,128)(2,1)} collective-permute-done((bf16[512,640]{1,0:T(8,128)(2,1)}, bf16[512,640]{1,0:T(8,128)(2,1)}, u32[]{:S(2)}, u32[]{:S(2)}) %collective-permute-start.93) | collective-permute-done | bytes 655392 | tf_op jit(solution)/shard_map/ppermute | solution.py:252
  570.2 11.8 %collective-permute-start.95 = (bf16[128,640]{1,0:T(8,128)(2,1)S(1)}, bf16[128,640]{1,0:T(8,128)(2,1)S(1)}, u32[]{:S(2)}, u32[]{:S(2)}) collective-permute-start(bf16[128,640]{1,0:T(8,128)(2,1)S(1)} %get-tuple-element.137), channel_id=1, source_target_pairs={{0,2},{2,4},{4,6},{6,0},{1,3},{3,5},{5,7},{7,1},{8,10},{10,12},{12... | collective-permute-start | bytes 491528 | tf_op jit(solution)/shard_map/ppermute | solution.py:252
  588.3 8.4 collective-permute-done.96
  608.2 3.4 collective-permute-start.91
  614.7 12.6 %collective-permute-done.90 = bf16[128,1280]{1,0:T(8,128)(2,1)S(1)} collective-permute-done((bf16[128,1280]{1,0:T(8,128)(2,1)S(1)}, bf16[128,1280]{1,0:T(8,128)(2,1)S(1)}, u32[]{:S(2)}, u32[]{:S(2)}) %collective-permute-start.90) | collective-permute-done | bytes 327712 | tf_op jit(solution)/shard_map/ppermute | solution.py:252
  632.4 8.0 collective-permute-start.65
  655.8 29.0 %collective-permute-done.64 = bf16[128,2048]{1,0:T(8,128)(2,1)} collective-permute-done((bf16[128,2048]{1,0:T(8,128)(2,1)S(1)}, bf16[128,2048]{1,0:T(8,128)(2,1)}, u32[]{:S(2)}, u32[]{:S(2)}) %collective-permute-start.64) | collective-permute-done | bytes 524320 | tf_op jit(solution)/shard_map/ppermute | solution.py:252
  689.3 4.7 convert_add_fusion.2
  704.8 3.3 collective-permute-start.69
  710.4 5.9 fusion.109
  719.9 17.5 %attend_back.1 = (bf16[1024,256]{1,0:T(8,128)(2,1)}, bf16[1024,256]{1,0:T(8,128)(2,1)}, bf16[1024,256]{1,0:T(8,128)(2,1)}, f32[2,2,1024]{2,1,0:T(2,128)}, f32[2,2,512]{2,1,0:T(2,128)}) custom-call(bf16[1024,768]{1,0:T(8,128)(2,1)} %convolution_convert_fusion.3.q_ref.k_ref.v_ref, bf16[1024,768]{1,0:T(8,128)(2,1)} %convolution_convert_fusion.3.q_ref.k_ref.v_ref, ...), custom_call_target="tpu_custom_call" | custom-call | flops 10737418240 | bytes 2097152 | tf_op jit(solution)/shard_map/attend_back/pallas_call | solution.py:218
  740.7 3.5 fusion.17
  747.2 4.9 fusion.37
  756.2 3.7 convolution_convert_fusion.2
  759.9 7.8 collective-permute-done.76
  769.2 64.0 %collective-permute-done.75 = bf16[512,768]{1,0:T(8,128)(2,1)} collective-permute-done((bf16[512,768]{1,0:T(8,128)(2,1)S(1)}, bf16[512,768]{1,0:T(8,128)(2,1)}, u32[]{:S(2)}, u32[]{:S(2)}) %collective-permute-start.75) | collective-permute-done | bytes 786464 | tf_op jit(solution)/shard_map/ppermute | solution.py:252
  872.7 7.4 collective-permute-start.73
  897.9 5.9 collective-permute-start.53
  905.8 16.5 %collective-permute-start.52 = (bf16[128,2048]{1,0:T(8,128)(2,1)}, bf16[128,2048]{1,0:T(8,128)(2,1)S(1)}, u32[]{:S(2)}, u32[]{:S(2)}) collective-permute-start(bf16[128,2048]{1,0:T(8,128)(2,1)} %get-tuple-element.114), channel_id=1, source_target_pairs={{0,2},{2,4},{4,6},{6,0},{1,3},{3,5},{5,7},{7,1},{8,10},{10,12},{12... | collective-permute-start | bytes 1572872 | tf_op jit(solution)/shard_map/ppermute | solution.py:252
  922.3 29.7 %collective-permute-done.72 = bf16[128,2048]{1,0:T(8,128)(2,1)} collective-permute-done((bf16[128,2048]{1,0:T(8,128)(2,1)}, bf16[128,2048]{1,0:T(8,128)(2,1)}, u32[]{:S(2)}, u32[]{:S(2)}) %collective-permute-start.72) | collective-permute-done | bytes 524320 | tf_op jit(solution)/shard_map/ppermute | solution.py:252
  954.3 19.8 %collective-permute-done.53 = bf16[128,2048]{1,0:T(8,128)(2,1)S(1)} collective-permute-done((bf16[128,2048]{1,0:T(8,128)(2,1)}, bf16[128,2048]{1,0:T(8,128)(2,1)S(1)}, u32[]{:S(2)}, u32[]{:S(2)}) %collective-permute-start.53) | collective-permute-done | bytes 524320 | tf_op jit(solution)/shard_map/ppermute | solution.py:252
  980.0 37.8 %all-reduce = (f32[2048]{0:T(1024)}, f32[32,32]{1,0:T(8,128)}, f32[2048]{0:T(1024)}, f32[3]{0:T(128)S(1)}) all-reduce(f32[2048]{0:T(1024)S(1)} %get-tuple-element.68, f32[32,32]{1,0:T(8,128)S(1)} %dynamic_update_slice.355, f32[2048]{0:T(1024)S(1)} %get-tuple-element.66, ...), channel_id=1, replica_groups=mesh['dp'=4,'ctx'=4,'tensor'=2] {'dp','ctx','tensor'}, use_global_device_ids=true, to_apply=%region_6.7 | all-reduce | flops 5123 | bytes 40984 | tf_op jit(solution)/shard_map/psum | solution.py:482
  (478 shorter events, 299.6 us)
Async XLA Ops:
  1.4 34.7 %collective-permute-start.7 = (bf16[2,128]{1,0:T(2,128)(2,1)S(1)}, bf16[2,128]{1,0:T(2,128)(2,1)S(1)}, u32[]{:S(2)}, u32[]{:S(2)}) collective-permute-start(bf16[2,128]{1,0:T(2,128)(2,1)S(1)} %get-tuple-element.92), channel_id=1, source_target_pairs={{0,2},{2,4},{4,6},{6,0},{1,3},{3,5},{5,7},{7,1},{8,10},{10,12},{12... | collective-permute-start | bytes 1544 | tf_op jit(solution)/shard_map/ppermute | solution.py:252
  4.4 31.9 %collective-permute-start.8 = (bf16[2,128]{1,0:T(2,128)(2,1)S(1)}, bf16[2,128]{1,0:T(2,128)(2,1)S(1)}, u32[]{:S(2)}, u32[]{:S(2)}) collective-permute-start(bf16[2,128]{1,0:T(2,128)(2,1)S(1)} %get-tuple-element.92), channel_id=1, source_target_pairs={{0,4},{2,6},{4,0},{6,2},{1,5},{3,7},{5,1},{7,3},{8,12},{10,14},{12... | collective-permute-start | bytes 1544 | tf_op jit(solution)/shard_map/ppermute | solution.py:252
  7.0 32.2 %collective-permute-start.9 = (bf16[2,128]{1,0:T(2,128)(2,1)S(1)}, bf16[2,128]{1,0:T(2,128)(2,1)S(1)}, u32[]{:S(2)}, u32[]{:S(2)}) collective-permute-start(bf16[2,128]{1,0:T(2,128)(2,1)S(1)} %get-tuple-element.92), channel_id=1, source_target_pairs={{0,6},{2,0},{4,2},{6,4},{1,7},{3,1},{5,3},{7,5},{8,14},{10,8},{12,... | collective-permute-start | bytes 1544 | tf_op jit(solution)/shard_map/ppermute | solution.py:252
  8.4 165.3 %collective-permute-start = (bf16[128,2048]{1,0:T(8,128)(2,1)}, bf16[128,2048]{1,0:T(8,128)(2,1)}, u32[]{:S(2)}, u32[]{:S(2)}) collective-permute-start(bf16[128,2048]{1,0:T(8,128)(2,1)} %param.13), channel_id=1, source_target_pairs={{0,1},{1,0},{2,3},{3,2},{4,5},{5,4},{6,7},{7,6},{8,9},{9,8},{10,11... | collective-permute-start | bytes 1572872 | tf_op jit(solution)/shard_map/ppermute | solution.py:252
  8.4 32.5 %collective-permute-start.19 = (s32[256]{0:T(256)}, s32[256]{0:T(256)S(1)}, u32[]{:S(2)}, u32[]{:S(2)}) collective-permute-start(s32[256]{0:T(256)} %param.14), channel_id=1, source_target_pairs={{0,2},{2,4},{4,6},{6,0},{1,3},{3,5},{5,7},{7,1},{8,10},{10,12},{12... | collective-permute-start | bytes 3080 | tf_op jit(solution)/shard_map/ppermute | solution.py:252
  40.8 138.0 %collective-permute-start.1 = (bf16[128,2048]{1,0:T(8,128)(2,1)S(1)}, bf16[128,2048]{1,0:T(8,128)(2,1)}, u32[]{:S(2)}, u32[]{:S(2)}) collective-permute-start(bf16[128,2048]{1,0:T(8,128)(2,1)S(1)} %copy-done.4), channel_id=1, source_target_pairs={{0,2},{2,4},{4,6},{6,0},{1,3},{3,5},{5,7},{7,1},{8,10},{10,12},{12... | collective-permute-start | bytes 1572872 | tf_op jit(solution)/shard_map/ppermute | solution.py:252
  41.5 200.9 %collective-permute-start.3 = (bf16[128,2048]{1,0:T(8,128)(2,1)S(1)}, bf16[128,2048]{1,0:T(8,128)(2,1)S(1)}, u32[]{:S(2)}, u32[]{:S(2)}) collective-permute-start(bf16[128,2048]{1,0:T(8,128)(2,1)S(1)} %copy-done.4), channel_id=1, source_target_pairs={{0,4},{2,6},{4,0},{6,2},{1,5},{3,7},{5,1},{7,3},{8,12},{10,14},{12... | collective-permute-start | bytes 1572872 | tf_op jit(solution)/shard_map/ppermute | solution.py:252
  43.0 58.1 %collective-permute-start.13 = (bf16[128,768]{1,0:T(8,128)(2,1)}, bf16[128,768]{1,0:T(8,128)(2,1)S(1)}, u32[]{:S(2)}, u32[]{:S(2)}) collective-permute-start(bf16[128,768]{1,0:T(8,128)(2,1)} %pad_maximum_fusion.6), channel_id=1, source_target_pairs={{0,2},{2,4},{4,6},{6,0},{1,3},{3,5},{5,7},{7,1},{8,10},{10,12},{12... | collective-permute-start | bytes 589832 | tf_op jit(solution)/shard_map/ppermute | solution.py:252
  53.7 21.5 %collective-permute-start.45 = (bf16[128,640]{1,0:T(8,128)(2,1)}, bf16[128,640]{1,0:T(8,128)(2,1)S(1)}, u32[]{:S(2)}, u32[]{:S(2)}) collective-permute-start(bf16[128,640]{1,0:T(8,128)(2,1)} %bitcast.525), channel_id=1, source_target_pairs={{0,2},{2,4},{4,6},{6,0},{1,3},{3,5},{5,7},{7,1},{8,10},{10,12},{12... | collective-permute-start | bytes 491528 | tf_op jit(solution)/shard_map/ppermute | solution.py:252
  75.2 18.1 %collective-permute-start.46 = (bf16[128,640]{1,0:T(8,128)(2,1)}, bf16[128,640]{1,0:T(8,128)(2,1)S(1)}, u32[]{:S(2)}, u32[]{:S(2)}) collective-permute-start(bf16[128,640]{1,0:T(8,128)(2,1)} %bitcast.524), channel_id=1, source_target_pairs={{0,4},{2,6},{4,0},{6,2},{1,5},{3,7},{5,1},{7,3},{8,12},{10,14},{12... | collective-permute-start | bytes 491528 | tf_op jit(solution)/shard_map/ppermute | solution.py:252
  112.6 19.0 %collective-permute-start.26 = (bf16[128,1024]{1,0:T(8,128)(2,1)S(1)}, bf16[128,1024]{1,0:T(8,128)(2,1)S(1)}, u32[]{:S(2)}, u32[]{:S(2)}) collective-permute-start(bf16[128,1024]{1,0:T(8,128)(2,1)S(1)} %bitcast.506), channel_id=1, source_target_pairs={{0,4},{2,6},{4,0},{6,2},{1,5},{3,7},{5,1},{7,3},{8,12},{10,14},{12... | collective-permute-start | bytes 786440 | tf_op jit(solution)/shard_map/ppermute | solution.py:252
  131.7 45.6 %collective-permute-start.55 = (bf16[128,2048]{1,0:T(8,128)(2,1)S(1)}, bf16[128,2048]{1,0:T(8,128)(2,1)S(1)}, u32[]{:S(2)}, u32[]{:S(2)}) collective-permute-start(bf16[128,2048]{1,0:T(8,128)(2,1)S(1)} %copy-done.8), channel_id=1, source_target_pairs={{0,1},{1,0},{2,3},{3,2},{4,5},{5,4},{6,7},{7,6},{8,9},{9,8},{10,11... | collective-permute-start | bytes 1572872 | tf_op jit(solution)/shard_map/ppermute | solution.py:252
  173.7 18.9 %collective-permute-start.48 = (bf16[512,640]{1,0:T(8,128)(2,1)}, bf16[512,640]{1,0:T(8,128)(2,1)S(1)}, u32[]{:S(2)}, u32[]{:S(2)}) collective-permute-start(bf16[512,640]{1,0:T(8,128)(2,1)} %bitcast.87), channel_id=1, source_target_pairs={{0,8},{8,16},{16,24},{24,0},{1,9},{9,17},{17,25},{25,1},{2,10},{10... | collective-permute-start | bytes 1966088 | tf_op jit(solution)/shard_map/ppermute | solution.py:252
  177.3 29.4 %collective-permute-start.49 = (bf16[512,640]{1,0:T(8,128)(2,1)}, bf16[512,640]{1,0:T(8,128)(2,1)S(1)}, u32[]{:S(2)}, u32[]{:S(2)}) collective-permute-start(bf16[512,640]{1,0:T(8,128)(2,1)} %bitcast.87), channel_id=1, source_target_pairs={{0,16},{8,24},{16,0},{24,8},{1,17},{9,25},{17,1},{25,9},{2,18},{10... | collective-permute-start | bytes 1966088 | tf_op jit(solution)/shard_map/ppermute | solution.py:252
  178.8 31.9 %collective-permute-start.50 = (bf16[512,640]{1,0:T(8,128)(2,1)}, bf16[512,640]{1,0:T(8,128)(2,1)S(1)}, u32[]{:S(2)}, u32[]{:S(2)}) collective-permute-start(bf16[512,640]{1,0:T(8,128)(2,1)} %bitcast.87), channel_id=1, source_target_pairs={{0,24},{8,0},{16,8},{24,16},{1,25},{9,1},{17,9},{25,17},{2,26},{10... | collective-permute-start | bytes 1966088 | tf_op jit(solution)/shard_map/ppermute | solution.py:252
  186.1 37.4 %collective-permute-start.16 = (bf16[512,768]{1,0:T(8,128)(2,1)}, bf16[512,768]{1,0:T(8,128)(2,1)S(1)}, u32[]{:S(2)}, u32[]{:S(2)}) collective-permute-start(bf16[512,768]{1,0:T(8,128)(2,1)} %bitcast.26), channel_id=1, source_target_pairs={{0,8},{8,16},{16,24},{24,0},{1,9},{9,17},{17,25},{25,1},{2,10},{10... | collective-permute-start | bytes 2359304 | tf_op jit(solution)/shard_map/ppermute | solution.py:252
  192.6 45.5 %collective-permute-start.17 = (bf16[512,768]{1,0:T(8,128)(2,1)}, bf16[512,768]{1,0:T(8,128)(2,1)S(1)}, u32[]{:S(2)}, u32[]{:S(2)}) collective-permute-start(bf16[512,768]{1,0:T(8,128)(2,1)} %bitcast.26), channel_id=1, source_target_pairs={{0,16},{8,24},{16,0},{24,8},{1,17},{9,25},{17,1},{25,9},{2,18},{10... | collective-permute-start | bytes 2359304 | tf_op jit(solution)/shard_map/ppermute | solution.py:252
  206.7 31.6 %collective-permute-start.18 = (bf16[512,768]{1,0:T(8,128)(2,1)}, bf16[512,768]{1,0:T(8,128)(2,1)S(1)}, u32[]{:S(2)}, u32[]{:S(2)}) collective-permute-start(bf16[512,768]{1,0:T(8,128)(2,1)} %bitcast.26), channel_id=1, source_target_pairs={{0,24},{8,0},{16,8},{24,16},{1,25},{9,1},{17,9},{25,17},{2,26},{10... | collective-permute-start | bytes 2359304 | tf_op jit(solution)/shard_map/ppermute | solution.py:252
  210.8 37.6 %collective-permute-start.5 = (bf16[128,2048]{1,0:T(8,128)(2,1)S(1)}, bf16[128,2048]{1,0:T(8,128)(2,1)S(1)}, u32[]{:S(2)}, u32[]{:S(2)}) collective-permute-start(bf16[128,2048]{1,0:T(8,128)(2,1)S(1)} %copy-done.4), channel_id=1, source_target_pairs={{0,6},{2,0},{4,2},{6,4},{1,7},{3,1},{5,3},{7,5},{8,14},{10,8},{12,... | collective-permute-start | bytes 1572872 | tf_op jit(solution)/shard_map/ppermute | solution.py:252
  223.5 44.5 %collective-permute-start.58 = (bf16[128,2048]{1,0:T(8,128)(2,1)S(1)}, bf16[128,2048]{1,0:T(8,128)(2,1)S(1)}, u32[]{:S(2)}, u32[]{:S(2)}) collective-permute-start(bf16[128,2048]{1,0:T(8,128)(2,1)S(1)} %copy-done.8), channel_id=1, source_target_pairs={{0,4},{2,6},{4,0},{6,2},{1,5},{3,7},{5,1},{7,3},{8,12},{10,14},{12... | collective-permute-start | bytes 1572872 | tf_op jit(solution)/shard_map/ppermute | solution.py:252
  238.2 48.0 %collective-permute-start.60 = (bf16[128,2048]{1,0:T(8,128)(2,1)S(1)}, bf16[128,2048]{1,0:T(8,128)(2,1)S(1)}, u32[]{:S(2)}, u32[]{:S(2)}) collective-permute-start(bf16[128,2048]{1,0:T(8,128)(2,1)S(1)} %copy-done.8), channel_id=1, source_target_pairs={{0,6},{2,0},{4,2},{6,4},{1,7},{3,1},{5,3},{7,5},{8,14},{10,8},{12,... | collective-permute-start | bytes 1572872 | tf_op jit(solution)/shard_map/ppermute | solution.py:252
  242.4 80.3 %collective-permute-start.28 = (bf16[4,128,1024]{2,1,0:T(8,128)(2,1)S(1)}, bf16[4,128,1024]{2,1,0:T(8,128)(2,1)}, u32[]{:S(2)}, u32[]{:S(2)}) collective-permute-start(bf16[4,128,1024]{2,1,0:T(8,128)(2,1)S(1)} %bitcast_dynamic-update-slice_fusion.49), channel_id=1, source_target_pairs={{0,8},{8,16},{16,24},{24,0},{1,9},{9,17},{17,25},{25,1},{2,10},{10... | collective-permute-start | bytes 3145736 | tf_op jit(solution)/shard_map/ppermute | solution.py:252
  248.3 78.2 %collective-permute-start.29 = (bf16[4,128,1024]{2,1,0:T(8,128)(2,1)S(1)}, bf16[4,128,1024]{2,1,0:T(8,128)(2,1)}, u32[]{:S(2)}, u32[]{:S(2)}) collective-permute-start(bf16[4,128,1024]{2,1,0:T(8,128)(2,1)S(1)} %bitcast_dynamic-update-slice_fusion.49), channel_id=1, source_target_pairs={{0,16},{8,24},{16,0},{24,8},{1,17},{9,25},{17,1},{25,9},{2,18},{10... | collective-permute-start | bytes 3145736 | tf_op jit(solution)/shard_map/ppermute | solution.py:252
  250.8 18.9 %collective-permute-start.57 = (bf16[128,2048]{1,0:T(8,128)(2,1)S(1)}, bf16[128,2048]{1,0:T(8,128)(2,1)S(1)}, u32[]{:S(2)}, u32[]{:S(2)}) collective-permute-start(bf16[128,2048]{1,0:T(8,128)(2,1)S(1)} %collective-permute-done.56), channel_id=1, source_target_pairs={{0,1},{1,0},{2,3},{3,2},{4,5},{5,4},{6,7},{7,6},{8,9},{9,8},{10,11... | collective-permute-start | bytes 1572872 | tf_op jit(solution)/shard_map/ppermute | solution.py:252
  268.0 60.8 %collective-permute-start.30 = (bf16[4,128,1024]{2,1,0:T(8,128)(2,1)S(1)}, bf16[4,128,1024]{2,1,0:T(8,128)(2,1)}, u32[]{:S(2)}, u32[]{:S(2)}) collective-permute-start(bf16[4,128,1024]{2,1,0:T(8,128)(2,1)S(1)} %bitcast_dynamic-update-slice_fusion.49), channel_id=1, source_target_pairs={{0,24},{8,0},{16,8},{24,16},{1,25},{9,1},{17,9},{25,17},{2,26},{10... | collective-permute-start | bytes 3145736 | tf_op jit(solution)/shard_map/ppermute | solution.py:252
  286.3 48.7 %collective-permute-start.42 = (bf16[512,1280]{1,0:T(8,128)(2,1)}, bf16[512,1280]{1,0:T(8,128)(2,1)}, u32[]{:S(2)}, u32[]{:S(2)}) collective-permute-start(bf16[512,1280]{1,0:T(8,128)(2,1)} %bitcast.73), channel_id=1, source_target_pairs={{0,8},{8,16},{16,24},{24,0},{1,9},{9,17},{17,25},{25,1},{2,10},{10... | collective-permute-start | bytes 3932168 | tf_op jit(solution)/shard_map/ppermute | solution.py:252
  319.2 31.3 %collective-permute-start.43 = (bf16[512,1280]{1,0:T(8,128)(2,1)}, bf16[512,1280]{1,0:T(8,128)(2,1)}, u32[]{:S(2)}, u32[]{:S(2)}) collective-permute-start(bf16[512,1280]{1,0:T(8,128)(2,1)} %bitcast.73), channel_id=1, source_target_pairs={{0,16},{8,24},{16,0},{24,8},{1,17},{9,25},{17,1},{25,9},{2,18},{10... | collective-permute-start | bytes 3932168 | tf_op jit(solution)/shard_map/ppermute | solution.py:252
  322.7 36.9 %collective-permute-start.44 = (bf16[512,1280]{1,0:T(8,128)(2,1)}, bf16[512,1280]{1,0:T(8,128)(2,1)S(1)}, u32[]{:S(2)}, u32[]{:S(2)}) collective-permute-start(bf16[512,1280]{1,0:T(8,128)(2,1)} %bitcast.73), channel_id=1, source_target_pairs={{0,24},{8,0},{16,8},{24,16},{1,25},{9,1},{17,9},{25,17},{2,26},{10... | collective-permute-start | bytes 3932168 | tf_op jit(solution)/shard_map/ppermute | solution.py:252
  355.8 39.3 %collective-permute-start.32 = (bf16[128,2048]{1,0:T(8,128)(2,1)S(1)}, bf16[128,2048]{1,0:T(8,128)(2,1)S(1)}, u32[]{:S(2)}, u32[]{:S(2)}) collective-permute-start(bf16[128,2048]{1,0:T(8,128)(2,1)S(1)} %get-tuple-element.88), channel_id=1, source_target_pairs={{0,1},{1,0},{2,3},{3,2},{4,5},{5,4},{6,7},{7,6},{8,9},{9,8},{10,11... | collective-permute-start | bytes 1572872 | tf_op jit(solution)/shard_map/ppermute | solution.py:252
  355.8 38.7 %collective-permute-start.35 = (bf16[128,2048]{1,0:T(8,128)(2,1)S(1)}, bf16[128,2048]{1,0:T(8,128)(2,1)S(1)}, u32[]{:S(2)}, u32[]{:S(2)}) collective-permute-start(bf16[128,2048]{1,0:T(8,128)(2,1)S(1)} %get-tuple-element.88), channel_id=1, source_target_pairs={{0,4},{2,6},{4,0},{6,2},{1,5},{3,7},{5,1},{7,3},{8,12},{10,14},{12... | collective-permute-start | bytes 1572872 | tf_op jit(solution)/shard_map/ppermute | solution.py:252
  359.6 34.9 %collective-permute-start.37 = (bf16[128,2048]{1,0:T(8,128)(2,1)S(1)}, bf16[128,2048]{1,0:T(8,128)(2,1)S(1)}, u32[]{:S(2)}, u32[]{:S(2)}) collective-permute-start(bf16[128,2048]{1,0:T(8,128)(2,1)S(1)} %get-tuple-element.88), channel_id=1, source_target_pairs={{0,6},{2,0},{4,2},{6,4},{1,7},{3,1},{5,3},{7,5},{8,14},{10,8},{12,... | collective-permute-start | bytes 1572872 | tf_op jit(solution)/shard_map/ppermute | solution.py:252
  372.5 24.3 %collective-permute-start.34 = (bf16[128,2048]{1,0:T(8,128)(2,1)S(1)}, bf16[128,2048]{1,0:T(8,128)(2,1)S(1)}, u32[]{:S(2)}, u32[]{:S(2)}) collective-permute-start(bf16[128,2048]{1,0:T(8,128)(2,1)S(1)} %collective-permute-done.33), channel_id=1, source_target_pairs={{0,1},{1,0},{2,3},{3,2},{4,5},{5,4},{6,7},{7,6},{8,9},{9,8},{10,11... | collective-permute-start | bytes 1572872 | tf_op jit(solution)/shard_map/ppermute | solution.py:252
  449.5 45.6 %collective-permute-start.94 = (bf16[512,640]{1,0:T(8,128)(2,1)}, bf16[512,640]{1,0:T(8,128)(2,1)S(1)}, u32[]{:S(2)}, u32[]{:S(2)}) collective-permute-start(bf16[512,640]{1,0:T(8,128)(2,1)} %get-tuple-element.105), channel_id=1, source_target_pairs={{0,24},{8,0},{16,8},{24,16},{1,25},{9,1},{17,9},{25,17},{2,26},{10... | collective-permute-start | bytes 1966088 | tf_op jit(solution)/shard_map/ppermute | solution.py:252
  481.5 115.3 %collective-permute-start.88 = (bf16[512,1280]{1,0:T(8,128)(2,1)}, bf16[512,1280]{1,0:T(8,128)(2,1)S(1)}, u32[]{:S(2)}, u32[]{:S(2)}) collective-permute-start(bf16[512,1280]{1,0:T(8,128)(2,1)} %get-tuple-element.94), channel_id=1, source_target_pairs={{0,24},{8,0},{16,8},{24,16},{1,25},{9,1},{17,9},{25,17},{2,26},{10... | collective-permute-start | bytes 3932168 | tf_op jit(solution)/shard_map/ppermute | solution.py:252
  481.5 117.4 %collective-permute-start.87 = (bf16[512,1280]{1,0:T(8,128)(2,1)}, bf16[512,1280]{1,0:T(8,128)(2,1)S(1)}, u32[]{:S(2)}, u32[]{:S(2)}) collective-permute-start(bf16[512,1280]{1,0:T(8,128)(2,1)} %get-tuple-element.95), channel_id=1, source_target_pairs={{0,16},{8,24},{16,0},{24,8},{1,17},{9,25},{17,1},{25,9},{2,18},{10... | collective-permute-start | bytes 3932168 | tf_op jit(solution)/shard_map/ppermute | solution.py:252
  482.0 86.4 %collective-permute-start.93 = (bf16[512,640]{1,0:T(8,128)(2,1)}, bf16[512,640]{1,0:T(8,128)(2,1)}, u32[]{:S(2)}, u32[]{:S(2)}) collective-permute-start(bf16[512,640]{1,0:T(8,128)(2,1)} %get-tuple-element.106), channel_id=1, source_target_pairs={{0,16},{8,24},{16,0},{24,8},{1,17},{9,25},{17,1},{25,9},{2,18},{10... | collective-permute-start | bytes 1966088 | tf_op jit(solution)/shard_map/ppermute | solution.py:252
  483.5 84.9 %collective-permute-start.92 = (bf16[512,640]{1,0:T(8,128)(2,1)S(1)}, bf16[512,640]{1,0:T(8,128)(2,1)}, u32[]{:S(2)}, u32[]{:S(2)}) collective-permute-start(bf16[512,640]{1,0:T(8,128)(2,1)S(1)} %get-tuple-element.104), channel_id=1, source_target_pairs={{0,8},{8,16},{16,24},{24,0},{1,9},{9,17},{17,25},{25,1},{2,10},{10... | collective-permute-start | bytes 1966088 | tf_op jit(solution)/shard_map/ppermute | solution.py:252
  495.1 103.8 %collective-permute-start.86 = (bf16[512,1280]{1,0:T(8,128)(2,1)S(1)}, bf16[512,1280]{1,0:T(8,128)(2,1)S(1)}, u32[]{:S(2)}, u32[]{:S(2)}) collective-permute-start(bf16[512,1280]{1,0:T(8,128)(2,1)S(1)} %get-tuple-element.93), channel_id=1, source_target_pairs={{0,8},{8,16},{16,24},{24,0},{1,9},{9,17},{17,25},{25,1},{2,10},{10... | collective-permute-start | bytes 3932168 | tf_op jit(solution)/shard_map/ppermute | solution.py:252
  568.4 59.7 %collective-permute-start.62 = (bf16[4,128,2048]{2,1,0:T(8,128)(2,1)}, bf16[4,128,2048]{2,1,0:T(8,128)(2,1)}, u32[]{:S(2)}, u32[]{:S(2)}) collective-permute-start(bf16[4,128,2048]{2,1,0:T(8,128)(2,1)} %dynamic-slice_bitcast_fusion.1), channel_id=1, source_target_pairs={{0,1},{1,0},{2,3},{3,2},{4,5},{5,4},{6,7},{7,6},{8,9},{9,8},{10,11... | collective-permute-start | bytes 6291464 | tf_op jit(solution)/shard_map/ppermute | solution.py:252
  596.8 90.9 %collective-permute-start.51 = (bf16[4,128,2048]{2,1,0:T(8,128)(2,1)}, bf16[4,128,2048]{2,1,0:T(8,128)(2,1)}, u32[]{:S(2)}, u32[]{:S(2)}) collective-permute-start(bf16[4,128,2048]{2,1,0:T(8,128)(2,1)} %dynamic-slice_bitcast_fusion.2), channel_id=1, source_target_pairs={{0,1},{1,0},{2,3},{3,2},{4,5},{5,4},{6,7},{7,6},{8,9},{9,8},{10,11... | collective-permute-start | bytes 6291464 | tf_op jit(solution)/shard_map/ppermute | solution.py:252
  607.6 19.7 %collective-permute-start.90 = (bf16[128,1280]{1,0:T(8,128)(2,1)S(1)}, bf16[128,1280]{1,0:T(8,128)(2,1)S(1)}, u32[]{:S(2)}, u32[]{:S(2)}) collective-permute-start(bf16[128,1280]{1,0:T(8,128)(2,1)S(1)} %get-tuple-element.123), channel_id=1, source_target_pairs={{0,4},{2,6},{4,0},{6,2},{1,5},{3,7},{5,1},{7,3},{8,12},{10,14},{12... | collective-permute-start | bytes 983048 | tf_op jit(solution)/shard_map/ppermute | solution.py:252
  608.2 32.7 %collective-permute-start.91 = (bf16[128,1280]{1,0:T(8,128)(2,1)S(1)}, bf16[128,1280]{1,0:T(8,128)(2,1)S(1)}, u32[]{:S(2)}, u32[]{:S(2)}) collective-permute-start(bf16[128,1280]{1,0:T(8,128)(2,1)S(1)} %get-tuple-element.122), channel_id=1, source_target_pairs={{0,6},{2,0},{4,2},{6,4},{1,7},{3,1},{5,3},{7,5},{8,14},{10,8},{12,... | collective-permute-start | bytes 983048 | tf_op jit(solution)/shard_map/ppermute | solution.py:252
  632.4 23.4 %collective-permute-start.65 = (bf16[128,2048]{1,0:T(8,128)(2,1)}, bf16[128,2048]{1,0:T(8,128)(2,1)}, u32[]{:S(2)}, u32[]{:S(2)}) collective-permute-start(bf16[128,2048]{1,0:T(8,128)(2,1)} %get-tuple-element.112), channel_id=1, source_target_pairs={{0,6},{2,0},{4,2},{6,4},{1,7},{3,1},{5,3},{7,5},{8,14},{10,8},{12,... | collective-permute-start | bytes 1572872 | tf_op jit(solution)/shard_map/ppermute | solution.py:252
  640.4 44.4 %collective-permute-start.64 = (bf16[128,2048]{1,0:T(8,128)(2,1)S(1)}, bf16[128,2048]{1,0:T(8,128)(2,1)}, u32[]{:S(2)}, u32[]{:S(2)}) collective-permute-start(bf16[128,2048]{1,0:T(8,128)(2,1)S(1)} %get-tuple-element.113), channel_id=1, source_target_pairs={{0,4},{2,6},{4,0},{6,2},{1,5},{3,7},{5,1},{7,3},{8,12},{10,14},{12... | collective-permute-start | bytes 1572872 | tf_op jit(solution)/shard_map/ppermute | solution.py:252
  640.4 44.4 %collective-permute-start.63 = (bf16[128,2048]{1,0:T(8,128)(2,1)S(1)}, bf16[128,2048]{1,0:T(8,128)(2,1)}, u32[]{:S(2)}, u32[]{:S(2)}) collective-permute-start(bf16[128,2048]{1,0:T(8,128)(2,1)S(1)} %get-tuple-element.111), channel_id=1, source_target_pairs={{0,2},{2,4},{4,6},{6,0},{1,3},{3,5},{5,7},{7,1},{8,10},{10,12},{12... | collective-permute-start | bytes 1572872 | tf_op jit(solution)/shard_map/ppermute | solution.py:252
  747.2 20.5 %collective-permute-start.76 = (bf16[512,768]{1,0:T(8,128)(2,1)S(1)}, bf16[512,768]{1,0:T(8,128)(2,1)S(1)}, u32[]{:S(2)}, u32[]{:S(2)}) collective-permute-start(bf16[512,768]{1,0:T(8,128)(2,1)S(1)} %get-tuple-element.102), channel_id=1, source_target_pairs={{0,24},{8,0},{16,8},{24,16},{1,25},{9,1},{17,9},{25,17},{2,26},{10... | collective-permute-start | bytes 2359304 | tf_op jit(solution)/shard_map/ppermute | solution.py:252
  752.1 88.4 %collective-permute-start.82 = (bf16[512,1024]{1,0:T(8,128)(2,1)}, bf16[512,1024]{1,0:T(8,128)(2,1)}, u32[]{:S(2)}, u32[]{:S(2)}) collective-permute-start(bf16[512,1024]{1,0:T(8,128)(2,1)} %get-tuple-element.97), channel_id=1, source_target_pairs={{0,24},{8,0},{16,8},{24,16},{1,25},{9,1},{17,9},{25,17},{2,26},{10... | collective-permute-start | bytes 3145736 | tf_op jit(solution)/shard_map/ppermute | solution.py:252
  753.9 87.5 %collective-permute-start.81 = (bf16[512,1024]{1,0:T(8,128)(2,1)}, bf16[512,1024]{1,0:T(8,128)(2,1)}, u32[]{:S(2)}, u32[]{:S(2)}) collective-permute-start(bf16[512,1024]{1,0:T(8,128)(2,1)} %get-tuple-element.98), channel_id=1, source_target_pairs={{0,16},{8,24},{16,0},{24,8},{1,17},{9,25},{17,1},{25,9},{2,18},{10... | collective-permute-start | bytes 3145736 | tf_op jit(solution)/shard_map/ppermute | solution.py:252
  755.5 88.9 %collective-permute-start.80 = (bf16[512,1024]{1,0:T(8,128)(2,1)}, bf16[512,1024]{1,0:T(8,128)(2,1)}, u32[]{:S(2)}, u32[]{:S(2)}) collective-permute-start(bf16[512,1024]{1,0:T(8,128)(2,1)} %get-tuple-element.96), channel_id=1, source_target_pairs={{0,8},{8,16},{16,24},{24,0},{1,9},{9,17},{17,25},{25,1},{2,10},{10... | collective-permute-start | bytes 3145736 | tf_op jit(solution)/shard_map/ppermute | solution.py:252
  755.5 77.7 %collective-permute-start.75 = (bf16[512,768]{1,0:T(8,128)(2,1)S(1)}, bf16[512,768]{1,0:T(8,128)(2,1)}, u32[]{:S(2)}, u32[]{:S(2)}) collective-permute-start(bf16[512,768]{1,0:T(8,128)(2,1)S(1)} %get-tuple-element.103), channel_id=1, source_target_pairs={{0,16},{8,24},{16,0},{24,8},{1,17},{9,25},{17,1},{25,9},{2,18},{10... | collective-permute-start | bytes 2359304 | tf_op jit(solution)/shard_map/ppermute | solution.py:252
  767.7 69.6 %collective-permute-start.74 = (bf16[512,768]{1,0:T(8,128)(2,1)}, bf16[512,768]{1,0:T(8,128)(2,1)}, u32[]{:S(2)}, u32[]{:S(2)}) collective-permute-start(bf16[512,768]{1,0:T(8,128)(2,1)} %get-tuple-element.101), channel_id=1, source_target_pairs={{0,8},{8,16},{16,24},{24,0},{1,9},{9,17},{17,25},{25,1},{2,10},{10... | collective-permute-start | bytes 2359304 | tf_op jit(solution)/shard_map/ppermute | solution.py:252
  833.2 33.3 %collective-permute-start.70 = (bf16[4,128,2048]{2,1,0:T(8,128)(2,1)}, bf16[4,128,2048]{2,1,0:T(8,128)(2,1)}, u32[]{:S(2)}, u32[]{:S(2)}) collective-permute-start(bf16[4,128,2048]{2,1,0:T(8,128)(2,1)} %dynamic-slice_bitcast_fusion), channel_id=1, source_target_pairs={{0,1},{1,0},{2,3},{3,2},{4,5},{5,4},{6,7},{7,6},{8,9},{9,8},{10,11... | collective-permute-start | bytes 6291464 | tf_op jit(solution)/shard_map/ppermute | solution.py:252
  840.5 19.6 %collective-permute-start.77 = (bf16[128,768]{1,0:T(8,128)(2,1)}, bf16[128,768]{1,0:T(8,128)(2,1)}, u32[]{:S(2)}, u32[]{:S(2)}) collective-permute-start(bf16[128,768]{1,0:T(8,128)(2,1)} %get-tuple-element.133), channel_id=1, source_target_pairs={{0,2},{2,4},{4,6},{6,0},{1,3},{3,5},{5,7},{7,1},{8,10},{10,12},{12... | collective-permute-start | bytes 589832 | tf_op jit(solution)/shard_map/ppermute | solution.py:252
  840.5 22.0 %collective-permute-start.78 = (bf16[128,768]{1,0:T(8,128)(2,1)}, bf16[128,768]{1,0:T(8,128)(2,1)}, u32[]{:S(2)}, u32[]{:S(2)}) collective-permute-start(bf16[128,768]{1,0:T(8,128)(2,1)} %get-tuple-element.132), channel_id=1, source_target_pairs={{0,4},{2,6},{4,0},{6,2},{1,5},{3,7},{5,1},{7,3},{8,12},{10,14},{12... | collective-permute-start | bytes 589832 | tf_op jit(solution)/shard_map/ppermute | solution.py:252
  841.5 24.1 %collective-permute-start.79 = (bf16[128,768]{1,0:T(8,128)(2,1)}, bf16[128,768]{1,0:T(8,128)(2,1)}, u32[]{:S(2)}, u32[]{:S(2)}) collective-permute-start(bf16[128,768]{1,0:T(8,128)(2,1)} %get-tuple-element.131), channel_id=1, source_target_pairs={{0,6},{2,0},{4,2},{6,4},{1,7},{3,1},{5,3},{7,5},{8,14},{10,8},{12,... | collective-permute-start | bytes 589832 | tf_op jit(solution)/shard_map/ppermute | solution.py:252
  856.0 24.6 %collective-permute-start.85 = (bf16[128,1024]{0,1:T(8,128)(2,1)}, bf16[128,1024]{0,1:T(8,128)(2,1)}, u32[]{:S(2)}, u32[]{:S(2)}) collective-permute-start(bf16[128,1024]{0,1:T(8,128)(2,1)} %bitcast.514), channel_id=1, source_target_pairs={{0,6},{2,0},{4,2},{6,4},{1,7},{3,1},{5,3},{7,5},{8,14},{10,8},{12,... | collective-permute-start | bytes 786440 | tf_op jit(solution)/shard_map/ppermute | solution.py:252
  860.1 36.0 %collective-permute-start.84 = (bf16[128,1024]{0,1:T(8,128)(2,1)}, bf16[128,1024]{0,1:T(8,128)(2,1)}, u32[]{:S(2)}, u32[]{:S(2)}) collective-permute-start(bf16[128,1024]{0,1:T(8,128)(2,1)} %bitcast.513), channel_id=1, source_target_pairs={{0,4},{2,6},{4,0},{6,2},{1,5},{3,7},{5,1},{7,3},{8,12},{10,14},{12... | collective-permute-start | bytes 786440 | tf_op jit(solution)/shard_map/ppermute | solution.py:252
  862.5 35.4 %collective-permute-start.83 = (bf16[128,1024]{0,1:T(8,128)(2,1)}, bf16[128,1024]{0,1:T(8,128)(2,1)}, u32[]{:S(2)}, u32[]{:S(2)}) collective-permute-start(bf16[128,1024]{0,1:T(8,128)(2,1)} %bitcast.512), channel_id=1, source_target_pairs={{0,2},{2,4},{4,6},{6,0},{1,3},{3,5},{5,7},{7,1},{8,10},{10,12},{12... | collective-permute-start | bytes 786440 | tf_op jit(solution)/shard_map/ppermute | solution.py:252
  872.7 33.1 %collective-permute-start.73 = (bf16[128,2048]{1,0:T(8,128)(2,1)}, bf16[128,2048]{1,0:T(8,128)(2,1)}, u32[]{:S(2)}, u32[]{:S(2)}) collective-permute-start(bf16[128,2048]{1,0:T(8,128)(2,1)} %get-tuple-element.109), channel_id=1, source_target_pairs={{0,6},{2,0},{4,2},{6,4},{1,7},{3,1},{5,3},{7,5},{8,14},{10,8},{12,... | collective-permute-start | bytes 1572872 | tf_op jit(solution)/shard_map/ppermute | solution.py:252
  880.1 71.9 %collective-permute-start.72 = (bf16[128,2048]{1,0:T(8,128)(2,1)}, bf16[128,2048]{1,0:T(8,128)(2,1)}, u32[]{:S(2)}, u32[]{:S(2)}) collective-permute-start(bf16[128,2048]{1,0:T(8,128)(2,1)} %get-tuple-element.110), channel_id=1, source_target_pairs={{0,4},{2,6},{4,0},{6,2},{1,5},{3,7},{5,1},{7,3},{8,12},{10,14},{12... | collective-permute-start | bytes 1572872 | tf_op jit(solution)/shard_map/ppermute | solution.py:252
  880.6 71.4 %collective-permute-start.71 = (bf16[128,2048]{1,0:T(8,128)(2,1)}, bf16[128,2048]{1,0:T(8,128)(2,1)}, u32[]{:S(2)}, u32[]{:S(2)}) collective-permute-start(bf16[128,2048]{1,0:T(8,128)(2,1)} %get-tuple-element.108), channel_id=1, source_target_pairs={{0,2},{2,4},{4,6},{6,0},{1,3},{3,5},{5,7},{7,1},{8,10},{10,12},{12... | collective-permute-start | bytes 1572872 | tf_op jit(solution)/shard_map/ppermute | solution.py:252
  896.1 58.2 %collective-permute-start.54 = (bf16[128,2048]{1,0:T(8,128)(2,1)}, bf16[128,2048]{1,0:T(8,128)(2,1)S(1)}, u32[]{:S(2)}, u32[]{:S(2)}) collective-permute-start(bf16[128,2048]{1,0:T(8,128)(2,1)} %get-tuple-element.115), channel_id=1, source_target_pairs={{0,6},{2,0},{4,2},{6,4},{1,7},{3,1},{5,3},{7,5},{8,14},{10,8},{12,... | collective-permute-start | bytes 1572872 | tf_op jit(solution)/shard_map/ppermute | solution.py:252
  897.9 76.2 %collective-permute-start.53 = (bf16[128,2048]{1,0:T(8,128)(2,1)}, bf16[128,2048]{1,0:T(8,128)(2,1)S(1)}, u32[]{:S(2)}, u32[]{:S(2)}) collective-permute-start(bf16[128,2048]{1,0:T(8,128)(2,1)} %get-tuple-element.116), channel_id=1, source_target_pairs={{0,4},{2,6},{4,0},{6,2},{1,5},{3,7},{5,1},{7,3},{8,12},{10,14},{12... | collective-permute-start | bytes 1572872 | tf_op jit(solution)/shard_map/ppermute | solution.py:252
  905.8 68.3 %collective-permute-start.52 = (bf16[128,2048]{1,0:T(8,128)(2,1)}, bf16[128,2048]{1,0:T(8,128)(2,1)S(1)}, u32[]{:S(2)}, u32[]{:S(2)}) collective-permute-start(bf16[128,2048]{1,0:T(8,128)(2,1)} %get-tuple-element.114), channel_id=1, source_target_pairs={{0,2},{2,4},{4,6},{6,0},{1,3},{3,5},{5,7},{7,1},{8,10},{10,12},{12... | collective-permute-start | bytes 1572872 | tf_op jit(solution)/shard_map/ppermute | solution.py:252
  (92 other events, 1887.6 us)

commit v2 on v1

--- a/solution.py
+++ b/solution.py
@@ -17,6 +17,8 @@
 f32 = jnp.float32
 
 TQ = 256
+BLOCK = 128
+CORES = 2
 REACH = 128
 SPAN = TQ + 2 * REACH
 WIDE = 1024
@@ -82,12 +84,42 @@
     return diagonals
 
 
+def core_major(block, here, seq_len):
+    core = lax.rem(block % CORES + CORES - here, CORES)
+    return pl.ds(pl.multiple_of((core * (seq_len // BLOCK // CORES) + block // CORES) * BLOCK, BLOCK), BLOCK)
+
+
+def piece_major(block, here):
+    core = lax.rem(block % CORES + CORES - here, CORES)
+    return pl.ds(pl.multiple_of((block // CORES * CORES + core) * BLOCK, BLOCK), BLOCK)
+
+
 def attend_kernel(
-    seq_len, q_ref, k_ref, v_ref, segc_ref, segr_ref, vec_ref, far_ref, mix_ref, lse_ref, strip_ref
+    seq_len,
+    here_ref,
+    q_in,
+    k_in,
+    v_in,
+    segc_ref,
+    segr_ref,
+    vec_ref,
+    far_ref,
+    mix_out,
+    lse_ref,
+    strip_ref,
+    q_ref,
+    k_ref,
+    v_ref,
+    mix_ref,
 ):
     seg_col = segc_ref[...]
     seg_row = segr_ref[...]
     pair = pl.program_id(0)
+    here = here_ref[0]
+    for block in range(seq_len // BLOCK):
+        rows = slice(block * BLOCK, (block + 1) * BLOCK)
+        source = core_major(block, here, seq_len)
+        q_ref[rows], k_ref[rows], v_ref[rows] = q_in[source], k_in[source], v_in[source]
     value_t = v_ref[...].T
     for half in range(2):
         make_strip(strip_ref, vec_ref[0, half : half + 1, :])
@@ -104,32 +136,46 @@
             mixed_t = dot_nn(value_t[lanes, :], expo.astype(bf16)) * (1.0 / total)
             mix_ref[rows, lanes] = mixed_t.T.astype(bf16)
             lse_ref[0, half : half + 1, rows] = top + jnp.log(total)
+    for block in range(seq_len // BLOCK):
+        mix_out[piece_major(block, here)] = mix_ref[block * BLOCK : (block + 1) * BLOCK]
 
 
 def attend_back_kernel(
     seq_len,
-    q_ref,
-    k_ref,
-    v_ref,
-    do_ref,
+    here_ref,
+    q_in,
+    k_in,
+    v_in,
+    do_in,
     segc_ref,
     segr_ref,
     vec_ref,
     far_ref,
     lse_ref,
-    dq_ref,
-    dk_ref,
-    dv_ref,
+    dqkv_out,
     diag_ref,
     farsum_ref,
     strip_ref,
     acc_ref,
     dk_acc,
     dv_acc,
+    q_ref,
+    k_ref,
+    v_ref,
+    do_ref,
+    dq_ref,
+    dk_ref,
+    dv_ref,
 ):
     seg_col = segc_ref[...]
     seg_row = segr_ref[...]
     pair = pl.program_id(0)
+    here = here_ref[0]
+    for block in range(seq_len // BLOCK):
+        rows = slice(block * BLOCK, (block + 1) * BLOCK)
+        source = core_major(block, here, seq_len)
+        q_ref[rows], k_ref[rows], v_ref[rows] = q_in[source], k_in[source], v_in[source]
+        do_ref[rows] = do_in[piece_major(block, here)]
     key_t = k_ref[...].T
     for half in range(2):
         make_strip(strip_ref, vec_ref[0, half : half + 1, :])
@@ -170,6 +216,12 @@
         diag_ref[0, half : half + 1, :] = fold_diagonals(acc_ref)
         farsum_ref[0, half : half + 1, 0:TQ] = far_before
         farsum_ref[0, half : half + 1, TQ : 2 * TQ] = far_after
+    for block in range(seq_len // BLOCK):
+        rows = slice(block * BLOCK, (block + 1) * BLOCK)
+        target = core_major(block, here, seq_len)
+        for at, ref in enumerate((dq_ref, dk_ref, dv_ref)):
+            start = (at * pl.num_programs(0) + pair) * (2 * DH)
+            dqkv_out[target, pl.ds(pl.multiple_of(start, 2 * DH), 2 * DH)] = ref[rows]
 
 
 def kernel_params():
@@ -186,7 +238,7 @@
     return wide, seg_c, seg_r, vec, far, lse
 
 
-def attend(qkv, segs, vectors, far):
+def attend(here, qkv, segs, vectors, far):
     seq_len = qkv.shape[0]
     pairs = vectors.shape[0]
     wide, seg_c, seg_r, vec, far_spec, lse = attention_specs(seq_len, pairs)
@@ -194,42 +246,38 @@
     return pl.pallas_call(
         functools.partial(attend_kernel, seq_len),
         grid=(pairs,),
-        in_specs=[wide(0), wide(1), wide(2), seg_c, seg_r, vec, far_spec],
+        in_specs=[far_spec, wide(0), wide(1), wide(2), seg_c, seg_r, vec, far_spec],
         out_specs=[wide(0), lse],
         out_shape=[
             jax.ShapeDtypeStruct((seq_len, pairs * 2 * DH), bf16),
             jax.ShapeDtypeStruct((pairs, 2, seq_len), f32),
         ],
-        scratch_shapes=[pltpu.VMEM((SPAN, TQ), f32)],
+        scratch_shapes=[pltpu.VMEM((SPAN, TQ), f32)] + [pltpu.VMEM((seq_len, 2 * DH), bf16)] * 4,
         compiler_params=kernel_params(),
         cost_estimate=pl.CostEstimate(
             flops=16 * DH * work, bytes_accessed=8 * seq_len * pairs * DH, transcendentals=work
         ),
         name="attend",
-    )(qkv, qkv, qkv, segs[:, None], segs[None, :], vectors, far)
-
-
-def attend_back(qkv, mixed_grad, segs, vectors, far, lse_rows):
+    )(here, qkv, qkv, qkv, segs[:, None], segs[None, :], vectors, far)
+
+
+def attend_back(here, qkv, mixed_grad, segs, vectors, far, lse_rows):
     seq_len = qkv.shape[0]
     pairs = vectors.shape[0]
     wide, seg_c, seg_r, vec, far_spec, lse = attention_specs(seq_len, pairs)
     work = pairs * 2 * seq_len * seq_len
-    heads_shape = jax.ShapeDtypeStruct((seq_len, pairs * 2 * DH), bf16)
+    dqkv_shape = (seq_len, pairs * 6 * DH)
     return pl.pallas_call(
         functools.partial(attend_back_kernel, seq_len),
         grid=(pairs,),
-        in_specs=[wide(0), wide(1), wide(2), wide(0), seg_c, seg_r, vec, far_spec, lse],
+        in_specs=[far_spec, wide(0), wide(1), wide(2), wide(0), seg_c, seg_r, vec, far_spec, lse],
         out_specs=[
-            wide(0),
-            wide(0),
-            wide(0),
+            pl.BlockSpec(dqkv_shape, lambda p: (0, 0)),
             vec,
             pl.BlockSpec((1, 2, 2 * TQ), lambda p: (p, 0, 0)),
         ],
         out_shape=[
-            heads_shape,
-            heads_shape,
-            heads_shape,
+            jax.ShapeDtypeStruct(dqkv_shape, bf16),
             jax.ShapeDtypeStruct((pairs, 2, WIDE), f32),
             jax.ShapeDtypeStruct((pairs, 2, 2 * TQ), f32),
         ],
@@ -238,13 +286,14 @@
             pltpu.VMEM((SPAN, TQ), f32),
             pltpu.VMEM((seq_len, DH), f32),
             pltpu.VMEM((seq_len, DH), f32),
-        ],
+        ]
+        + [pltpu.VMEM((seq_len, 2 * DH), bf16)] * 7,
         compiler_params=kernel_params(),
         cost_estimate=pl.CostEstimate(
             flops=40 * DH * work, bytes_accessed=16 * seq_len * pairs * DH, transcendentals=work
         ),
         name="attend_back",
-    )(qkv, qkv, qkv, mixed_grad, segs[:, None], segs[None, :], vectors, far, lse_rows)
+    )(here, qkv, qkv, qkv, mixed_grad, segs[:, None], segs[None, :], vectors, far, lse_rows)
 
 
 def shift(value, axis, by):
@@ -260,12 +309,39 @@
     return lax.dynamic_update_slice(stack, block[None], (at,) + (jnp.int32(0),) * block.ndim)
 
 
-def gather_axis(block, axis):
+def arrivals(block, axis):
+    return [shift(block, axis, k) for k in range(1, lax.axis_size(axis))]
+
+
+def assemble(block, arrived, axis):
     size, me = lax.axis_size(axis), lax.axis_index(axis)
     stack = place(jnp.zeros((size,) + block.shape, block.dtype), block, me)
     for k in range(1, size):
-        stack = place(stack, shift(block, axis, k), (me - k) % size)
+        stack = place(stack, arrived[k - 1], (me - k) % size)
     return stack
+
+
+def gather_axis(block, axis):
+    return assemble(block, arrivals(block, axis), axis)
+
+
+def flip(value, mask):
+    size = lax.axis_size("dp")
+    return lax.ppermute(value, "dp", [(i, i ^ mask) for i in range(size)])
+
+
+def gather_rows(block):
+    if lax.axis_size("dp") != 4:
+        return flat(gather_axis(block, "dp"))
+    me, half = lax.axis_index("dp"), block.shape[0] // 2
+    near, other = flip(block, 1), flip(block, 2)
+    first, second = flip(near[:half], 2), flip(other[half:], 1)
+    stack = place(jnp.zeros((4,) + block.shape, block.dtype), block, me)
+    stack = place(place(stack, near, me ^ 1), other, me ^ 2)
+    zero = jnp.int32(0)
+    stack = lax.dynamic_update_slice(stack, first[None], (me ^ 3, zero, zero))
+    stack = lax.dynamic_update_slice(stack, second[None], (me ^ 3, jnp.int32(half), zero))
+    return flat(stack)
 
 
 def exchange_axis(block_of, axis):
@@ -286,55 +362,110 @@
     return total
 
 
-def gather_tokens(rows):
-    parts, pieces = lax.axis_size("tensor"), lax.axis_size("ctx")
-    t, z = lax.axis_index("tensor"), lax.axis_index("ctx")
-    stack = jnp.zeros((pieces * parts,) + rows.shape, rows.dtype)
-    for k in range(pieces):
-        block = shift(rows, "ctx", k) if k else rows
-        at = (z - k) % pieces
-        stack = place(stack, block, at * parts + t)
-        for j in range(1, parts):
-            stack = place(stack, shift(block, "tensor", j), at * parts + (t - j) % parts)
-    return stack.reshape(-1, rows.shape[1])
-
-
-def scatter_tokens(partial):
-    parts, pieces = lax.axis_size("tensor"), lax.axis_size("ctx")
-    stack = partial.reshape(pieces, parts, -1, partial.shape[1])
-    pieces_sum = scatter_sum_axis(
-        lambda j: lax.dynamic_index_in_dim(stack, j, 1, keepdims=False), "tensor"
-    )
-    return scatter_sum_axis(lambda j: block_at(pieces_sum, j), "ctx")
-
-
-def gather_weight(weights):
+def tie(value, *others):
+    return lax.optimization_barrier((value,) + others)[0]
+
+
+def swap(block):
+    return shift(block, "tensor", 1)
+
+
+def exchange(stack, axis):
+    return lax.all_to_all(stack, axis, 0, 0)
+
+
+def gather_bcast(rows, axis):
+    return exchange(jnp.broadcast_to(rows[None], (lax.axis_size(axis),) + rows.shape), axis)
+
+
+def gather_tokens(rows, axis):
+    return both_cores(gather_bcast(rows, axis))
+
+
+def both_cores(stack):
+    return jnp.concatenate([stack, swap(stack)], axis=0).reshape(-1, stack.shape[-1])
+
+
+def sum_of_cores(partial, axis):
+    stack = partial.reshape(CORES, lax.axis_size(axis), -1, partial.shape[-1])
+    return (stack[0].astype(f32) + swap(stack[1].astype(bf16)).astype(f32)).astype(bf16)
+
+
+def sum_of_axis(stack, axis):
+    return jnp.sum(exchange(stack, axis).astype(f32), axis=0)
+
+
+def columns_in(matrix, order):
+    wide = matrix.shape[1] // len(order)
+    return jnp.concatenate([matrix[:, j * wide : (j + 1) * wide] for j in order], axis=1)
+
+
+def by_piece(matrix):
+    dps, pieces = lax.axis_size("dp"), lax.axis_size("ctx")
+    return columns_in(matrix, [j * pieces + i for i in range(pieces) for j in range(dps)])
+
+
+def by_dp(matrix):
+    dps, pieces = lax.axis_size("dp"), lax.axis_size("ctx")
+    return columns_in(matrix, [i * dps + j for j in range(dps) for i in range(pieces)])
+
+
+def piece_columns(weights):
     pieces = lax.axis_size("ctx")
-
-    def block_of(j):
-        columns = [
-            lax.dynamic_slice_in_dim(w, j * (w.shape[1] // pieces), w.shape[1] // pieces, 1)
-            for w in weights
-        ]
-        return jnp.concatenate(columns, axis=1) if len(columns) > 1 else columns[0]
-
-    stack = exchange_axis(block_of, "ctx")
-    stack = stack.reshape(-1, stack.shape[-1])
-    return gather_axis(stack, "dp").reshape(-1, stack.shape[-1])
-
-
-def scatter_weight(grad, widths):
-    dps, pieces = lax.axis_size("dp"), lax.axis_size("ctx")
-    stack = grad.reshape(dps, -1, grad.shape[1])
-    mine = scatter_sum_axis(lambda j: block_at(stack, j), "dp")
-    mine = mine.reshape(pieces, -1, grad.shape[1])
-    back = exchange_axis(lambda j: block_at(mine, j).astype(bf16), "ctx")
+    split = [jnp.transpose(w.reshape(w.shape[0], pieces, -1), (1, 0, 2)) for w in weights]
+    return jnp.concatenate(split, axis=2)
+
+
+def own_rows(stack, widths):
     outs, at = [], 0
     for width in widths:
-        part = back[:, :, at : at + width].astype(f32)
+        part = stack[:, :, at : at + width].astype(f32)
         outs.append(jnp.transpose(part, (1, 0, 2)).reshape(part.shape[1], -1))
         at += width
     return outs
+
+
+def send_weight(left, right):
+    size, me = lax.axis_size("dp"), lax.axis_index("dp")
+    wide = left.shape[1] // size
+
+    def block_of(j):
+        return mm_tn(lax.dynamic_slice_in_dim(left, j * wide, wide, 1), right)
+
+    arrived = [shift(block_of((me + k) % size).astype(bf16), "dp", k) for k in range(1, size)]
+    return block_of(me), arrived
+
+
+def sum_weight(own, arrived):
+    for block in arrived:
+        own = own + block.astype(f32)
+    return own.astype(bf16).reshape(lax.axis_size("ctx"), -1, own.shape[1])
+
+
+def reduce_weight(left, right):
+    if lax.axis_size("dp") != 4:
+        own, arrived = send_weight(left, right)
+        return sum_weight(own, arrived), arrived
+    me, wide, half = lax.axis_index("dp"), left.shape[1] // 4, right.shape[1] // 2
+
+    def block_of(j):
+        return mm_tn(lax.dynamic_slice_in_dim(left, j * wide, wide, 1), right)
+
+    far = block_of(me ^ 3).astype(bf16)
+    near = block_of(me ^ 1).astype(bf16)
+    other = block_of(me ^ 2).astype(bf16)
+    from_near = flip(jnp.stack([near[:, :half], far[:, :half]]), 1)
+    from_other = flip(jnp.stack([other[:, half:], far[:, half:]]), 2)
+    own = block_of(me)
+    low = flip((other[:, :half].astype(f32) + from_near[1].astype(f32)).astype(bf16), 2)
+    high = flip((near[:, half:].astype(f32) + from_other[1].astype(f32)).astype(bf16), 1)
+    low = own[:, :half] + from_near[0].astype(f32) + low.astype(f32)
+    high = own[:, half:] + from_other[0].astype(f32) + high.astype(f32)
+    return sum_weight(jnp.concatenate([low, high], axis=1), []), [from_near, from_other]
+
+
+def flat(stack):
+    return stack.reshape(-1, stack.shape[-1])
 
 
 def root_mean_square_backward(grad, normalized, scale, gain):
@@ -381,32 +512,57 @@
     heads = part_heads // pieces
     head_cols = heads * DH
 
-    x_seq = gather_tokens(layer_input)
-    gains = gather_axis(gather_axis(jnp.stack([attn_gain, ff_gain]), "ctx"), "dp")
+
+    here = jnp.reshape(t, (1,)).astype(jnp.int32)
+
+    small_in = jnp.concatenate([attn_gain, ff_gain, segments.astype(bf16)]).reshape(1, -1)
+    small_pieces = gather_axis(small_in, "ctx").reshape(pieces, -1)
+    gain_cols = attn_gain.shape[0]
+    segs = small_pieces[:, 2 * gain_cols :].astype(jnp.int32).reshape(seq_len)
+    gains = gather_axis(small_pieces[:, : 2 * gain_cols], "dp").reshape(dps, pieces, 2, gain_cols)
     gains = jnp.transpose(gains, (2, 0, 1, 3)).reshape(2, width).astype(f32)
     gain_one, gain_two = gains[0:1], gains[1:2]
-    w_qkv = gather_weight([query_weight, key_weight, value_weight])
-    output_t = gather_axis(output_weight.T, "ctx")
-    w_out = gather_axis(output_t, "dp").reshape(width, -1)
-    w_gu = gather_weight([gate_weight, up_weight])
-    w_down = gather_weight([down_weight.T])
-    dy_seq = gather_tokens(cotangent)
-    segs = gather_axis(segments, "ctx").reshape(seq_len)
+    attn_blocks = piece_columns([query_weight, key_weight, value_weight])
+    out_block = jnp.broadcast_to(output_weight.T[None], (pieces, output_weight.shape[1], part_heads * DH))
+    attn_blocks = jnp.concatenate([attn_blocks, out_block], axis=2)
+    attn_pieces = flat(exchange(tie(attn_blocks, small_pieces), "ctx"))
+
+    units = down_weight.shape[0] // dps
+    ff_weights = (gate_weight, up_weight, down_weight.T)
+    ff_weights = lax.optimization_barrier(ff_weights + (small_pieces,))[:3]
+
+    def ff_block(j):
+        columns = [lax.dynamic_slice_in_dim(w, j * units, units, 1) for w in ff_weights]
+        return jnp.concatenate(columns, axis=1)
+
+    ff_arrived = [shift(ff_block((s + k) % dps), "dp", k) for k in range(1, dps)]
+    x_copies = jnp.broadcast_to(layer_input[None], (pieces,) + layer_input.shape)
+    x_core = exchange(tie(x_copies, attn_pieces, gains, *ff_arrived), "ctx")
+    ff_rows = assemble(ff_block(s), ff_arrived, "dp")
+    w_ff = lax.all_gather(flat(ff_rows), "ctx", axis=0, tiled=True)
+    w_gu, w_down = w_ff[:, : 2 * units], w_ff[:, 2 * units :]
+
+    w_qkv = gather_rows(attn_pieces[:, : 3 * head_cols])
+    w_out = gather_rows(tie(attn_pieces, w_qkv)[:, 3 * head_cols :])
+    x_seq = both_cores(tie(x_core, w_out))
 
     own_table = lax.dynamic_slice_in_dim(bias_table, z * heads, heads, 1)
     lanes_onehot = lane_buckets()
     vectors = jnp.dot(lanes_onehot, own_table, precision=highest).T.reshape(heads // 2, 2, WIDE)
     far = jnp.stack([own_table[NB // 2 - 1], own_table[NB - 1]], axis=1)
 
-    x_wide = x_seq.astype(f32)
+    x_wide = tie(x_seq, w_qkv).astype(f32)
     normed_seq = (x_wide * inverse_scale(x_wide) * gain_one).astype(bf16)
     qkv = mm(normed_seq, w_qkv).astype(bf16)
-    mixed_heads, lse_rows = attend(qkv, segs, vectors, far)
-    mixed_stack = mixed_heads.reshape(pieces, -1, head_cols)
-    mixed = exchange_axis(lambda j: block_at(mixed_stack, j), "ctx")
+    dy_arrived = arrivals(tie(by_piece(cotangent), qkv), "dp")
+    mixed_heads, lse_rows = attend(here, qkv, segs, vectors, far)
+    mixed = exchange(
+        tie(mixed_heads, *dy_arrived).reshape(pieces, parts * rows, head_cols), "ctx"
+    )
+    dy_all = both_cores(assemble(by_piece(cotangent), dy_arrived, "dp"))
     mixed = jnp.transpose(mixed, (1, 0, 2)).reshape(rows * parts, -1)
-    attn_part = mm_nt(mixed, w_out).reshape(parts, rows, width)
-    attn_own = scatter_sum_axis(lambda j: block_at(attn_part, j), "tensor")
+    attn_part = mm_nt(mixed, w_out)
+    attn_own = attn_part[:rows] + swap(attn_part[rows:].astype(bf16)).astype(f32)
 
     x_own = layer_input.astype(f32)
     scale_one = inverse_scale(x_own)
@@ -416,45 +572,62 @@
     unit_two = hidden * scale_two
     normed_two = (unit_two * gain_two).astype(bf16)
 
-    normed_two_seq = gather_tokens(normed_two)
-    units = w_down.shape[1]
-    gate_up = mm(normed_two_seq, w_gu)
+    normed_two_all = gather_tokens(tie(by_piece(normed_two), dy_all), "dp")
+    gate_up = mm(normed_two_all, w_gu)
+    inner_grad = mm(dy_all, w_down)
     gate, upper = gate_up[:, :units], gate_up[:, units:]
-    inner_grad = mm(dy_seq, w_down)
     inner, gelu_pull = jax.vjp(lambda g, u: jax.nn.gelu(g, approximate=True) * u, gate, upper)
     inner = inner.astype(bf16)
     gate_grad, upper_grad = gelu_pull(inner_grad)
     gate_up_grad = jnp.concatenate([gate_grad.astype(bf16), upper_grad.astype(bf16)], axis=1)
     normed_two_part = mm_nt(gate_up_grad, w_gu).astype(bf16)
-    normed_two_grad = scatter_tokens(normed_two_part)
-    ff_part = mm_nt(inner, w_down).astype(bf16)
-    ff_own = scatter_tokens(ff_part)
-    block_output = (hidden + ff_own).astype(bf16)
-    gate_out, up_out = scatter_weight(mm_tn(normed_two_seq, gate_up_grad), (units, units))
-    (down_out,) = scatter_weight(mm_tn(dy_seq, inner), (units,))
+    normed_two_core = sum_of_cores(normed_two_part, "dp")
+    normed_two_sum = sum_of_axis(normed_two_core, "dp")
+    gate_up_late, inner_late = lax.optimization_barrier(
+        (gate_up_grad, inner, normed_two_core)
+    )[:2]
+    ff_wgrad = jnp.concatenate(
+        [mm_tn(normed_two_all, gate_up_late).astype(bf16), mm_tn(dy_all, inner_late).astype(bf16)],
+        axis=1,
+    )
+    ff_sum = lax.psum_scatter(ff_wgrad, "ctx", scatter_dimension=0, tiled=True)
+    normed_two_sum = tie(normed_two_sum, ff_wgrad)
+    normed_two_sum = by_dp(normed_two_sum)
+    normed_two_grad = normed_two_sum
 
     ff_gain_share = jnp.sum(normed_two_grad * unit_two, axis=0)
     hidden_grad = cotangent.astype(f32) + root_mean_square_backward(
         normed_two_grad, unit_two, scale_two, gain_two
     )
-    attn_step = gather_axis(hidden_grad.astype(bf16), "tensor").reshape(rows * parts, width)
+    attn_step = hidden_grad.astype(bf16)
+    attn_step = jnp.concatenate([attn_step, swap(attn_step)], axis=0)
     mixed_grad = mm(attn_step, w_out).astype(bf16).reshape(rows * parts, pieces, head_cols)
-    mixed_grad = exchange_axis(
-        lambda j: lax.dynamic_index_in_dim(mixed_grad, j, 1, keepdims=False), "ctx"
-    ).reshape(seq_len, head_cols)
-    output_wgrad = mm_tn(attn_step, mixed)
-    output_stack = output_wgrad.reshape(dps, -1, output_wgrad.shape[1])
-    output_sum = scatter_sum_axis(lambda j: block_at(output_stack, j), "dp")
-    output_sum = output_sum.reshape(pieces, -1, output_wgrad.shape[1])
-    output_out = scatter_sum_axis(lambda j: block_at(output_sum, j), "ctx").T
-
-    dq, dk, dv, diagonals, far_sums = attend_back(qkv, mixed_grad, segs, vectors, far, lse_rows)
-    dqkv = jnp.concatenate([dq, dk, dv], axis=1)
+    mixed_grad = flat(exchange(jnp.transpose(mixed_grad, (1, 0, 2)), "ctx"))
+    output_sum, output_arrived = reduce_weight(attn_step, mixed)
+    ff_part = mm_nt(tie(inner_late, attn_step), w_down).astype(bf16)
+    ff_core = sum_of_cores(ff_part, "dp")
+    ff_stack = exchange(tie(ff_core, mixed_grad), "dp")
+
+    mixed_grad = tie(mixed_grad, *output_arrived)
+    dqkv, diagonals, far_sums = attend_back(
+        here, qkv, mixed_grad, segs, vectors, far, lse_rows
+    )
+    dqkv = tie(dqkv, ff_stack, output_sum)
     normed_one_part = mm_nt(dqkv, w_qkv).astype(bf16)
-    normed_one_grad = scatter_tokens(normed_one_part)
-    query_out, key_out, value_out = scatter_weight(
-        mm_tn(normed_seq, dqkv), (head_cols, head_cols, head_cols)
-    )
+    normed_one_core = sum_of_cores(normed_one_part, "ctx")
+    normed_one_sum = sum_of_axis(normed_one_core, "ctx")
+    ff_own = by_dp(jnp.sum(tie(ff_stack, normed_one_core).astype(f32), axis=0))
+    block_output = (hidden + ff_own).astype(bf16)
+    qkv_sum, _ = reduce_weight(normed_seq, tie(dqkv, normed_one_core))
+    ff_blocks = tie(ff_sum, qkv_sum).reshape(dps, -1, 3 * units)
+    ff_back = exchange_axis(lambda j: block_at(ff_blocks, j), "dp")
+    gate_out, up_out, down_out = own_rows(ff_back, (units,) * 3)
+    normed_one_grad = tie(normed_one_sum, block_output, ff_back)
+    sums = jnp.concatenate([output_sum, qkv_sum], axis=2)
+    back = exchange(tie(sums, normed_one_sum), "ctx")
+    at = output_sum.shape[2]
+    output_out = jnp.sum(back[:, :, :at].astype(f32), axis=0).T
+    query_out, key_out, value_out = own_rows(back[:, :, at:], (head_cols,) * 3)
     attn_gain_share = jnp.sum(normed_one_grad * unit_one, axis=0)
     input_grads = (
         hidden_grad + root_mean_square_backward(normed_one_grad, unit_one, scale_one, gain_one)
@@ -479,9 +652,15 @@
             jnp.sum(valid),
         ]
     )
-    gain_one_total, gain_two_total, bias_total, sums_total = lax.psum(
-        (attn_gain_share, ff_gain_share, bias_full, local_sums), ("dp", "ctx", "tensor")
-    )
+    small = jnp.concatenate(
+        [attn_gain_share, ff_gain_share, bias_full.reshape(-1), jnp.pad(local_sums, (0, BLOCK - 3))]
+    ).reshape(-1, BLOCK)
+    for axis in ("tensor", "dp", "ctx"):
+        small = jnp.sum(gather_axis(small, axis), axis=0)
+    small = small.reshape(-1)
+    gain_one_total, gain_two_total = small[:width], small[width : 2 * width]
+    bias_total = small[2 * width : 2 * width + bias_full.size].reshape(bias_full.shape)
+    sums_total = small[2 * width + bias_full.size :]
     rms_stats = jnp.sqrt(sums_total[:2] / (sums_total[2] * width))
     return (
         block_output,

time: 1030 us -> 641 us (0.62)
  waiting for transfers between devices: 430 us -> 229 us
  starting transfers between devices: 214 us -> 89.6 us
  local copies, waits for them, and re-layouts: 175 us -> 85.5 us
  other arithmetic: 58 us -> 72.7 us
  between operations: 2.74 us -> 16.6 us
    ppermute x98 -> x30, waiting for transfers between devices: 430 us -> 34.4 us  [shift(): lax.ppermute(value, axis, [(i, (i + by) % size) for i in range(size)])]
    ppermute x98 -> x30, starting transfers between devices: 214 us -> 34.6 us  [shift(): lax.ppermute(value, axis, [(i, (i + by) % size) for i in range(size)])]
    all_to_all x0 -> x8, waiting for transfers between devices: none -> 117 us  [exchange(): return lax.all_to_all(stack, axis, 0, 0)]
    ppermute x0 -> x16, waiting for transfers between devices: none -> 48.4 us  [flip(): return lax.ppermute(value, 'dp', [(i, i ^ mask) for i in range(size)])]
    psum x1 -> x0, blocking collectives: 37.8 us -> none  [shards(): lax.psum((attn_gain_share, ff_gain_share, bias_full, local_sums), ('dp',...]
    all_to_all x0 -> x8, starting transfers between devices: none -> 35.7 us  [exchange(): return lax.all_to_all(stack, axis, 0, 0)]
    all_to_all x0 -> x1, blocking collectives: none -> 29.4 us  [exchange(): return lax.all_to_all(stack, axis, 0, 0)]
    dynamic_update_slice x81 -> x34, local copies, waits for them, and re-layouts: 51.6 us -> 22.3 us  [place(): lax.dynamic_update_slice(stack, block[None], (at,) + (jnp.int32(0),) * bl...]
  transfers between devices with their start and end apart: 98 -> 56, of which waited for: 35 -> 25; matrix products, arithmetic and copies ran while one was open for 22% -> 31% of each run, Pallas kernels for 1% -> 5%
where the time goes in v2:
time: 641 us; the launch traced here: 631 us
  waiting for transfers between devices  229 us (36%)
  starting transfers between devices  89.6 us (14%)
  local copies, waits for them, and re-layouts  85.5 us (13%)
  matrix products  75.1 us (12%)
  other arithmetic  72.7 us (11%)
  Pallas kernels  32.7 us (5%)
  blocking collectives  29.4 us (5%)
  between operations  16.6 us (3%)
    all_to_all x8, waiting for transfers between devices, exchange(): return lax.all_to_all(stack, axis, 0, 0)  117 us
    ppermute x16, waiting for transfers between devices, flip(): return lax.ppermute(value, 'dp', [(i, i ^ mask) for i in range(size)])  48.4 us
    all_to_all x8, starting transfers between devices, exchange(): return lax.all_to_all(stack, axis, 0, 0)  35.7 us
    ppermute x30, starting transfers between devices, shift(): lax.ppermute(value, axis, [(i, (i + by) % size) for i in range(size)])  34.6 us
    ppermute x30, waiting for transfers between devices, shift(): lax.ppermute(value, axis, [(i, (i + by) % size) for i in range(size)])  34.4 us
    all_to_all x1, blocking collectives, exchange(): return lax.all_to_all(stack, axis, 0, 0)  29.4 us
    all_gather x1, waiting for transfers between devices, shards(): w_ff = lax.all_gather(flat(ff_rows), 'ctx', axis=0, tiled=True)  28.9 us
    dot_general x4, matrix products, mm(): return jnp.dot(a, b, preferred_element_type=f32)  26.9 us
  transfers between devices with their start and end apart: 56, of which 25 were waited for; matrix products, arithmetic and copies ran while one was open for 31% of the time, Pallas kernels for 5%

profile of v2, /device:TPU:0, one launch (start us, length us, event | category | flops | bytes accessed | tf_op | source)
XLA Modules:
  0.0 630.8 jit_solution(3808595301088349932)
XLA Ops:
  8.7 3.1 collective-permute-start
  11.7 2.6 collective-permute-start.1
  22.2 3.6 all-to-all-start
  36.9 30.9 %all-to-all-done = bf16[4,128,1792]{2,1,0:T(8,128)(2,1)S(1)} async-done(((bf16[4,128,1792]{2,1,0:T(8,128)(2,1)}), bf16[4,128,1792]{2,1,0:T(8,128)(2,1)S(1)}, u32[]{:S(2)}, u32[]{:S(2)}) %all-to-all-start) | async-done | bytes 1835040 | tf_op jit(solution)/shard_map/all_to_all | solution.py:374
  75.1 4.5 all-to-all-start.1
  82.5 5.0 collective-permute-done.6
  105.1 2.4 collective-permute-start.17
  109.8 13.5 %collective-permute-done.15 = bf16[4,256]{1,0:T(4,128)(2,1)S(1)} collective-permute-done((bf16[4,256]{1,0:T(4,128)(2,1)S(1)}, bf16[4,256]{1,0:T(4,128)(2,1)S(1)}, u32[]{:S(2)}, u32[]{:S(2)}) %collective-permute-start.15) | collective-permute-done | bytes 2080 | tf_op jit(solution)/shard_map/ppermute | solution.py:301
  123.3 2.5 broadcast_in_dim.192
  131.2 5.7 collective-permute-done.12
  148.7 8.2 %convolution_convert_fusion.4.q_in.k_in.v_in = bf16[1024,768]{1,0:T(8,128)(2,1)} fusion(bf16[1024,2048]{1,0:T(8,128)(2,1)S(1)} %fusion.2, bf16[2048,768]{1,0:T(8,128)(2,1)} %bitcast.12), kind=kOutput, calls=%fused_computation.46 | convolution fusion | flops 3222011904 | bytes 8912896 | tf_op jit(solution)/shard_map/dot_general | solution.py:477
  158.9 2.5 collective-permute-start.20
  163.8 15.2 %attend.1 = (bf16[1024,256]{1,0:T(8,128)(2,1)}, f32[2,2,1024]{2,1,0:T(2,128)}) custom-call(s32[1]{0:T(128)} %bitcast.here_ref, bf16[1024,768]{1,0:T(8,128)(2,1)} %convolution_convert_fusion.4.q_in.k_in.v_in, bf16[1024,768]{1,0:T(8,128)(2,1)} %convolution_convert_fusion.4.q_in.k_in.v_in, bf16[1024,768]{1,0:T(8,128)(2,1)} %convolution_convert_fusion.4.q_in.k_in.v_in, ...), custom_call_target="tpu_custom_call" | custom-call | flops 4294967296 | bytes 1048576 | tf_op jit(solution)/shard_map/attend/pallas_call | solution.py:246
  179.0 4.4 collective-permute-done.19
  185.4 3.5 all-to-all-start.2
  192.2 23.4 %all-to-all-done.2 = bf16[4,256,256]{1,2,0:T(8,128)(2,1)S(1)} async-done(((bf16[4,256,256]{1,2,0:T(8,128)(2,1)}), bf16[4,256,256]{1,2,0:T(8,128)(2,1)S(1)}, u32[]{:S(2)}, u32[]{:S(2)}) %all-to-all-start.2) | async-done | bytes 524320 | tf_op jit(solution)/shard_map/all_to_all | solution.py:374
  215.6 3.6 fusion.97
  222.4 3.1 collective-permute-done.22
  225.5 3.9 pad_maximum_fusion.2
  229.7 29.4 %all_to_all.45 = bf16[4,128,2048]{2,1,0:T(8,128)(2,1)S(1)} all-to-all(bf16[4,128,2048]{2,1,0:T(8,128)(2,1)S(1)} %broadcast_in_dim.218), channel_id=1, replica_groups=mesh['dp'=4,'ctx'=4,'tensor'=2] {'dp'}, dimensions={0} | all-to-all | bytes 4194304 | tf_op jit(solution)/shard_map/all_to_all | solution.py:374
  259.1 4.2 collective-permute-done.23
  263.3 2.4 pad_maximum_fusion.3
  265.7 28.9 %all-gather.2.cloned.1.call-done = bf16[2048,1920]{1,0:T(8,128)(2,1)} async-done(((bf16[512,1920]{1,0:T(8,128)(2,1)}), bf16[2048,1920]{1,0:T(8,128)(2,1)}) %all-gather.2.cloned.1.call-update) | async-done | bytes 7864336 | tf_op jit(solution)/shard_map/all_gather | solution.py:542
  294.6 9.2 %fusion.5 = f32[1024,1280]{0,1:T(8,128)S(1)} fusion(bf16[1024,2048]{1,0:T(8,128)(2,1)} %bitcast.255, bf16[2048,1920]{1,0:T(8,128)(2,1)} %all-gather.2.cloned.1.call-done), kind=kOutput, calls=%fused_computation.9 | convolution fusion | flops 5368709120 | bytes 14680064 | tf_op jit(solution)/shard_map/dot_general | solution.py:477
  303.8 5.8 fusion.19
  309.6 5.9 fusion.10
  315.5 2.4 fusion.95
  318.0 3.6 pad_maximum_fusion.4
  322.5 3.8 fusion.9
  326.3 4.5 all-to-all-start.4
  331.1 10.0 %convolution_convert_fusion = bf16[2048,1280]{0,1:T(8,128)(2,1)} fusion(bf16[1024,1280]{0,1:T(8,128)(2,1)} %pad_maximum_fusion.4, bf16[1024,2048]{1,0:T(8,128)(2,1)} %bitcast.256), kind=kOutput, calls=%fused_computation.6 | convolution fusion | flops 5371330560 | bytes 12058624 | tf_op jit(solution)/shard_map/dot_general | solution.py:485
  341.1 4.2 convolution_convert_fusion.3
  345.3 7.9 %pad_maximum_fusion = bf16[2048,1920]{0,1:T(8,128)(2,1)} fusion(bf16[2048,640]{0,1:T(8,128)(2,1)} %convolution_convert_fusion.3, bf16[2048,1280]{0,1:T(8,128)(2,1)} %convolution_convert_fusion), kind=kLoop, calls=%fused_computation.5 | loop fusion | flops 15728640 | bytes 15728640 | tf_op jit(solution)/shard_map/concatenate | solution.py:589
  353.2 7.5 %convolution_convert_fusion.1 = bf16[1024,2048]{1,0:T(8,128)(2,1)} fusion(bf16[1024,640]{0,1:T(8,128)(2,1)} %get-tuple-element.55, bf16[2048,1920]{1,0:T(8,128)(2,1)} %all-gather.2.cloned.1.call-done), kind=kOutput, calls=%fused_computation.24 | convolution fusion | flops 2686451712 | bytes 8126464 | tf_op jit(solution)/shard_map/dot_general | solution.py:44
  365.4 2.5 fusion.94
  368.1 3.7 convolution_convert_fusion.11
  372.6 4.1 all-to-all-start.5
  386.1 3.8 fusion.8
  389.9 18.7 %all-to-all-done.5 = bf16[4,256,256]{2,1,0:T(8,128)(2,1)} async-done(((bf16[4,256,256]{2,1,0:T(8,128)(2,1)}), bf16[4,256,256]{2,1,0:T(8,128)(2,1)}, u32[]{:S(2)}, u32[]{:S(2)}) %all-to-all-start.5) | async-done | bytes 524320 | tf_op jit(solution)/shard_map/all_to_all | solution.py:374
  408.6 4.9 all-to-all-start.6
  413.5 17.5 %attend_back.1 = (bf16[1024,768]{1,0:T(8,128)(2,1)}, f32[2,2,1024]{2,1,0:T(2,128)}, f32[2,2,512]{2,1,0:T(2,128)}) custom-call(s32[1]{0:T(128)} %bitcast.here_ref, bf16[1024,768]{1,0:T(8,128)(2,1)} %convolution_convert_fusion.4.q_in.k_in.v_in, bf16[1024,768]{1,0:T(8,128)(2,1)} %convolution_convert_fusion.4.q_in.k_in.v_in, ...), custom_call_target="tpu_custom_call" | custom-call | flops 10737418240 | bytes 2097152 | tf_op jit(solution)/shard_map/attend_back/pallas_call | solution.py:270
  431.1 7.6 %all-to-all-done.6 = bf16[4,128,2048]{2,1,0:T(8,128)(2,1)} async-done(((bf16[4,128,2048]{2,1,0:T(8,128)(2,1)}), bf16[4,128,2048]{2,1,0:T(8,128)(2,1)}, u32[]{:S(2)}, u32[]{:S(2)}) %all-to-all-start.6) | async-done | bytes 2097184 | tf_op jit(solution)/shard_map/all_to_all | solution.py:374
  438.7 5.8 convolution_convert_fusion.2
  444.5 2.2 fusion.93
  446.7 2.2 fusion.39
  450.4 2.1 fusion.38
  456.1 7.5 %collective-permute-done.40 = bf16[512,512]{1,0:T(8,128)(2,1)} collective-permute-done((bf16[512,512]{1,0:T(8,128)(2,1)}, bf16[512,512]{1,0:T(8,128)(2,1)}, u32[]{:S(2)}, u32[]{:S(2)}) %collective-permute-start.40) | collective-permute-done | bytes 524320 | tf_op jit(solution)/shard_map/ppermute | solution.py:330
  463.6 3.3 collective-permute-done.41
  466.9 2.6 fusion.37
  469.5 3.8 fusion.7
  473.3 6.2 all-to-all-start.7
  479.5 2.9 convolution_convert_fusion.10
  488.5 14.3 %collective-permute-done.42 = bf16[2,512,384]{2,1,0:T(8,128)(2,1)S(1)} collective-permute-done((bf16[2,512,384]{2,1,0:T(8,128)(2,1)S(1)}, bf16[2,512,384]{2,1,0:T(8,128)(2,1)S(1)}, u32[]{:S(2)}, u32[]{:S(2)}) %collective-permute-start.42) | collective-permute-done | bytes 786464 | tf_op jit(solution)/shard_map/ppermute | solution.py:330
  503.8 4.8 collective-permute-done.44
  511.7 3.5 collective-permute-done.43
  518.2 4.0 copy.186
  527.6 16.0 %all-to-all-done.7 = bf16[4,128,2048]{2,1,0:T(8,128)(2,1)} async-done(((bf16[4,128,2048]{2,1,0:T(8,128)(2,1)}), bf16[4,128,2048]{2,1,0:T(8,128)(2,1)}, u32[]{:S(2)}, u32[]{:S(2)}) %all-to-all-start.7) | async-done | bytes 2097184 | tf_op jit(solution)/shard_map/all_to_all | solution.py:374
  543.6 2.1 convert_reduce_fusion
  545.7 4.4 all-to-all-start.8
  551.7 2.2 multiply_reduce_fusion.1
  557.2 5.9 collective-permute-done.31
  563.9 2.5 collective-permute-done.32
  571.9 20.8 %all-to-all-done.8 = bf16[4,128,1792]{2,1,0:T(8,128)(2,1)} async-done(((bf16[4,128,1792]{2,1,0:T(8,128)(2,1)}), bf16[4,128,1792]{2,1,0:T(8,128)(2,1)}, u32[]{:S(2)}, u32[]{:S(2)}) %all-to-all-start.8) | async-done | bytes 1835040 | tf_op jit(solution)/shard_map/all_to_all | solution.py:374
  608.8 3.3 convert_bitcast_fusion
  (394 shorter events, 157.6 us)
Async XLA Ops:
  7.2 13.0 %copy-start = (f32[32,16]{0,1:T(8,128)S(1)}, f32[32,16]{0,1:T(8,128)}, u32[]{:S(2)}) copy-start(f32[32,16]{0,1:T(8,128)} %param.20) | copy-start | bytes 6148
  7.2 12.8 %copy-start.11 = (bf16[128,2048]{1,0:T(8,128)(2,1)S(1)}, bf16[128,2048]{1,0:T(8,128)(2,1)}, u32[]{:S(2)}) copy-start(bf16[128,2048]{1,0:T(8,128)(2,1)} %param.25) | copy-start | bytes 1572868
  8.7 13.4 %collective-permute-start = (bf16[1,512]{1,0:T(2,128)(2,1)S(1)}, bf16[1,512]{1,0:T(2,128)(2,1)S(1)}, u32[]{:S(2)}, u32[]{:S(2)}) collective-permute-start(bf16[1,512]{1,0:T(2,128)(2,1)S(1)} %reshape.301), channel_id=1, source_target_pairs={{0,2},{2,4},{4,6},{6,0},{1,3},{3,5},{5,7},{7,1},{8,10},{10,12},{12... | collective-permute-start | bytes 3080 | tf_op jit(solution)/shard_map/ppermute | solution.py:301
  11.7 10.4 %collective-permute-start.1 = (bf16[1,512]{1,0:T(2,128)(2,1)S(1)}, bf16[1,512]{1,0:T(2,128)(2,1)S(1)}, u32[]{:S(2)}, u32[]{:S(2)}) collective-permute-start(bf16[1,512]{1,0:T(2,128)(2,1)S(1)} %reshape.301), channel_id=1, source_target_pairs={{0,4},{2,6},{4,0},{6,2},{1,5},{3,7},{5,1},{7,3},{8,12},{10,14},{12... | collective-permute-start | bytes 3080 | tf_op jit(solution)/shard_map/ppermute | solution.py:301
  14.3 7.8 %collective-permute-start.2 = (bf16[1,512]{1,0:T(2,128)(2,1)S(1)}, bf16[1,512]{1,0:T(2,128)(2,1)S(1)}, u32[]{:S(2)}, u32[]{:S(2)}) collective-permute-start(bf16[1,512]{1,0:T(2,128)(2,1)S(1)} %reshape.301), channel_id=1, source_target_pairs={{0,6},{2,0},{4,2},{6,4},{1,7},{3,1},{5,3},{7,5},{8,14},{10,8},{12,... | collective-permute-start | bytes 3080 | tf_op jit(solution)/shard_map/ppermute | solution.py:301
  22.2 45.6 %all-to-all-start = ((bf16[4,128,1792]{2,1,0:T(8,128)(2,1)}), bf16[4,128,1792]{2,1,0:T(8,128)(2,1)S(1)}, u32[]{:S(2)}, u32[]{:S(2)}) async-start(bf16[4,128,1792]{2,1,0:T(8,128)(2,1)} %pad_maximum_fusion.5), calls=%async_computation | async-start | bytes 3670016 | tf_op jit(solution)/shard_map/all_to_all | solution.py:374
  30.0 41.8 %copy-start.35 = (s32[1024]{0:T(1024)S(1)}, s32[1024]{0:T(1024)}, u32[]{:S(2)}) copy-start(s32[1024]{0:T(1024)} %fusion.74) | copy-start | bytes 12292
  30.0 43.5 %copy-start.5 = (bf16[128,2048]{1,0:T(8,128)(2,1)S(1)}, bf16[128,2048]{1,0:T(8,128)(2,1)}, u32[]{:S(2)}) copy-start(bf16[128,2048]{1,0:T(8,128)(2,1)} %param.13) | copy-start | bytes 1572868
  30.8 42.7 %collective-permute-start.3 = (bf16[128,1920]{1,0:T(8,128)(2,1)}, bf16[128,1920]{1,0:T(8,128)(2,1)}, u32[]{:S(2)}, u32[]{:S(2)}) collective-permute-start(bf16[128,1920]{1,0:T(8,128)(2,1)} %pad_maximum_fusion.12), channel_id=1, source_target_pairs={{0,8},{8,16},{16,24},{24,0},{1,9},{9,17},{17,25},{25,1},{2,10},{10... | collective-permute-start | bytes 1474568 | tf_op jit(solution)/shard_map/ppermute | solution.py:301
  33.1 40.4 %collective-permute-start.4 = (bf16[128,1920]{1,0:T(8,128)(2,1)}, bf16[128,1920]{1,0:T(8,128)(2,1)}, u32[]{:S(2)}, u32[]{:S(2)}) collective-permute-start(bf16[128,1920]{1,0:T(8,128)(2,1)} %pad_maximum_fusion.13), channel_id=1, source_target_pairs={{0,16},{8,24},{16,0},{24,8},{1,17},{9,25},{17,1},{25,9},{2,18},{10... | collective-permute-start | bytes 1474568 | tf_op jit(solution)/shard_map/ppermute | solution.py:301
  35.5 38.0 %collective-permute-start.5 = (bf16[128,1920]{1,0:T(8,128)(2,1)}, bf16[128,1920]{1,0:T(8,128)(2,1)}, u32[]{:S(2)}, u32[]{:S(2)}) collective-permute-start(bf16[128,1920]{1,0:T(8,128)(2,1)} %pad_maximum_fusion.14), channel_id=1, source_target_pairs={{0,24},{8,0},{16,8},{24,16},{1,25},{9,1},{17,9},{25,17},{2,26},{10... | collective-permute-start | bytes 1474568 | tf_op jit(solution)/shard_map/ppermute | solution.py:301
  68.7 18.8 %collective-permute-start.6 = (bf16[512,768]{1,0:T(8,128)(2,1)}, bf16[512,768]{1,0:T(8,128)(2,1)}, u32[]{:S(2)}, u32[]{:S(2)}) collective-permute-start(bf16[512,768]{1,0:T(8,128)(2,1)} %slice.548), channel_id=1, source_target_pairs={{0,8},{8,0},{16,24},{24,16},{1,9},{9,1},{17,25},{25,17},{2,10},{10... | collective-permute-start | bytes 2359304 | tf_op jit(solution)/shard_map/ppermute | solution.py:330
  70.2 19.9 %collective-permute-start.7 = (bf16[512,768]{1,0:T(8,128)(2,1)}, bf16[512,768]{1,0:T(8,128)(2,1)}, u32[]{:S(2)}, u32[]{:S(2)}) collective-permute-start(bf16[512,768]{1,0:T(8,128)(2,1)} %slice.548), channel_id=1, source_target_pairs={{0,16},{8,24},{16,0},{24,8},{1,17},{9,25},{17,1},{25,9},{2,18},{10... | collective-permute-start | bytes 2359304 | tf_op jit(solution)/shard_map/ppermute | solution.py:330
  75.1 64.0 %all-to-all-start.1 = ((bf16[4,128,2048]{2,1,0:T(8,128)(2,1)}), bf16[4,128,2048]{2,1,0:T(8,128)(2,1)}, u32[]{:S(2)}, u32[]{:S(2)}) async-start(bf16[4,128,2048]{2,1,0:T(8,128)(2,1)} %broadcast_in_dim.190), calls=%async_computation.1 | async-start | bytes 4194304 | tf_op jit(solution)/shard_map/all_to_all | solution.py:374
  79.6 215.0 %all-gather.2.cloned.1.call-start = ((), (), s32[]{:S(2)}) async-start(), calls=%async_computation.10 | async-start | bytes 9830400 | tf_op jit(solution)/shard_map/all_gather | solution.py:542
  88.5 9.2 %collective-permute-start.8 = (bf16[256,768]{1,0:T(8,128)(2,1)S(1)}, bf16[256,768]{1,0:T(8,128)(2,1)S(1)}, u32[]{:S(2)}, u32[]{:S(2)}) collective-permute-start(bf16[256,768]{1,0:T(8,128)(2,1)S(1)} %slice.549), channel_id=1, source_target_pairs={{0,16},{8,24},{16,0},{24,8},{1,17},{9,25},{17,1},{25,9},{2,18},{10... | collective-permute-start | bytes 1179656 | tf_op jit(solution)/shard_map/ppermute | solution.py:330
  91.1 8.9 %collective-permute-start.9 = (bf16[256,768]{1,0:T(8,128)(2,1)S(1)}, bf16[256,768]{1,0:T(8,128)(2,1)S(1)}, u32[]{:S(2)}, u32[]{:S(2)}) collective-permute-start(bf16[256,768]{1,0:T(8,128)(2,1)S(1)} %slice.550), channel_id=1, source_target_pairs={{0,8},{8,0},{16,24},{24,16},{1,9},{9,1},{17,25},{25,17},{2,10},{10... | collective-permute-start | bytes 1179656 | tf_op jit(solution)/shard_map/ppermute | solution.py:330
  101.0 25.9 %collective-permute-start.10 = (bf16[512,1024]{1,0:T(8,128)(2,1)S(1)}, bf16[512,1024]{1,0:T(8,128)(2,1)S(1)}, u32[]{:S(2)}, u32[]{:S(2)}) collective-permute-start(bf16[512,1024]{1,0:T(8,128)(2,1)S(1)} %slice.423), channel_id=1, source_target_pairs={{0,8},{8,0},{16,24},{24,16},{1,9},{9,1},{17,25},{25,17},{2,10},{10... | collective-permute-start | bytes 3145736 | tf_op jit(solution)/shard_map/ppermute | solution.py:330
  102.5 26.0 %collective-permute-start.11 = (bf16[512,1024]{1,0:T(8,128)(2,1)S(1)}, bf16[512,1024]{1,0:T(8,128)(2,1)S(1)}, u32[]{:S(2)}, u32[]{:S(2)}) collective-permute-start(bf16[512,1024]{1,0:T(8,128)(2,1)S(1)} %slice.423), channel_id=1, source_target_pairs={{0,16},{8,24},{16,0},{24,8},{1,17},{9,25},{17,1},{25,9},{2,18},{10... | collective-permute-start | bytes 3145736 | tf_op jit(solution)/shard_map/ppermute | solution.py:330
  103.1 20.2 %collective-permute-start.15 = (bf16[4,256]{1,0:T(4,128)(2,1)S(1)}, bf16[4,256]{1,0:T(4,128)(2,1)S(1)}, u32[]{:S(2)}, u32[]{:S(2)}) collective-permute-start(bf16[4,256]{1,0:T(4,128)(2,1)S(1)} %get-tuple-element.181), channel_id=1, source_target_pairs={{0,8},{8,16},{16,24},{24,0},{1,9},{9,17},{17,25},{25,1},{2,10},{10... | collective-permute-start | bytes 6152 | tf_op jit(solution)/shard_map/ppermute | solution.py:301
  103.6 35.5 %collective-permute-start.16 = (bf16[4,256]{1,0:T(4,128)(2,1)S(1)}, bf16[4,256]{1,0:T(4,128)(2,1)S(1)}, u32[]{:S(2)}, u32[]{:S(2)}) collective-permute-start(bf16[4,256]{1,0:T(4,128)(2,1)S(1)} %get-tuple-element.181), channel_id=1, source_target_pairs={{0,16},{8,24},{16,0},{24,8},{1,17},{9,25},{17,1},{25,9},{2,18},{10... | collective-permute-start | bytes 6152 | tf_op jit(solution)/shard_map/ppermute | solution.py:301
  105.1 34.0 %collective-permute-start.17 = (bf16[4,256]{1,0:T(4,128)(2,1)S(1)}, bf16[4,256]{1,0:T(4,128)(2,1)S(1)}, u32[]{:S(2)}, u32[]{:S(2)}) collective-permute-start(bf16[4,256]{1,0:T(4,128)(2,1)S(1)} %get-tuple-element.181), channel_id=1, source_target_pairs={{0,24},{8,0},{16,8},{24,16},{1,25},{9,1},{17,9},{25,17},{2,26},{10... | collective-permute-start | bytes 6152 | tf_op jit(solution)/shard_map/ppermute | solution.py:301
  126.9 10.0 %collective-permute-start.12 = (bf16[256,1024]{1,0:T(8,128)(2,1)S(1)}, bf16[256,1024]{1,0:T(8,128)(2,1)S(1)}, u32[]{:S(2)}, u32[]{:S(2)}) collective-permute-start(bf16[256,1024]{1,0:T(8,128)(2,1)S(1)} %slice.551), channel_id=1, source_target_pairs={{0,16},{8,24},{16,0},{24,8},{1,17},{9,25},{17,1},{25,9},{2,18},{10... | collective-permute-start | bytes 1572872 | tf_op jit(solution)/shard_map/ppermute | solution.py:330
  128.6 9.7 %collective-permute-start.13 = (bf16[256,1024]{1,0:T(8,128)(2,1)S(1)}, bf16[256,1024]{1,0:T(8,128)(2,1)S(1)}, u32[]{:S(2)}, u32[]{:S(2)}) collective-permute-start(bf16[256,1024]{1,0:T(8,128)(2,1)S(1)} %slice.552), channel_id=1, source_target_pairs={{0,8},{8,0},{16,24},{24,16},{1,9},{9,1},{17,25},{25,17},{2,10},{10... | collective-permute-start | bytes 1572872 | tf_op jit(solution)/shard_map/ppermute | solution.py:330
  139.1 5.7 collective-permute-start.14
  157.0 22.0 %collective-permute-start.18 = (bf16[128,2048]{1,0:T(8,128)(2,1)S(1)}, bf16[128,2048]{1,0:T(8,128)(2,1)S(1)}, u32[]{:S(2)}, u32[]{:S(2)}) collective-permute-start(bf16[128,2048]{1,0:T(8,128)(2,1)S(1)} %copy-done.27), channel_id=1, source_target_pairs={{0,8},{8,16},{16,24},{24,0},{1,9},{9,17},{17,25},{25,1},{2,10},{10... | collective-permute-start | bytes 1572872 | tf_op jit(solution)/shard_map/ppermute | solution.py:301
  158.0 25.3 %collective-permute-start.19 = (bf16[128,2048]{1,0:T(8,128)(2,1)S(1)}, bf16[128,2048]{1,0:T(8,128)(2,1)S(1)}, u32[]{:S(2)}, u32[]{:S(2)}) collective-permute-start(bf16[128,2048]{1,0:T(8,128)(2,1)S(1)} %copy-done.27), channel_id=1, source_target_pairs={{0,16},{8,24},{16,0},{24,8},{1,17},{9,25},{17,1},{25,9},{2,18},{10... | collective-permute-start | bytes 1572872 | tf_op jit(solution)/shard_map/ppermute | solution.py:301
  158.9 24.4 %collective-permute-start.20 = (bf16[128,2048]{1,0:T(8,128)(2,1)S(1)}, bf16[128,2048]{1,0:T(8,128)(2,1)S(1)}, u32[]{:S(2)}, u32[]{:S(2)}) collective-permute-start(bf16[128,2048]{1,0:T(8,128)(2,1)S(1)} %copy-done.27), channel_id=1, source_target_pairs={{0,24},{8,0},{16,8},{24,16},{1,25},{9,1},{17,9},{25,17},{2,26},{10... | collective-permute-start | bytes 1572872 | tf_op jit(solution)/shard_map/ppermute | solution.py:301
  185.4 30.2 %all-to-all-start.2 = ((bf16[4,256,256]{1,2,0:T(8,128)(2,1)}), bf16[4,256,256]{1,2,0:T(8,128)(2,1)S(1)}, u32[]{:S(2)}, u32[]{:S(2)}) async-start(bf16[4,256,256]{1,2,0:T(8,128)(2,1)} %copy.158), calls=%async_computation.2 | async-start | bytes 1048576 | tf_op jit(solution)/shard_map/all_to_all | solution.py:374
  219.3 2.2 collective-permute-start.21
  221.0 4.5 collective-permute-start.22
  259.1 4.2 collective-permute-start.23
  318.0 4.5 collective-permute-start.24
  326.3 34.5 %all-to-all-start.4 = ((bf16[4,128,2048]{2,1,0:T(8,128)(2,1)}), bf16[4,128,2048]{2,1,0:T(8,128)(2,1)}, u32[]{:S(2)}, u32[]{:S(2)}) async-start(bf16[4,128,2048]{2,1,0:T(8,128)(2,1)} %fusion.9), calls=%async_computation.4 | async-start | bytes 4194304 | tf_op jit(solution)/shard_map/all_to_all | solution.py:374
  330.8 187.4 %reduce-scatter.2.cloned.1.call-start = ((), (), s32[]{:S(2)}) async-start(), calls=%async_computation.11 | async-start | bytes 9830400 | tf_op jit(solution)/shard_map/reduce_scatter | solution.py:593
  364.3 3.8 collective-permute-start.25
  367.9 18.1 %collective-permute-start.26 = (bf16[4,128,2048]{2,1,0:T(8,128)(2,1)}, bf16[4,128,2048]{2,1,0:T(8,128)(2,1)}, u32[]{:S(2)}, u32[]{:S(2)}) collective-permute-start(bf16[4,128,2048]{2,1,0:T(8,128)(2,1)} %bitcast.46), channel_id=1, source_target_pairs={{0,1},{1,0},{2,3},{3,2},{4,5},{5,4},{6,7},{7,6},{8,9},{9,8},{10,11... | collective-permute-start | bytes 6291464 | tf_op jit(solution)/shard_map/ppermute | solution.py:301
  372.6 36.0 %all-to-all-start.5 = ((bf16[4,256,256]{2,1,0:T(8,128)(2,1)}), bf16[4,256,256]{2,1,0:T(8,128)(2,1)}, u32[]{:S(2)}, u32[]{:S(2)}) async-start(bf16[4,256,256]{2,1,0:T(8,128)(2,1)} %bitcast.261), calls=%async_computation.5 | async-start | bytes 1048576 | tf_op jit(solution)/shard_map/all_to_all | solution.py:374
  380.2 33.3 %collective-permute-start.27 = (bf16[2,512,512]{2,1,0:T(8,128)(2,1)}, bf16[2,512,512]{2,1,0:T(8,128)(2,1)}, u32[]{:S(2)}, u32[]{:S(2)}) collective-permute-start(bf16[2,512,512]{2,1,0:T(8,128)(2,1)} %pad_maximum_fusion.8), channel_id=1, source_target_pairs={{0,8},{8,0},{16,24},{24,16},{1,9},{9,1},{17,25},{25,17},{2,10},{10... | collective-permute-start | bytes 3145736 | tf_op jit(solution)/shard_map/ppermute | solution.py:330
  384.6 28.9 %collective-permute-start.28 = (bf16[2,512,512]{2,1,0:T(8,128)(2,1)}, bf16[2,512,512]{2,1,0:T(8,128)(2,1)}, u32[]{:S(2)}, u32[]{:S(2)}) collective-permute-start(bf16[2,512,512]{2,1,0:T(8,128)(2,1)} %pad_maximum_fusion.9), channel_id=1, source_target_pairs={{0,16},{8,24},{16,0},{24,8},{1,17},{9,25},{17,1},{25,9},{2,18},{10... | collective-permute-start | bytes 3145736 | tf_op jit(solution)/shard_map/ppermute | solution.py:330
  408.6 30.0 %all-to-all-start.6 = ((bf16[4,128,2048]{2,1,0:T(8,128)(2,1)}), bf16[4,128,2048]{2,1,0:T(8,128)(2,1)}, u32[]{:S(2)}, u32[]{:S(2)}) async-start(bf16[4,128,2048]{2,1,0:T(8,128)(2,1)} %fusion.8), calls=%async_computation.6 | async-start | bytes 4194304 | tf_op jit(solution)/shard_map/all_to_all | solution.py:374
  446.7 22.8 %collective-permute-start.29 = (bf16[4,128,2048]{2,1,0:T(8,128)(2,1)}, bf16[4,128,2048]{2,1,0:T(8,128)(2,1)}, u32[]{:S(2)}, u32[]{:S(2)}) collective-permute-start(bf16[4,128,2048]{2,1,0:T(8,128)(2,1)} %bitcast.55), channel_id=1, source_target_pairs={{0,1},{1,0},{2,3},{3,2},{4,5},{5,4},{6,7},{7,6},{8,9},{9,8},{10,11... | collective-permute-start | bytes 6291464 | tf_op jit(solution)/shard_map/ppermute | solution.py:301
  448.9 14.6 %collective-permute-start.40 = (bf16[512,512]{1,0:T(8,128)(2,1)}, bf16[512,512]{1,0:T(8,128)(2,1)}, u32[]{:S(2)}, u32[]{:S(2)}) collective-permute-start(bf16[512,512]{1,0:T(8,128)(2,1)} %fusion.39), channel_id=1, source_target_pairs={{0,16},{8,24},{16,0},{24,8},{1,17},{9,25},{17,1},{25,9},{2,18},{10... | collective-permute-start | bytes 1572872 | tf_op jit(solution)/shard_map/ppermute | solution.py:330
  452.5 14.4 %collective-permute-start.41 = (bf16[512,512]{1,0:T(8,128)(2,1)}, bf16[512,512]{1,0:T(8,128)(2,1)}, u32[]{:S(2)}, u32[]{:S(2)}) collective-permute-start(bf16[512,512]{1,0:T(8,128)(2,1)} %fusion.38), channel_id=1, source_target_pairs={{0,8},{8,0},{16,24},{24,16},{1,9},{9,1},{17,25},{25,17},{2,10},{10... | collective-permute-start | bytes 1572872 | tf_op jit(solution)/shard_map/ppermute | solution.py:330
  456.1 13.4 %copy-start.2 = (bf16[512,2048]{1,0:T(8,128)(2,1)S(1)}, bf16[512,2048]{1,0:T(8,128)(2,1)}, u32[]{:S(2)}) copy-start(bf16[512,2048]{1,0:T(8,128)(2,1)} %get-tuple-element.138) | copy-start | bytes 6291460
  473.3 70.3 %all-to-all-start.7 = ((bf16[4,128,2048]{2,1,0:T(8,128)(2,1)}), bf16[4,128,2048]{2,1,0:T(8,128)(2,1)}, u32[]{:S(2)}, u32[]{:S(2)}) async-start(bf16[4,128,2048]{2,1,0:T(8,128)(2,1)} %fusion.7), calls=%async_computation.7 | async-start | bytes 4194304 | tf_op jit(solution)/shard_map/all_to_all | solution.py:374
  484.2 18.6 %collective-permute-start.42 = (bf16[2,512,384]{2,1,0:T(8,128)(2,1)S(1)}, bf16[2,512,384]{2,1,0:T(8,128)(2,1)S(1)}, u32[]{:S(2)}, u32[]{:S(2)}) collective-permute-start(bf16[2,512,384]{2,1,0:T(8,128)(2,1)S(1)} %pad_maximum_fusion.10), channel_id=1, source_target_pairs={{0,8},{8,0},{16,24},{24,16},{1,9},{9,1},{17,25},{25,17},{2,10},{10... | collective-permute-start | bytes 2359304 | tf_op jit(solution)/shard_map/ppermute | solution.py:330
  488.1 20.5 %collective-permute-start.44 = (bf16[2,512,384]{2,1,0:T(8,128)(2,1)S(1)}, bf16[2,512,384]{2,1,0:T(8,128)(2,1)S(1)}, u32[]{:S(2)}, u32[]{:S(2)}) collective-permute-start(bf16[2,512,384]{2,1,0:T(8,128)(2,1)S(1)} %pad_maximum_fusion.11), channel_id=1, source_target_pairs={{0,16},{8,24},{16,0},{24,8},{1,17},{9,25},{17,1},{25,9},{2,18},{10... | collective-permute-start | bytes 2359304 | tf_op jit(solution)/shard_map/ppermute | solution.py:330
  502.9 12.2 %collective-permute-start.43 = (bf16[512,384]{1,0:T(8,128)(2,1)S(1)}, bf16[512,384]{1,0:T(8,128)(2,1)S(1)}, u32[]{:S(2)}, u32[]{:S(2)}) collective-permute-start(bf16[512,384]{1,0:T(8,128)(2,1)S(1)} %fusion.50), channel_id=1, source_target_pairs={{0,16},{8,24},{16,0},{24,8},{1,17},{9,25},{17,1},{25,9},{2,18},{10... | collective-permute-start | bytes 1179656 | tf_op jit(solution)/shard_map/ppermute | solution.py:330
  508.7 7.8 %collective-permute-start.45 = (bf16[512,384]{1,0:T(8,128)(2,1)S(1)}, bf16[512,384]{1,0:T(8,128)(2,1)S(1)}, u32[]{:S(2)}, u32[]{:S(2)}) collective-permute-start(bf16[512,384]{1,0:T(8,128)(2,1)S(1)} %fusion.49), channel_id=1, source_target_pairs={{0,8},{8,0},{16,24},{24,16},{1,9},{9,1},{17,25},{25,17},{2,10},{10... | collective-permute-start | bytes 1179656 | tf_op jit(solution)/shard_map/ppermute | solution.py:330
  525.8 29.6 %collective-permute-start.30 = (bf16[128,1920]{1,0:T(8,128)(2,1)}, bf16[128,1920]{1,0:T(8,128)(2,1)}, u32[]{:S(2)}, u32[]{:S(2)}) collective-permute-start(bf16[128,1920]{1,0:T(8,128)(2,1)} %get-tuple-element.150), channel_id=1, source_target_pairs={{0,8},{8,16},{16,24},{24,0},{1,9},{9,17},{17,25},{25,1},{2,10},{10... | collective-permute-start | bytes 1474568 | tf_op jit(solution)/shard_map/ppermute | solution.py:301
  545.7 47.1 %all-to-all-start.8 = ((bf16[4,128,1792]{2,1,0:T(8,128)(2,1)}), bf16[4,128,1792]{2,1,0:T(8,128)(2,1)}, u32[]{:S(2)}, u32[]{:S(2)}) async-start(bf16[4,128,1792]{2,1,0:T(8,128)(2,1)} %pad_maximum_fusion.6), calls=%async_computation.9 | async-start | bytes 3670016 | tf_op jit(solution)/shard_map/all_to_all | solution.py:374
  550.1 17.1 %copy-start.6 = (bf16[128,2048]{1,0:T(8,128)(2,1)S(1)}, bf16[128,2048]{1,0:T(8,128)(2,1)}, u32[]{:S(2)}) copy-start(bf16[128,2048]{1,0:T(8,128)(2,1)} %param.13) | copy-start | bytes 1572868
  550.2 17.1 %copy-start.31 = (f32[1,4,4,128]{3,0,2,1:T(1,128)S(1)}, f32[1,4,4,128]{3,0,2,1:T(1,128)}, u32[]{:S(2)}) copy-start(f32[1,4,4,128]{3,0,2,1:T(1,128)} %copy-done.30) | copy-start | bytes 24580
  550.2 13.0 %collective-permute-start.31 = (bf16[128,1920]{1,0:T(8,128)(2,1)}, bf16[128,1920]{1,0:T(8,128)(2,1)S(1)}, u32[]{:S(2)}, u32[]{:S(2)}) collective-permute-start(bf16[128,1920]{1,0:T(8,128)(2,1)} %get-tuple-element.149), channel_id=1, source_target_pairs={{0,16},{8,24},{16,0},{24,8},{1,17},{9,25},{17,1},{25,9},{2,18},{10... | collective-permute-start | bytes 1474568 | tf_op jit(solution)/shard_map/ppermute | solution.py:301
  553.9 13.8 %copy-start.13 = (bf16[128,2048]{1,0:T(8,128)(2,1)S(1)}, bf16[128,2048]{1,0:T(8,128)(2,1)}, u32[]{:S(2)}) copy-start(bf16[128,2048]{1,0:T(8,128)(2,1)} %param.25) | copy-start | bytes 1572868
  553.9 12.6 %collective-permute-start.32 = (bf16[128,1920]{1,0:T(8,128)(2,1)S(1)}, bf16[128,1920]{1,0:T(8,128)(2,1)S(1)}, u32[]{:S(2)}, u32[]{:S(2)}) collective-permute-start(bf16[128,1920]{1,0:T(8,128)(2,1)S(1)} %copy-done.28), channel_id=1, source_target_pairs={{0,24},{8,0},{16,8},{24,16},{1,25},{9,1},{17,9},{25,17},{2,26},{10... | collective-permute-start | bytes 1474568 | tf_op jit(solution)/shard_map/ppermute | solution.py:301
  571.9 22.3 %collective-permute-start.33 = (f32[41,128]{1,0:T(8,128)S(1)}, f32[41,128]{1,0:T(8,128)S(1)}, u32[]{:S(2)}, u32[]{:S(2)}) collective-permute-start(f32[41,128]{1,0:T(8,128)S(1)} %get-tuple-element.176), channel_id=1, source_target_pairs={{0,1},{1,0},{2,3},{3,2},{4,5},{5,4},{6,7},{7,6},{8,9},{9,8},{10,11... | collective-permute-start | bytes 62984 | tf_op jit(solution)/shard_map/ppermute | solution.py:301
  594.4 9.8 %collective-permute-start.34 = (f32[41,128]{1,0:T(8,128)S(1)}, f32[41,128]{1,0:T(8,128)S(1)}, u32[]{:S(2)}, u32[]{:S(2)}) collective-permute-start(f32[41,128]{1,0:T(8,128)S(1)} %reduce_sum.196), channel_id=1, source_target_pairs={{0,8},{8,16},{16,24},{24,0},{1,9},{9,17},{17,25},{25,1},{2,10},{10... | collective-permute-start | bytes 62984 | tf_op jit(solution)/shard_map/ppermute | solution.py:301
  596.0 8.2 %collective-permute-start.35 = (f32[41,128]{1,0:T(8,128)S(1)}, f32[41,128]{1,0:T(8,128)S(1)}, u32[]{:S(2)}, u32[]{:S(2)}) collective-permute-start(f32[41,128]{1,0:T(8,128)S(1)} %reduce_sum.196), channel_id=1, source_target_pairs={{0,16},{8,24},{16,0},{24,8},{1,17},{9,25},{17,1},{25,9},{2,18},{10... | collective-permute-start | bytes 62984 | tf_op jit(solution)/shard_map/ppermute | solution.py:301
  597.9 6.4 %collective-permute-start.36 = (f32[41,128]{1,0:T(8,128)S(1)}, f32[41,128]{1,0:T(8,128)S(1)}, u32[]{:S(2)}, u32[]{:S(2)}) collective-permute-start(f32[41,128]{1,0:T(8,128)S(1)} %reduce_sum.196), channel_id=1, source_target_pairs={{0,24},{8,0},{16,8},{24,16},{1,25},{9,1},{17,9},{25,17},{2,26},{10... | collective-permute-start | bytes 62984 | tf_op jit(solution)/shard_map/ppermute | solution.py:301
  604.9 15.2 %collective-permute-start.37 = (f32[41,128]{1,0:T(8,128)S(1)}, f32[41,128]{1,0:T(8,128)S(1)}, u32[]{:S(2)}, u32[]{:S(2)}) collective-permute-start(f32[41,128]{1,0:T(8,128)S(1)} %reduce_sum.197), channel_id=1, source_target_pairs={{0,2},{2,4},{4,6},{6,0},{1,3},{3,5},{5,7},{7,1},{8,10},{10,12},{12... | collective-permute-start | bytes 62984 | tf_op jit(solution)/shard_map/ppermute | solution.py:301
  605.0 15.2 %collective-permute-start.38 = (f32[41,128]{1,0:T(8,128)S(1)}, f32[41,128]{1,0:T(8,128)S(1)}, u32[]{:S(2)}, u32[]{:S(2)}) collective-permute-start(f32[41,128]{1,0:T(8,128)S(1)} %reduce_sum.197), channel_id=1, source_target_pairs={{0,4},{2,6},{4,0},{6,2},{1,5},{3,7},{5,1},{7,3},{8,12},{10,14},{12... | collective-permute-start | bytes 62984 | tf_op jit(solution)/shard_map/ppermute | solution.py:301
  607.0 13.2 %collective-permute-start.39 = (f32[41,128]{1,0:T(8,128)S(1)}, f32[41,128]{1,0:T(8,128)S(1)}, u32[]{:S(2)}, u32[]{:S(2)}) collective-permute-start(f32[41,128]{1,0:T(8,128)S(1)} %reduce_sum.197), channel_id=1, source_target_pairs={{0,6},{2,0},{4,2},{6,4},{1,7},{3,1},{5,3},{7,5},{8,14},{10,8},{12,... | collective-permute-start | bytes 62984 | tf_op jit(solution)/shard_map/ppermute | solution.py:301
  (32 other events, 165.8 us)
Sparse Core Ops, SparseCore 0:
  144.9 149.5 all-gather.1
  353.4 162.0 reduce-scatter.1

commit v3 on v2

--- a/solution.py
+++ b/solution.py
@@ -515,13 +515,11 @@
 
     here = jnp.reshape(t, (1,)).astype(jnp.int32)
 
+    x_core = lax.all_gather(layer_input, "ctx", axis=0)
     small_in = jnp.concatenate([attn_gain, ff_gain, segments.astype(bf16)]).reshape(1, -1)
     small_pieces = gather_axis(small_in, "ctx").reshape(pieces, -1)
     gain_cols = attn_gain.shape[0]
     segs = small_pieces[:, 2 * gain_cols :].astype(jnp.int32).reshape(seq_len)
-    gains = gather_axis(small_pieces[:, : 2 * gain_cols], "dp").reshape(dps, pieces, 2, gain_cols)
-    gains = jnp.transpose(gains, (2, 0, 1, 3)).reshape(2, width).astype(f32)
-    gain_one, gain_two = gains[0:1], gains[1:2]
     attn_blocks = piece_columns([query_weight, key_weight, value_weight])
     out_block = jnp.broadcast_to(output_weight.T[None], (pieces, output_weight.shape[1], part_heads * DH))
     attn_blocks = jnp.concatenate([attn_blocks, out_block], axis=2)
@@ -536,15 +534,19 @@
         return jnp.concatenate(columns, axis=1)
 
     ff_arrived = [shift(ff_block((s + k) % dps), "dp", k) for k in range(1, dps)]
-    x_copies = jnp.broadcast_to(layer_input[None], (pieces,) + layer_input.shape)
-    x_core = exchange(tie(x_copies, attn_pieces, gains, *ff_arrived), "ctx")
+    gains = gather_axis(tie(small_pieces, *ff_arrived)[:, : 2 * gain_cols], "dp")
+    gains = gains.reshape(dps, pieces, 2, gain_cols)
+    gains = jnp.transpose(gains, (2, 0, 1, 3)).reshape(2, width).astype(f32)
+    gain_one, gain_two = gains[0:1], gains[1:2]
+    dy_own = by_piece(cotangent)
+    dy_arrived = arrivals(tie(dy_own, *ff_arrived), "dp")
+    attn_pieces = tie(attn_pieces, gains, *ff_arrived, *dy_arrived)
     ff_rows = assemble(ff_block(s), ff_arrived, "dp")
     w_ff = lax.all_gather(flat(ff_rows), "ctx", axis=0, tiled=True)
     w_gu, w_down = w_ff[:, : 2 * units], w_ff[:, 2 * units :]
 
     w_qkv = gather_rows(attn_pieces[:, : 3 * head_cols])
-    w_out = gather_rows(tie(attn_pieces, w_qkv)[:, 3 * head_cols :])
-    x_seq = both_cores(tie(x_core, w_out))
+    x_seq = both_cores(x_core)
 
     own_table = lax.dynamic_slice_in_dim(bias_table, z * heads, heads, 1)
     lanes_onehot = lane_buckets()
@@ -554,12 +556,10 @@
     x_wide = tie(x_seq, w_qkv).astype(f32)
     normed_seq = (x_wide * inverse_scale(x_wide) * gain_one).astype(bf16)
     qkv = mm(normed_seq, w_qkv).astype(bf16)
-    dy_arrived = arrivals(tie(by_piece(cotangent), qkv), "dp")
+    w_out = gather_rows(tie(attn_pieces, qkv)[:, 3 * head_cols :])
     mixed_heads, lse_rows = attend(here, qkv, segs, vectors, far)
-    mixed = exchange(
-        tie(mixed_heads, *dy_arrived).reshape(pieces, parts * rows, head_cols), "ctx"
-    )
-    dy_all = both_cores(assemble(by_piece(cotangent), dy_arrived, "dp"))
+    mixed = exchange(mixed_heads.reshape(pieces, parts * rows, head_cols), "ctx")
+    dy_all = both_cores(assemble(tie(dy_own, qkv), dy_arrived, "dp"))
     mixed = jnp.transpose(mixed, (1, 0, 2)).reshape(rows * parts, -1)
     attn_part = mm_nt(mixed, w_out)
     attn_own = attn_part[:rows] + swap(attn_part[rows:].astype(bf16)).astype(f32)
@@ -586,12 +586,11 @@
     gate_up_late, inner_late = lax.optimization_barrier(
         (gate_up_grad, inner, normed_two_core)
     )[:2]
-    ff_wgrad = jnp.concatenate(
-        [mm_tn(normed_two_all, gate_up_late).astype(bf16), mm_tn(dy_all, inner_late).astype(bf16)],
-        axis=1,
-    )
-    ff_sum = lax.psum_scatter(ff_wgrad, "ctx", scatter_dimension=0, tiled=True)
-    normed_two_sum = tie(normed_two_sum, ff_wgrad)
+    down_wgrad = mm_tn(dy_all, inner).astype(bf16)
+    down_sum = lax.psum_scatter(down_wgrad, "ctx", scatter_dimension=0, tiled=True)
+    gu_wgrad = mm_tn(normed_two_all, gate_up_late).astype(bf16)
+    gu_sum = lax.psum_scatter(gu_wgrad, "ctx", scatter_dimension=0, tiled=True)
+    normed_two_sum = tie(normed_two_sum, gu_wgrad)
     normed_two_sum = by_dp(normed_two_sum)
     normed_two_grad = normed_two_sum
 
@@ -608,7 +607,7 @@
     ff_core = sum_of_cores(ff_part, "dp")
     ff_stack = exchange(tie(ff_core, mixed_grad), "dp")
 
-    mixed_grad = tie(mixed_grad, *output_arrived)
+    mixed_grad = tie(mixed_grad, down_sum, *output_arrived)
     dqkv, diagonals, far_sums = attend_back(
         here, qkv, mixed_grad, segs, vectors, far, lse_rows
     )
@@ -619,15 +618,14 @@
     ff_own = by_dp(jnp.sum(tie(ff_stack, normed_one_core).astype(f32), axis=0))
     block_output = (hidden + ff_own).astype(bf16)
     qkv_sum, _ = reduce_weight(normed_seq, tie(dqkv, normed_one_core))
-    ff_blocks = tie(ff_sum, qkv_sum).reshape(dps, -1, 3 * units)
+    ff_blocks = jnp.concatenate([gu_sum, down_sum], axis=1)
+    ff_blocks = tie(ff_blocks, qkv_sum).reshape(dps, -1, 3 * units)
     ff_back = exchange_axis(lambda j: block_at(ff_blocks, j), "dp")
     gate_out, up_out, down_out = own_rows(ff_back, (units,) * 3)
+    down_out = down_out.T
     normed_one_grad = tie(normed_one_sum, block_output, ff_back)
     sums = jnp.concatenate([output_sum, qkv_sum], axis=2)
     back = exchange(tie(sums, normed_one_sum), "ctx")
-    at = output_sum.shape[2]
-    output_out = jnp.sum(back[:, :, :at].astype(f32), axis=0).T
-    query_out, key_out, value_out = own_rows(back[:, :, at:], (head_cols,) * 3)
     attn_gain_share = jnp.sum(normed_one_grad * unit_one, axis=0)
     input_grads = (
         hidden_grad + root_mean_square_backward(normed_one_grad, unit_one, scale_one, gain_one)
@@ -657,6 +655,10 @@
     ).reshape(-1, BLOCK)
     for axis in ("tensor", "dp", "ctx"):
         small = jnp.sum(gather_axis(small, axis), axis=0)
+    back = tie(back, small, gate_out, up_out, down_out)
+    at = output_sum.shape[2]
+    output_out = jnp.sum(back[:, :, :at].astype(f32), axis=0).T
+    query_out, key_out, value_out = own_rows(back[:, :, at:], (head_cols,) * 3)
     small = small.reshape(-1)
     gain_one_total, gain_two_total = small[:width], small[width : 2 * width]
     bias_total = small[2 * width : 2 * width + bias_full.size].reshape(bias_full.shape)
@@ -674,7 +676,7 @@
         gain_two_total,
         gate_out,
         up_out,
-        down_out.T,
+        down_out,
         rms_stats,
     )
 

time: 641 us -> 564 us (0.88)
  waiting for transfers between devices: 229 us -> 177 us
  local copies, waits for them, and re-layouts: 85.5 us -> 72.5 us
  other arithmetic: 72.7 us -> 65.3 us
    all_to_all x8 -> x7, waiting for transfers between devices: 117 us -> 46.8 us  [exchange(): return lax.all_to_all(stack, axis, 0, 0)]
    ppermute x16, waiting for transfers between devices: 48.4 us -> 87.2 us  [flip(): return lax.ppermute(value, 'dp', [(i, i ^ mask) for i in range(size)])]
    all_gather x1, waiting for transfers between devices: 28.9 us -> 2.11 us  [shards(): w_ff = lax.all_gather(flat(ff_rows), 'ctx', axis=0, tiled=True)]
    ppermute x30, starting transfers between devices: 34.6 us -> 46.7 us  [shift(): lax.ppermute(value, axis, [(i, (i + by) % size) for i in range(size)])]
    all_gather x0 -> x1, waiting for transfers between devices: none -> 9.17 us  [shards(): x_core = lax.all_gather(layer_input, 'ctx', axis=0)]
    unnamed x146 -> x170, local copies, waits for them, and re-layouts: 11.6 us -> 19 us
    concatenate x1, other arithmetic: 7.93 us -> 1.46 us  [shards(): ff_blocks = jnp.concatenate([gu_sum, down_sum], axis=1)]
    all_to_all x8 -> x7, starting transfers between devices: 35.7 us -> 30.2 us  [exchange(): return lax.all_to_all(stack, axis, 0, 0)]
  transfers between devices with their start and end apart: 56 -> 57, of which waited for: 25 -> 31; matrix products, arithmetic and copies ran while one was open for 31% -> 31% of each run, Pallas kernels for 5% -> 6%
where the time goes in v3:
time: 564 us; the launch traced here: 558 us
  waiting for transfers between devices  177 us (31%)
  starting transfers between devices  92.9 us (16%)
  matrix products  72.8 us (13%)
  local copies, waits for them, and re-layouts  72.5 us (13%)
  other arithmetic  65.3 us (12%)
  Pallas kernels  33.1 us (6%)
  blocking collectives  28.4 us (5%)
  between operations  16.4 us (3%)
    ppermute x16, waiting for transfers between devices, flip(): return lax.ppermute(value, 'dp', [(i, i ^ mask) for i in range(size)])  87.2 us
    all_to_all x7, waiting for transfers between devices, exchange(): return lax.all_to_all(stack, axis, 0, 0)  46.8 us
    ppermute x30, starting transfers between devices, shift(): lax.ppermute(value, axis, [(i, (i + by) % size) for i in range(size)])  46.7 us
    ppermute x30, waiting for transfers between devices, shift(): lax.ppermute(value, axis, [(i, (i + by) % size) for i in range(size)])  30.6 us
    all_to_all x7, starting transfers between devices, exchange(): return lax.all_to_all(stack, axis, 0, 0)  30.2 us
    all_to_all x1, blocking collectives, exchange(): return lax.all_to_all(stack, axis, 0, 0)  28.4 us
    dot_general x10, matrix products, mm_tn(): lax.dot_general(a, b, (((0,), (0,)), ((), ())), preferred_element_type=f32)  25.5 us
    dot_general x4, matrix products, dot_nt(): lax.dot_general(a, b, (((1,), (1,)), ((), ())), preferred_element_type=f32)  23.2 us
  transfers between devices with their start and end apart: 57, of which 31 were waited for; matrix products, arithmetic and copies ran while one was open for 31% of the time, Pallas kernels for 6%

profile of v3, /device:TPU:0, one launch (start us, length us, event | category | flops | bytes accessed | tf_op | source)
XLA Modules:
  0.0 557.9 jit_solution(1530167969067015405)
XLA Ops:
  8.7 5.1 collective-permute-start.3
  34.0 4.1 all-to-all-start
  48.0 8.4 %collective-permute-done.5 = bf16[128,1920]{1,0:T(8,128)(2,1)} collective-permute-done((bf16[128,1920]{1,0:T(8,128)(2,1)}, bf16[128,1920]{1,0:T(8,128)(2,1)}, u32[]{:S(2)}, u32[]{:S(2)}) %collective-permute-start.5) | collective-permute-done | bytes 491552 | tf_op jit(solution)/shard_map/ppermute | solution.py:301
  58.0 5.9 %collective-permute-start.14 = (bf16[4,256]{1,0:T(4,128)(2,1)S(1)}, bf16[4,256]{1,0:T(4,128)(2,1)S(1)}, u32[]{:S(2)}, u32[]{:S(2)}) collective-permute-start(bf16[4,256]{1,0:T(4,128)(2,1)S(1)} %slice.423), channel_id=1, source_target_pairs={{0,8},{8,16},{16,24},{24,0},{1,9},{9,17},{17,25},{25,1},{2,10},{10... | collective-permute-start | bytes 6152 | tf_op jit(solution)/shard_map/ppermute | solution.py:301
  72.9 9.2 %all-gather.6.cloned.1.call-done = bf16[512,2048]{1,0:T(8,128)(2,1)} async-done(((bf16[128,2048]{1,0:T(8,128)(2,1)}), bf16[512,2048]{1,0:T(8,128)(2,1)}) %all-gather.6.cloned.1.call-update) | async-done | bytes 2097168 | tf_op jit(solution)/shard_map/all_gather | solution.py:518
  82.1 12.0 %collective-permute-start.16 = (bf16[4,256]{1,0:T(4,128)(2,1)S(1)}, bf16[4,256]{1,0:T(4,128)(2,1)S(1)}, u32[]{:S(2)}, u32[]{:S(2)}) collective-permute-start(bf16[4,256]{1,0:T(4,128)(2,1)S(1)} %slice.423), channel_id=1, source_target_pairs={{0,24},{8,0},{16,8},{24,16},{1,25},{9,1},{17,9},{25,17},{2,26},{10... | collective-permute-start | bytes 6152 | tf_op jit(solution)/shard_map/ppermute | solution.py:301
  94.1 6.1 %all-to-all-done = bf16[4,128,1792]{2,1,0:T(8,128)(2,1)S(1)} async-done(((bf16[4,128,1792]{2,1,0:T(8,128)(2,1)}), bf16[4,128,1792]{2,1,0:T(8,128)(2,1)S(1)}, u32[]{:S(2)}, u32[]{:S(2)}) %all-to-all-start) | async-done | bytes 1835040 | tf_op jit(solution)/shard_map/all_to_all | solution.py:374
  104.5 16.1 %collective-permute-done.10 = bf16[512,768]{1,0:T(8,128)(2,1)S(1)} collective-permute-done((bf16[512,768]{1,0:T(8,128)(2,1)}, bf16[512,768]{1,0:T(8,128)(2,1)S(1)}, u32[]{:S(2)}, u32[]{:S(2)}) %collective-permute-start.10) | collective-permute-done | bytes 786464 | tf_op jit(solution)/shard_map/ppermute | solution.py:330
  123.9 6.7 %collective-permute-done.12 = bf16[256,768]{1,0:T(8,128)(2,1)S(1)} collective-permute-done((bf16[256,768]{1,0:T(8,128)(2,1)S(1)}, bf16[256,768]{1,0:T(8,128)(2,1)S(1)}, u32[]{:S(2)}, u32[]{:S(2)}) %collective-permute-start.12) | collective-permute-done | bytes 393248 | tf_op jit(solution)/shard_map/ppermute | solution.py:330
  132.0 3.1 pad_maximum_fusion
  137.0 4.5 convolution_convert_fusion.4.q_in.k_in.v_in
  144.7 15.1 %attend.1 = (bf16[1024,256]{1,0:T(8,128)(2,1)}, f32[2,2,1024]{2,1,0:T(2,128)}) custom-call(s32[1]{0:T(128)} %bitcast.here_ref, bf16[1024,768]{1,0:T(8,128)(2,1)} %convolution_convert_fusion.4.q_in.k_in.v_in, bf16[1024,768]{1,0:T(8,128)(2,1)} %convolution_convert_fusion.4.q_in.k_in.v_in, bf16[1024,768]{1,0:T(8,128)(2,1)} %convolution_convert_fusion.4.q_in.k_in.v_in, ...), custom_call_target="tpu_custom_call" | custom-call | flops 4294967296 | bytes 1048576 | tf_op jit(solution)/shard_map/attend/pallas_call | solution.py:246
  161.8 3.5 all-to-all-start.1
  165.8 2.6 broadcast_in_dim.196
  175.3 2.3 bitcast_dynamic-update-slice_fusion
  177.5 4.8 collective-permute-done.19
  185.6 9.9 %all-to-all-done.1 = bf16[4,256,256]{1,2,0:T(8,128)(2,1)S(1)} async-done(((bf16[4,256,256]{1,2,0:T(8,128)(2,1)}), bf16[4,256,256]{1,2,0:T(8,128)(2,1)S(1)}, u32[]{:S(2)}, u32[]{:S(2)}) %all-to-all-start.1) | async-done | bytes 524320 | tf_op jit(solution)/shard_map/all_to_all | solution.py:374
  195.5 3.7 fusion.97
  204.2 2.3 pad_maximum_fusion.1
  206.8 28.4 %all_to_all.40 = bf16[4,128,2048]{2,1,0:T(8,128)(2,1)S(1)} all-to-all(bf16[4,128,2048]{2,1,0:T(8,128)(2,1)S(1)} %broadcast_in_dim.211), channel_id=1, replica_groups=mesh['dp'=4,'ctx'=4,'tensor'=2] {'dp'}, dimensions={0} | all-to-all | bytes 4194304 | tf_op jit(solution)/shard_map/all_to_all | solution.py:374
  235.3 4.2 collective-permute-done.23
  239.4 2.3 pad_maximum_fusion.2
  241.7 2.1 all-gather.4.cloned.1.call-done
  243.8 9.2 %fusion.5 = f32[1024,1280]{0,1:T(8,128)S(1)} fusion(bf16[1024,2048]{1,0:T(8,128)(2,1)} %bitcast.254, bf16[2048,1920]{1,0:T(8,128)(2,1)} %all-gather.4.cloned.1.call-done), kind=kOutput, calls=%fused_computation.8 | convolution fusion | flops 5368709120 | bytes 14680064 | tf_op jit(solution)/shard_map/dot_general | solution.py:477
  253.0 5.8 %fusion.19 = (bf16[1024,640]{0,1:T(8,128)(2,1)S(1)}, bf16[1024,640]{0,1:T(8,128)(2,1)S(1)}, bf16[1024,640]{0,1:T(8,128)(2,1)}) fusion(f32[1024,1280]{0,1:T(8,128)S(1)} %fusion.5, bf16[1024,2048]{1,0:T(8,128)(2,1)S(1)} %bitcast.257, bf16[2048,1920]{1,0:T(8,128)(2,1)S(1)} %copy-done.50), kind=kOutput, calls=%fused_computation.34 | convolution fusion | flops 2701393920 | bytes 15990784 | tf_op jit(solution)/shard_map/dot_general | solution.py:477
  258.9 6.0 %fusion.10 = bf16[1024,2048]{1,0:T(8,128)(2,1)S(1)} fusion(bf16[2048,1920]{1,0:T(8,128)(2,1)S(1)} %copy-done.50, bf16[1024,640]{0,1:T(8,128)(2,1)S(1)} %get-tuple-element.137, bf16[1024,640]{0,1:T(8,128)(2,1)S(1)} %get-tuple-element.136), kind=kOutput, calls=%fused_computation.22 | convolution fusion | flops 5376049152 | bytes 12058624 | tf_op jit(solution)/shard_map/dot_general | solution.py:44
  264.9 2.5 fusion.95
  267.5 7.6 %convolution_convert_fusion.3 = bf16[2048,640]{1,0:T(8,128)(2,1)} fusion(bf16[1024,2048]{1,0:T(8,128)(2,1)} %bitcast.256, bf16[1024,640]{0,1:T(8,128)(2,1)} %get-tuple-element.56), kind=kOutput, calls=%fused_computation.27 | convolution fusion | flops 2685665280 | bytes 8126464 | tf_op jit(solution)/shard_map/dot_general | solution.py:485
  275.2 3.6 pad_maximum_fusion.3
  278.8 4.2 fusion.9
  283.0 4.5 all-to-all-start.3
  287.5 7.7 %convolution_convert_fusion.1 = bf16[1024,2048]{1,0:T(8,128)(2,1)} fusion(bf16[1024,640]{0,1:T(8,128)(2,1)} %get-tuple-element.56, bf16[2048,1920]{1,0:T(8,128)(2,1)} %all-gather.4.cloned.1.call-done), kind=kOutput, calls=%fused_computation.23 | convolution fusion | flops 2686451712 | bytes 8126464 | tf_op jit(solution)/shard_map/dot_general | solution.py:44
  295.2 7.4 %convolution_convert_fusion = bf16[2048,1280]{1,0:T(8,128)(2,1)} fusion(bf16[1024,2048]{1,0:T(8,128)(2,1)S(1)} %bitcast.255, bf16[1024,1280]{0,1:T(8,128)(2,1)S(1)} %copy-done.24), kind=kOutput, calls=%fused_computation.5 | convolution fusion | flops 5371330560 | bytes 12058624 | tf_op jit(solution)/shard_map/dot_general | solution.py:485
  302.6 10.6 %all-to-all-done.3 = bf16[4,128,2048]{2,1,0:T(8,128)(2,1)} async-done(((bf16[4,128,2048]{2,1,0:T(8,128)(2,1)}), bf16[4,128,2048]{2,1,0:T(8,128)(2,1)}, u32[]{:S(2)}, u32[]{:S(2)}) %all-to-all-start.3) | async-done | bytes 2097184 | tf_op jit(solution)/shard_map/all_to_all | solution.py:374
  317.9 2.5 fusion.94
  320.4 3.7 convolution_convert_fusion.11
  324.9 4.1 all-to-all-start.4
  336.2 3.7 fusion.8
  339.9 4.7 all-to-all-done.4
  344.6 4.5 all-to-all-start.5
  349.6 9.8 %collective-permute-done.27 = bf16[2,512,512]{2,1,0:T(8,128)(2,1)} collective-permute-done((bf16[2,512,512]{2,1,0:T(8,128)(2,1)}, bf16[2,512,512]{2,1,0:T(8,128)(2,1)}, u32[]{:S(2)}, u32[]{:S(2)}) %collective-permute-start.27) | collective-permute-done | bytes 1048608 | tf_op jit(solution)/shard_map/ppermute | solution.py:330
  359.4 13.8 %collective-permute-done.28 = bf16[2,512,512]{2,1,0:T(8,128)(2,1)} collective-permute-done((bf16[2,512,512]{2,1,0:T(8,128)(2,1)}, bf16[2,512,512]{2,1,0:T(8,128)(2,1)}, u32[]{:S(2)}, u32[]{:S(2)}) %collective-permute-start.28) | collective-permute-done | bytes 1048608 | tf_op jit(solution)/shard_map/ppermute | solution.py:330
  373.2 17.9 %attend_back.1 = (bf16[1024,768]{1,0:T(8,128)(2,1)}, f32[2,2,1024]{2,1,0:T(2,128)}, f32[2,2,512]{2,1,0:T(2,128)}) custom-call(s32[1]{0:T(128)} %bitcast.here_ref, bf16[1024,768]{1,0:T(8,128)(2,1)} %convolution_convert_fusion.4.q_in.k_in.v_in, bf16[1024,768]{1,0:T(8,128)(2,1)} %convolution_convert_fusion.4.q_in.k_in.v_in, ...), custom_call_target="tpu_custom_call" | custom-call | flops 10737418240 | bytes 2097152 | tf_op jit(solution)/shard_map/attend_back/pallas_call | solution.py:270
  391.1 5.8 %convolution_convert_fusion.2 = bf16[1024,2048]{1,0:T(8,128)(2,1)S(1)} fusion(bf16[1024,768]{1,0:T(8,128)(2,1)} %get-tuple-element.66, bf16[2048,768]{1,0:T(8,128)(2,1)} %bitcast.259), kind=kOutput, calls=%fused_computation.24 | convolution fusion | flops 3223322624 | bytes 8912896 | tf_op jit(solution)/shard_map/dot_general | solution.py:44
  397.0 2.3 fusion.93
  399.3 2.2 fusion.39
  402.0 2.1 fusion.38
  407.3 8.9 %collective-permute-done.40 = bf16[512,512]{1,0:T(8,128)(2,1)} collective-permute-done((bf16[512,512]{1,0:T(8,128)(2,1)}, bf16[512,512]{1,0:T(8,128)(2,1)}, u32[]{:S(2)}, u32[]{:S(2)}) %collective-permute-start.40) | collective-permute-done | bytes 524320 | tf_op jit(solution)/shard_map/ppermute | solution.py:330
  416.1 2.4 collective-permute-done.41
  418.5 3.5 fusion.37
  422.1 3.7 fusion.7
  425.7 5.2 all-to-all-start.6
  430.9 2.9 convolution_convert_fusion.8
  441.2 13.2 %collective-permute-done.44 = bf16[2,512,384]{2,1,0:T(8,128)(2,1)S(1)} collective-permute-done((bf16[2,512,384]{2,1,0:T(8,128)(2,1)S(1)}, bf16[2,512,384]{2,1,0:T(8,128)(2,1)S(1)}, u32[]{:S(2)}, u32[]{:S(2)}) %collective-permute-start.44) | collective-permute-done | bytes 786464 | tf_op jit(solution)/shard_map/ppermute | solution.py:330
  455.1 3.2 collective-permute-done.42
  460.4 4.9 collective-permute-done.45
  474.1 15.5 %all-to-all-done.6 = bf16[4,128,2048]{2,1,0:T(8,128)(2,1)} async-done(((bf16[4,128,2048]{2,1,0:T(8,128)(2,1)}), bf16[4,128,2048]{2,1,0:T(8,128)(2,1)}, u32[]{:S(2)}, u32[]{:S(2)}) %all-to-all-start.6) | async-done | bytes 2097184 | tf_op jit(solution)/shard_map/all_to_all | solution.py:374
  491.7 4.4 all-to-all-start.7
  496.1 2.4 collective-permute-start.32
  502.3 7.4 %collective-permute-done.32 = bf16[128,1920]{1,0:T(8,128)(2,1)S(1)} collective-permute-done((bf16[128,1920]{1,0:T(8,128)(2,1)}, bf16[128,1920]{1,0:T(8,128)(2,1)S(1)}, u32[]{:S(2)}, u32[]{:S(2)}) %collective-permute-start.32) | collective-permute-done | bytes 491552 | tf_op jit(solution)/shard_map/ppermute | solution.py:301
  516.5 3.4 collective-permute-start.36
  521.4 2.5 collective-permute-done.35
  525.5 3.5 collective-permute-start.39
  530.3 2.9 convert_bitcast_fusion
  (421 shorter events, 143.2 us)
Async XLA Ops:
  7.2 74.8 %all-gather.6.cloned.1.call-start = ((), (), s32[]{:S(2)}) async-start(), calls=%async_computation.13 | async-start | bytes 2621440 | tf_op jit(solution)/shard_map/all_gather | solution.py:518
  8.7 21.5 %collective-permute-start.3 = (bf16[1,512]{1,0:T(2,128)(2,1)S(1)}, bf16[1,512]{1,0:T(2,128)(2,1)S(1)}, u32[]{:S(2)}, u32[]{:S(2)}) collective-permute-start(bf16[1,512]{1,0:T(2,128)(2,1)S(1)} %reshape.301), channel_id=1, source_target_pairs={{0,6},{2,0},{4,2},{6,4},{1,7},{3,1},{5,3},{7,5},{8,14},{10,8},{12,... | collective-permute-start | bytes 3080 | tf_op jit(solution)/shard_map/ppermute | solution.py:301
  13.8 16.4 %collective-permute-start.2 = (bf16[1,512]{1,0:T(2,128)(2,1)S(1)}, bf16[1,512]{1,0:T(2,128)(2,1)S(1)}, u32[]{:S(2)}, u32[]{:S(2)}) collective-permute-start(bf16[1,512]{1,0:T(2,128)(2,1)S(1)} %reshape.301), channel_id=1, source_target_pairs={{0,4},{2,6},{4,0},{6,2},{1,5},{3,7},{5,1},{7,3},{8,12},{10,14},{12... | collective-permute-start | bytes 3080 | tf_op jit(solution)/shard_map/ppermute | solution.py:301
  13.8 16.3 %collective-permute-start.1 = (bf16[1,512]{1,0:T(2,128)(2,1)S(1)}, bf16[1,512]{1,0:T(2,128)(2,1)S(1)}, u32[]{:S(2)}, u32[]{:S(2)}) collective-permute-start(bf16[1,512]{1,0:T(2,128)(2,1)S(1)} %reshape.301), channel_id=1, source_target_pairs={{0,2},{2,4},{4,6},{6,0},{1,3},{3,5},{5,7},{7,1},{8,10},{10,12},{12... | collective-permute-start | bytes 3080 | tf_op jit(solution)/shard_map/ppermute | solution.py:301
  32.5 15.4 %collective-permute-start.4 = (bf16[128,1920]{1,0:T(8,128)(2,1)}, bf16[128,1920]{1,0:T(8,128)(2,1)}, u32[]{:S(2)}, u32[]{:S(2)}) collective-permute-start(bf16[128,1920]{1,0:T(8,128)(2,1)} %pad_maximum_fusion.12), channel_id=1, source_target_pairs={{0,8},{8,16},{16,24},{24,0},{1,9},{9,17},{17,25},{25,1},{2,10},{10... | collective-permute-start | bytes 1474568 | tf_op jit(solution)/shard_map/ppermute | solution.py:301
  34.0 66.2 %all-to-all-start = ((bf16[4,128,1792]{2,1,0:T(8,128)(2,1)}), bf16[4,128,1792]{2,1,0:T(8,128)(2,1)S(1)}, u32[]{:S(2)}, u32[]{:S(2)}) async-start(bf16[4,128,1792]{2,1,0:T(8,128)(2,1)} %pad_maximum_fusion.5), calls=%async_computation | async-start | bytes 3670016 | tf_op jit(solution)/shard_map/all_to_all | solution.py:374
  38.1 205.7 %all-gather.4.cloned.1.call-start = ((), (), s32[]{:S(2)}) async-start(), calls=%async_computation.10 | async-start | bytes 9830400 | tf_op jit(solution)/shard_map/all_gather | solution.py:545
  38.9 17.5 %collective-permute-start.5 = (bf16[128,1920]{1,0:T(8,128)(2,1)}, bf16[128,1920]{1,0:T(8,128)(2,1)}, u32[]{:S(2)}, u32[]{:S(2)}) collective-permute-start(bf16[128,1920]{1,0:T(8,128)(2,1)} %pad_maximum_fusion.13), channel_id=1, source_target_pairs={{0,16},{8,24},{16,0},{24,8},{1,17},{9,25},{17,1},{25,9},{2,18},{10... | collective-permute-start | bytes 1474568 | tf_op jit(solution)/shard_map/ppermute | solution.py:301
  41.3 15.1 %collective-permute-start.6 = (bf16[128,1920]{1,0:T(8,128)(2,1)}, bf16[128,1920]{1,0:T(8,128)(2,1)S(1)}, u32[]{:S(2)}, u32[]{:S(2)}) collective-permute-start(bf16[128,1920]{1,0:T(8,128)(2,1)} %pad_maximum_fusion.14), channel_id=1, source_target_pairs={{0,24},{8,0},{16,8},{24,16},{1,25},{9,1},{17,9},{25,17},{2,26},{10... | collective-permute-start | bytes 1474568 | tf_op jit(solution)/shard_map/ppermute | solution.py:301
  44.0 27.0 %copy-start.46 = (s32[1,1,4,256]{3,1,2,0:T(1,128)}, s32[1,1,4,256]{3,1,2,0:T(1,128)S(1)}, u32[]{:S(2)}) copy-start(s32[1,1,4,256]{3,1,2,0:T(1,128)S(1)} %copy.170) | copy-start | bytes 12292
  56.4 47.7 %collective-permute-start.15 = (bf16[4,256]{1,0:T(4,128)(2,1)S(1)}, bf16[4,256]{1,0:T(4,128)(2,1)S(1)}, u32[]{:S(2)}, u32[]{:S(2)}) collective-permute-start(bf16[4,256]{1,0:T(4,128)(2,1)S(1)} %slice.423), channel_id=1, source_target_pairs={{0,16},{8,24},{16,0},{24,8},{1,17},{9,25},{17,1},{25,9},{2,18},{10... | collective-permute-start | bytes 6152 | tf_op jit(solution)/shard_map/ppermute | solution.py:301
  58.0 14.9 %collective-permute-start.14 = (bf16[4,256]{1,0:T(4,128)(2,1)S(1)}, bf16[4,256]{1,0:T(4,128)(2,1)S(1)}, u32[]{:S(2)}, u32[]{:S(2)}) collective-permute-start(bf16[4,256]{1,0:T(4,128)(2,1)S(1)} %slice.423), channel_id=1, source_target_pairs={{0,8},{8,16},{16,24},{24,0},{1,9},{9,17},{17,25},{25,1},{2,10},{10... | collective-permute-start | bytes 6152 | tf_op jit(solution)/shard_map/ppermute | solution.py:301
  63.9 18.2 %collective-permute-start.9 = (bf16[128,2048]{1,0:T(8,128)(2,1)}, bf16[128,2048]{1,0:T(8,128)(2,1)S(1)}, u32[]{:S(2)}, u32[]{:S(2)}) collective-permute-start(bf16[128,2048]{1,0:T(8,128)(2,1)} %constant_dynamic-update-slice_fusion), channel_id=1, source_target_pairs={{0,24},{8,0},{16,8},{24,16},{1,25},{9,1},{17,9},{25,17},{2,26},{10... | collective-permute-start | bytes 1572872 | tf_op jit(solution)/shard_map/ppermute | solution.py:301
  64.7 29.4 %collective-permute-start.8 = (bf16[128,2048]{1,0:T(8,128)(2,1)}, bf16[128,2048]{1,0:T(8,128)(2,1)S(1)}, u32[]{:S(2)}, u32[]{:S(2)}) collective-permute-start(bf16[128,2048]{1,0:T(8,128)(2,1)} %constant_dynamic-update-slice_fusion), channel_id=1, source_target_pairs={{0,16},{8,24},{16,0},{24,8},{1,17},{9,25},{17,1},{25,9},{2,18},{10... | collective-permute-start | bytes 1572872 | tf_op jit(solution)/shard_map/ppermute | solution.py:301
  65.4 28.7 %collective-permute-start.7 = (bf16[128,2048]{1,0:T(8,128)(2,1)}, bf16[128,2048]{1,0:T(8,128)(2,1)S(1)}, u32[]{:S(2)}, u32[]{:S(2)}) collective-permute-start(bf16[128,2048]{1,0:T(8,128)(2,1)} %constant_dynamic-update-slice_fusion), channel_id=1, source_target_pairs={{0,8},{8,16},{16,24},{24,0},{1,9},{9,17},{17,25},{25,1},{2,10},{10... | collective-permute-start | bytes 1572872 | tf_op jit(solution)/shard_map/ppermute | solution.py:301
  82.1 49.9 %collective-permute-start = (bf16[4,128,2048]{2,1,0:T(8,128)(2,1)}, bf16[4,128,2048]{2,1,0:T(8,128)(2,1)}, u32[]{:S(2)}, u32[]{:S(2)}) collective-permute-start(bf16[4,128,2048]{2,1,0:T(8,128)(2,1)} %bitcast.265), channel_id=1, source_target_pairs={{0,1},{1,0},{2,3},{3,2},{4,5},{5,4},{6,7},{7,6},{8,9},{9,8},{10,11... | collective-permute-start | bytes 6291464 | tf_op jit(solution)/shard_map/ppermute | solution.py:301
  82.1 18.1 %copy-start.35 = (bf16[128,2048]{1,0:T(8,128)(2,1)}, bf16[128,2048]{1,0:T(8,128)(2,1)S(1)}, u32[]{:S(2)}) copy-start(bf16[128,2048]{1,0:T(8,128)(2,1)S(1)} %collective-permute-done.9) | copy-start | bytes 1572868
  82.1 22.0 %collective-permute-start.16 = (bf16[4,256]{1,0:T(4,128)(2,1)S(1)}, bf16[4,256]{1,0:T(4,128)(2,1)S(1)}, u32[]{:S(2)}, u32[]{:S(2)}) collective-permute-start(bf16[4,256]{1,0:T(4,128)(2,1)S(1)} %slice.423), channel_id=1, source_target_pairs={{0,24},{8,0},{16,8},{24,16},{1,25},{9,1},{17,9},{25,17},{2,26},{10... | collective-permute-start | bytes 6152 | tf_op jit(solution)/shard_map/ppermute | solution.py:301
  101.2 19.4 %collective-permute-start.10 = (bf16[512,768]{1,0:T(8,128)(2,1)}, bf16[512,768]{1,0:T(8,128)(2,1)S(1)}, u32[]{:S(2)}, u32[]{:S(2)}) collective-permute-start(bf16[512,768]{1,0:T(8,128)(2,1)} %slice.420), channel_id=1, source_target_pairs={{0,8},{8,0},{16,24},{24,16},{1,9},{9,1},{17,25},{25,17},{2,10},{10... | collective-permute-start | bytes 2359304 | tf_op jit(solution)/shard_map/ppermute | solution.py:330
  102.6 19.5 %collective-permute-start.11 = (bf16[512,768]{1,0:T(8,128)(2,1)}, bf16[512,768]{1,0:T(8,128)(2,1)S(1)}, u32[]{:S(2)}, u32[]{:S(2)}) collective-permute-start(bf16[512,768]{1,0:T(8,128)(2,1)} %slice.420), channel_id=1, source_target_pairs={{0,16},{8,24},{16,0},{24,8},{1,17},{9,25},{17,1},{25,9},{2,18},{10... | collective-permute-start | bytes 2359304 | tf_op jit(solution)/shard_map/ppermute | solution.py:330
  104.2 31.8 %copy-start.44 = (f32[1,4,4,128]{3,0,2,1:T(1,128)}, f32[1,4,4,128]{3,0,2,1:T(1,128)S(1)}, u32[]{:S(2)}) copy-start(f32[1,4,4,128]{3,0,2,1:T(1,128)S(1)} %get-tuple-element.181) | copy-start | bytes 24580
  120.6 10.0 %collective-permute-start.12 = (bf16[256,768]{1,0:T(8,128)(2,1)S(1)}, bf16[256,768]{1,0:T(8,128)(2,1)S(1)}, u32[]{:S(2)}, u32[]{:S(2)}) collective-permute-start(bf16[256,768]{1,0:T(8,128)(2,1)S(1)} %slice.532), channel_id=1, source_target_pairs={{0,16},{8,24},{16,0},{24,8},{1,17},{9,25},{17,1},{25,9},{2,18},{10... | collective-permute-start | bytes 1179656 | tf_op jit(solution)/shard_map/ppermute | solution.py:330
  122.2 9.7 %collective-permute-start.13 = (bf16[256,768]{1,0:T(8,128)(2,1)S(1)}, bf16[256,768]{1,0:T(8,128)(2,1)S(1)}, u32[]{:S(2)}, u32[]{:S(2)}) collective-permute-start(bf16[256,768]{1,0:T(8,128)(2,1)S(1)} %slice.533), channel_id=1, source_target_pairs={{0,8},{8,0},{16,24},{24,16},{1,9},{9,1},{17,25},{25,17},{2,10},{10... | collective-permute-start | bytes 1179656 | tf_op jit(solution)/shard_map/ppermute | solution.py:330
  142.6 28.2 %collective-permute-start.17 = (bf16[512,1024]{1,0:T(8,128)(2,1)}, bf16[512,1024]{1,0:T(8,128)(2,1)S(1)}, u32[]{:S(2)}, u32[]{:S(2)}) collective-permute-start(bf16[512,1024]{1,0:T(8,128)(2,1)} %slice.428), channel_id=1, source_target_pairs={{0,8},{8,0},{16,24},{24,16},{1,9},{9,1},{17,25},{25,17},{2,10},{10... | collective-permute-start | bytes 3145736 | tf_op jit(solution)/shard_map/ppermute | solution.py:330
  144.3 28.3 %collective-permute-start.18 = (bf16[512,1024]{1,0:T(8,128)(2,1)}, bf16[512,1024]{1,0:T(8,128)(2,1)}, u32[]{:S(2)}, u32[]{:S(2)}) collective-permute-start(bf16[512,1024]{1,0:T(8,128)(2,1)} %slice.428), channel_id=1, source_target_pairs={{0,16},{8,24},{16,0},{24,8},{1,17},{9,25},{17,1},{25,9},{2,18},{10... | collective-permute-start | bytes 3145736 | tf_op jit(solution)/shard_map/ppermute | solution.py:330
  161.8 33.7 %all-to-all-start.1 = ((bf16[4,256,256]{1,2,0:T(8,128)(2,1)}), bf16[4,256,256]{1,2,0:T(8,128)(2,1)S(1)}, u32[]{:S(2)}, u32[]{:S(2)}) async-start(bf16[4,256,256]{1,2,0:T(8,128)(2,1)} %copy.142), calls=%async_computation.1 | async-start | bytes 1048576 | tf_op jit(solution)/shard_map/all_to_all | solution.py:374
  165.3 184.3 %reduce-scatter.3.cloned.1.call-start = ((), (), s32[]{:S(2)}) async-start(), calls=%async_computation.11 | async-start | bytes 3276800 | tf_op jit(solution)/shard_map/reduce_scatter | solution.py:590
  170.9 11.4 %collective-permute-start.19 = (bf16[256,1024]{1,0:T(8,128)(2,1)S(1)}, bf16[256,1024]{1,0:T(8,128)(2,1)S(1)}, u32[]{:S(2)}, u32[]{:S(2)}) collective-permute-start(bf16[256,1024]{1,0:T(8,128)(2,1)S(1)} %slice.536), channel_id=1, source_target_pairs={{0,16},{8,24},{16,0},{24,8},{1,17},{9,25},{17,1},{25,9},{2,18},{10... | collective-permute-start | bytes 1572872 | tf_op jit(solution)/shard_map/ppermute | solution.py:330
  173.7 11.0 %collective-permute-start.20 = (bf16[256,1024]{1,0:T(8,128)(2,1)S(1)}, bf16[256,1024]{1,0:T(8,128)(2,1)S(1)}, u32[]{:S(2)}, u32[]{:S(2)}) collective-permute-start(bf16[256,1024]{1,0:T(8,128)(2,1)S(1)} %slice.537), channel_id=1, source_target_pairs={{0,8},{8,0},{16,24},{24,16},{1,9},{9,1},{17,25},{25,17},{2,10},{10... | collective-permute-start | bytes 1572872 | tf_op jit(solution)/shard_map/ppermute | solution.py:330
  199.3 2.0 collective-permute-start.21
  199.5 4.8 collective-permute-start.22
  235.2 4.2 collective-permute-start.23
  267.4 11.3 %collective-permute-start.24 = (bf16[4,128,2048]{2,1,0:T(8,128)(2,1)}, bf16[4,128,2048]{2,1,0:T(8,128)(2,1)}, u32[]{:S(2)}, u32[]{:S(2)}) collective-permute-start(bf16[4,128,2048]{2,1,0:T(8,128)(2,1)} %bitcast.45), channel_id=1, source_target_pairs={{0,1},{1,0},{2,3},{3,2},{4,5},{5,4},{6,7},{7,6},{8,9},{9,8},{10,11... | collective-permute-start | bytes 6291464 | tf_op jit(solution)/shard_map/ppermute | solution.py:301
  283.0 30.3 %all-to-all-start.3 = ((bf16[4,128,2048]{2,1,0:T(8,128)(2,1)}), bf16[4,128,2048]{2,1,0:T(8,128)(2,1)}, u32[]{:S(2)}, u32[]{:S(2)}) async-start(bf16[4,128,2048]{2,1,0:T(8,128)(2,1)} %fusion.9), calls=%async_computation.3 | async-start | bytes 4194304 | tf_op jit(solution)/shard_map/all_to_all | solution.py:374
  316.8 3.6 collective-permute-start.25
  320.4 15.8 %collective-permute-start.26 = (bf16[4,128,2048]{2,1,0:T(8,128)(2,1)}, bf16[4,128,2048]{2,1,0:T(8,128)(2,1)}, u32[]{:S(2)}, u32[]{:S(2)}) collective-permute-start(bf16[4,128,2048]{2,1,0:T(8,128)(2,1)} %bitcast.47), channel_id=1, source_target_pairs={{0,1},{1,0},{2,3},{3,2},{4,5},{5,4},{6,7},{7,6},{8,9},{9,8},{10,11... | collective-permute-start | bytes 6291464 | tf_op jit(solution)/shard_map/ppermute | solution.py:301
  324.9 19.6 %all-to-all-start.4 = ((bf16[4,256,256]{2,1,0:T(8,128)(2,1)}), bf16[4,256,256]{2,1,0:T(8,128)(2,1)}, u32[]{:S(2)}, u32[]{:S(2)}) async-start(bf16[4,256,256]{2,1,0:T(8,128)(2,1)} %bitcast.264), calls=%async_computation.4 | async-start | bytes 1048576 | tf_op jit(solution)/shard_map/all_to_all | solution.py:374
  333.1 26.3 %collective-permute-start.27 = (bf16[2,512,512]{2,1,0:T(8,128)(2,1)}, bf16[2,512,512]{2,1,0:T(8,128)(2,1)}, u32[]{:S(2)}, u32[]{:S(2)}) collective-permute-start(bf16[2,512,512]{2,1,0:T(8,128)(2,1)} %pad_maximum_fusion.8), channel_id=1, source_target_pairs={{0,8},{8,0},{16,24},{24,16},{1,9},{9,1},{17,25},{25,17},{2,10},{10... | collective-permute-start | bytes 3145736 | tf_op jit(solution)/shard_map/ppermute | solution.py:330
  335.6 37.5 %collective-permute-start.28 = (bf16[2,512,512]{2,1,0:T(8,128)(2,1)}, bf16[2,512,512]{2,1,0:T(8,128)(2,1)}, u32[]{:S(2)}, u32[]{:S(2)}) collective-permute-start(bf16[2,512,512]{2,1,0:T(8,128)(2,1)} %pad_maximum_fusion.9), channel_id=1, source_target_pairs={{0,16},{8,24},{16,0},{24,8},{1,17},{9,25},{17,1},{25,9},{2,18},{10... | collective-permute-start | bytes 3145736 | tf_op jit(solution)/shard_map/ppermute | solution.py:330
  344.6 46.6 %all-to-all-start.5 = ((bf16[4,128,2048]{2,1,0:T(8,128)(2,1)}), bf16[4,128,2048]{2,1,0:T(8,128)(2,1)}, u32[]{:S(2)}, u32[]{:S(2)}) async-start(bf16[4,128,2048]{2,1,0:T(8,128)(2,1)} %fusion.8), calls=%async_computation.5 | async-start | bytes 4194304 | tf_op jit(solution)/shard_map/all_to_all | solution.py:374
  349.0 118.4 %reduce-scatter.5.cloned.1.call-start = ((), (), s32[]{:S(2)}) async-start(), calls=%async_computation.12 | async-start | bytes 6553600 | tf_op jit(solution)/shard_map/reduce_scatter | solution.py:592
  399.2 22.8 %collective-permute-start.29 = (bf16[4,128,2048]{2,1,0:T(8,128)(2,1)}, bf16[4,128,2048]{2,1,0:T(8,128)(2,1)}, u32[]{:S(2)}, u32[]{:S(2)}) collective-permute-start(bf16[4,128,2048]{2,1,0:T(8,128)(2,1)} %bitcast.56), channel_id=1, source_target_pairs={{0,1},{1,0},{2,3},{3,2},{4,5},{5,4},{6,7},{7,6},{8,9},{9,8},{10,11... | collective-permute-start | bytes 6291464 | tf_op jit(solution)/shard_map/ppermute | solution.py:301
  401.4 14.7 %collective-permute-start.40 = (bf16[512,512]{1,0:T(8,128)(2,1)}, bf16[512,512]{1,0:T(8,128)(2,1)}, u32[]{:S(2)}, u32[]{:S(2)}) collective-permute-start(bf16[512,512]{1,0:T(8,128)(2,1)} %fusion.39), channel_id=1, source_target_pairs={{0,16},{8,24},{16,0},{24,8},{1,17},{9,25},{17,1},{25,9},{2,18},{10... | collective-permute-start | bytes 1572872 | tf_op jit(solution)/shard_map/ppermute | solution.py:330
  404.1 14.4 %collective-permute-start.41 = (bf16[512,512]{1,0:T(8,128)(2,1)}, bf16[512,512]{1,0:T(8,128)(2,1)}, u32[]{:S(2)}, u32[]{:S(2)}) collective-permute-start(bf16[512,512]{1,0:T(8,128)(2,1)} %fusion.38), channel_id=1, source_target_pairs={{0,8},{8,0},{16,24},{24,16},{1,9},{9,1},{17,25},{25,17},{2,10},{10... | collective-permute-start | bytes 1572872 | tf_op jit(solution)/shard_map/ppermute | solution.py:330
  407.3 14.8 %copy-start.2 = (bf16[512,2048]{1,0:T(8,128)(2,1)S(1)}, bf16[512,2048]{1,0:T(8,128)(2,1)}, u32[]{:S(2)}) copy-start(bf16[512,2048]{1,0:T(8,128)(2,1)} %get-tuple-element.140) | copy-start | bytes 6291460
  425.7 63.9 %all-to-all-start.6 = ((bf16[4,128,2048]{2,1,0:T(8,128)(2,1)}), bf16[4,128,2048]{2,1,0:T(8,128)(2,1)}, u32[]{:S(2)}, u32[]{:S(2)}) async-start(bf16[4,128,2048]{2,1,0:T(8,128)(2,1)} %fusion.7), calls=%async_computation.7 | async-start | bytes 4194304 | tf_op jit(solution)/shard_map/all_to_all | solution.py:374
  435.7 18.7 %collective-permute-start.44 = (bf16[2,512,384]{2,1,0:T(8,128)(2,1)S(1)}, bf16[2,512,384]{2,1,0:T(8,128)(2,1)S(1)}, u32[]{:S(2)}, u32[]{:S(2)}) collective-permute-start(bf16[2,512,384]{2,1,0:T(8,128)(2,1)S(1)} %pad_maximum_fusion.11), channel_id=1, source_target_pairs={{0,16},{8,24},{16,0},{24,8},{1,17},{9,25},{17,1},{25,9},{2,18},{10... | collective-permute-start | bytes 2359304 | tf_op jit(solution)/shard_map/ppermute | solution.py:330
  438.5 19.8 %collective-permute-start.42 = (bf16[2,512,384]{2,1,0:T(8,128)(2,1)S(1)}, bf16[2,512,384]{2,1,0:T(8,128)(2,1)S(1)}, u32[]{:S(2)}, u32[]{:S(2)}) collective-permute-start(bf16[2,512,384]{2,1,0:T(8,128)(2,1)S(1)} %pad_maximum_fusion.10), channel_id=1, source_target_pairs={{0,8},{8,0},{16,24},{24,16},{1,9},{9,1},{17,25},{25,17},{2,10},{10... | collective-permute-start | bytes 2359304 | tf_op jit(solution)/shard_map/ppermute | solution.py:330
  454.5 10.9 %collective-permute-start.45 = (bf16[512,384]{1,0:T(8,128)(2,1)S(1)}, bf16[512,384]{1,0:T(8,128)(2,1)S(1)}, u32[]{:S(2)}, u32[]{:S(2)}) collective-permute-start(bf16[512,384]{1,0:T(8,128)(2,1)S(1)} %fusion.49), channel_id=1, source_target_pairs={{0,8},{8,0},{16,24},{24,16},{1,9},{9,1},{17,25},{25,17},{2,10},{10... | collective-permute-start | bytes 1179656 | tf_op jit(solution)/shard_map/ppermute | solution.py:330
  458.4 7.8 %collective-permute-start.43 = (bf16[512,384]{1,0:T(8,128)(2,1)S(1)}, bf16[512,384]{1,0:T(8,128)(2,1)S(1)}, u32[]{:S(2)}, u32[]{:S(2)}) collective-permute-start(bf16[512,384]{1,0:T(8,128)(2,1)S(1)} %fusion.50), channel_id=1, source_target_pairs={{0,16},{8,24},{16,0},{24,8},{1,17},{9,25},{17,1},{25,9},{2,18},{10... | collective-permute-start | bytes 1179656 | tf_op jit(solution)/shard_map/ppermute | solution.py:330
  471.5 27.1 %collective-permute-start.30 = (bf16[128,1920]{1,0:T(8,128)(2,1)}, bf16[128,1920]{1,0:T(8,128)(2,1)}, u32[]{:S(2)}, u32[]{:S(2)}) collective-permute-start(bf16[128,1920]{1,0:T(8,128)(2,1)} %get-tuple-element.152), channel_id=1, source_target_pairs={{0,8},{8,16},{16,24},{24,0},{1,9},{9,17},{17,25},{25,1},{2,10},{10... | collective-permute-start | bytes 1474568 | tf_op jit(solution)/shard_map/ppermute | solution.py:301
  473.7 26.8 %collective-permute-start.31 = (bf16[128,1920]{1,0:T(8,128)(2,1)}, bf16[128,1920]{1,0:T(8,128)(2,1)}, u32[]{:S(2)}, u32[]{:S(2)}) collective-permute-start(bf16[128,1920]{1,0:T(8,128)(2,1)} %get-tuple-element.151), channel_id=1, source_target_pairs={{0,16},{8,24},{16,0},{24,8},{1,17},{9,25},{17,1},{25,9},{2,18},{10... | collective-permute-start | bytes 1474568 | tf_op jit(solution)/shard_map/ppermute | solution.py:301
  491.7 18.8 %copy-start.45 = (f32[1,4,4,128]{3,0,2,1:T(1,128)S(1)}, f32[1,4,4,128]{3,0,2,1:T(1,128)}, u32[]{:S(2)}) copy-start(f32[1,4,4,128]{3,0,2,1:T(1,128)} %copy-done.44) | copy-start | bytes 24580
  491.7 53.2 %all-to-all-start.7 = ((bf16[4,128,1792]{2,1,0:T(8,128)(2,1)}), bf16[4,128,1792]{2,1,0:T(8,128)(2,1)}, u32[]{:S(2)}, u32[]{:S(2)}) async-start(bf16[4,128,1792]{2,1,0:T(8,128)(2,1)} %pad_maximum_fusion.6), calls=%async_computation.9 | async-start | bytes 3670016 | tf_op jit(solution)/shard_map/all_to_all | solution.py:374
  496.1 14.4 %copy-start.6 = (bf16[128,2048]{1,0:T(8,128)(2,1)S(1)}, bf16[128,2048]{1,0:T(8,128)(2,1)}, u32[]{:S(2)}) copy-start(bf16[128,2048]{1,0:T(8,128)(2,1)} %param.13) | copy-start | bytes 1572868
  496.1 14.8 %copy-start.15 = (bf16[128,2048]{1,0:T(8,128)(2,1)S(1)}, bf16[128,2048]{1,0:T(8,128)(2,1)}, u32[]{:S(2)}) copy-start(bf16[128,2048]{1,0:T(8,128)(2,1)} %param.25) | copy-start | bytes 1572868
  496.1 13.5 %collective-permute-start.32 = (bf16[128,1920]{1,0:T(8,128)(2,1)}, bf16[128,1920]{1,0:T(8,128)(2,1)S(1)}, u32[]{:S(2)}, u32[]{:S(2)}) collective-permute-start(bf16[128,1920]{1,0:T(8,128)(2,1)} %get-tuple-element.150), channel_id=1, source_target_pairs={{0,24},{8,0},{16,8},{24,16},{1,25},{9,1},{17,9},{25,17},{2,26},{10... | collective-permute-start | bytes 1474568 | tf_op jit(solution)/shard_map/ppermute | solution.py:301
  515.0 1.2 collective-permute-start.33
  516.5 4.9 collective-permute-start.36
  519.8 4.1 collective-permute-start.35
  520.4 4.7 collective-permute-start.34
  525.5 14.4 %collective-permute-start.39 = (f32[41,128]{1,0:T(8,128)S(1)}, f32[41,128]{1,0:T(8,128)S(1)}, u32[]{:S(2)}, u32[]{:S(2)}) collective-permute-start(f32[41,128]{1,0:T(8,128)S(1)} %reduce_sum.197), channel_id=1, source_target_pairs={{0,6},{2,0},{4,2},{6,4},{1,7},{3,1},{5,3},{7,5},{8,14},{10,8},{12,... | collective-permute-start | bytes 62984 | tf_op jit(solution)/shard_map/ppermute | solution.py:301
  529.0 12.3 %collective-permute-start.38 = (f32[41,128]{1,0:T(8,128)S(1)}, f32[41,128]{1,0:T(8,128)S(1)}, u32[]{:S(2)}, u32[]{:S(2)}) collective-permute-start(f32[41,128]{1,0:T(8,128)S(1)} %reduce_sum.197), channel_id=1, source_target_pairs={{0,4},{2,6},{4,0},{6,2},{1,5},{3,7},{5,1},{7,3},{8,12},{10,14},{12... | collective-permute-start | bytes 62984 | tf_op jit(solution)/shard_map/ppermute | solution.py:301
  529.0 12.3 %collective-permute-start.37 = (f32[41,128]{1,0:T(8,128)S(1)}, f32[41,128]{1,0:T(8,128)S(1)}, u32[]{:S(2)}, u32[]{:S(2)}) collective-permute-start(f32[41,128]{1,0:T(8,128)S(1)} %reduce_sum.197), channel_id=1, source_target_pairs={{0,2},{2,4},{4,6},{6,0},{1,3},{3,5},{5,7},{7,1},{8,10},{10,12},{12... | collective-permute-start | bytes 62984 | tf_op jit(solution)/shard_map/ppermute | solution.py:301
  (45 other events, 218.0 us)
Sparse Core Ops, SparseCore 0:
  15.0 67.0 all-gather.5
  83.6 160.1 all-gather.3
  275.3 50.3 reduce-scatter.2
  351.8 109.1 reduce-scatter.4

commit v4 on v3

--- a/solution.py
+++ b/solution.py
@@ -607,7 +607,7 @@
     ff_core = sum_of_cores(ff_part, "dp")
     ff_stack = exchange(tie(ff_core, mixed_grad), "dp")
 
-    mixed_grad = tie(mixed_grad, down_sum, *output_arrived)
+    mixed_grad = tie(mixed_grad, down_sum, output_arrived[1])
     dqkv, diagonals, far_sums = attend_back(
         here, qkv, mixed_grad, segs, vectors, far, lse_rows
     )

time: 564 us -> 550 us (0.975)
  waiting for transfers between devices: 177 us -> 150 us
  local copies, waits for them, and re-layouts: 72.5 us -> 78.5 us
    ppermute x16, waiting for transfers between devices: 87.2 us -> 63.1 us  [flip(): return lax.ppermute(value, 'dp', [(i, i ^ mask) for i in range(size)])]
    unnamed x170 -> x174, local copies, waits for them, and re-layouts: 19 us -> 20.6 us
  transfers between devices with their start and end apart: 57 -> 57, of which waited for: 31 -> 32; matrix products, arithmetic and copies ran while one was open for 31% -> 33% of each run, Pallas kernels for 6% -> 6%
where the time goes in v4:
time: 550 us; the launch traced here: 544 us
  waiting for transfers between devices  150 us (27%)
  starting transfers between devices  96.8 us (18%)
  local copies, waits for them, and re-layouts  78.5 us (14%)
  matrix products  75.1 us (14%)
  other arithmetic  65.7 us (12%)
  Pallas kernels  32.7 us (6%)
  blocking collectives  28.4 us (5%)
  between operations  16.4 us (3%)
    ppermute x16, waiting for transfers between devices, flip(): return lax.ppermute(value, 'dp', [(i, i ^ mask) for i in range(size)])  63.1 us
    ppermute x30, starting transfers between devices, shift(): lax.ppermute(value, axis, [(i, (i + by) % size) for i in range(size)])  46.4 us
    all_to_all x7, waiting for transfers between devices, exchange(): return lax.all_to_all(stack, axis, 0, 0)  46.2 us
    ppermute x30, waiting for transfers between devices, shift(): lax.ppermute(value, axis, [(i, (i + by) % size) for i in range(size)])  29.9 us
    all_to_all x7, starting transfers between devices, exchange(): return lax.all_to_all(stack, axis, 0, 0)  29.7 us
    all_to_all x1, blocking collectives, exchange(): return lax.all_to_all(stack, axis, 0, 0)  28.4 us
    dot_general x10, matrix products, mm_tn(): lax.dot_general(a, b, (((0,), (0,)), ((), ())), preferred_element_type=f32)  25.5 us
    dot_general x4, matrix products, mm(): return jnp.dot(a, b, preferred_element_type=f32)  25.5 us
  transfers between devices with their start and end apart: 57, of which 32 were waited for; matrix products, arithmetic and copies ran while one was open for 33% of the time, Pallas kernels for 6%

profile of v4, /device:TPU:0, one launch (start us, length us, event | category | flops | bytes accessed | tf_op | source)
XLA Modules:
  0.0 544.0 jit_solution(7322106036229561922)
XLA Ops:
  8.7 5.1 collective-permute-start.3
  34.1 4.1 all-to-all-start
  48.0 8.4 %collective-permute-done.5 = bf16[128,1920]{1,0:T(8,128)(2,1)} collective-permute-done((bf16[128,1920]{1,0:T(8,128)(2,1)}, bf16[128,1920]{1,0:T(8,128)(2,1)}, u32[]{:S(2)}, u32[]{:S(2)}) %collective-permute-start.5) | collective-permute-done | bytes 491552 | tf_op jit(solution)/shard_map/ppermute | solution.py:301
  58.0 5.9 %collective-permute-start.14 = (bf16[4,256]{1,0:T(4,128)(2,1)S(1)}, bf16[4,256]{1,0:T(4,128)(2,1)S(1)}, u32[]{:S(2)}, u32[]{:S(2)}) collective-permute-start(bf16[4,256]{1,0:T(4,128)(2,1)S(1)} %slice.423), channel_id=1, source_target_pairs={{0,8},{8,16},{16,24},{24,0},{1,9},{9,17},{17,25},{25,1},{2,10},{10... | collective-permute-start | bytes 6152 | tf_op jit(solution)/shard_map/ppermute | solution.py:301
  72.9 9.1 %all-gather.6.cloned.1.call-done = bf16[512,2048]{1,0:T(8,128)(2,1)} async-done(((bf16[128,2048]{1,0:T(8,128)(2,1)}), bf16[512,2048]{1,0:T(8,128)(2,1)}) %all-gather.6.cloned.1.call-update) | async-done | bytes 2097168 | tf_op jit(solution)/shard_map/all_gather | solution.py:518
  82.1 12.1 %collective-permute-start.16 = (bf16[4,256]{1,0:T(4,128)(2,1)S(1)}, bf16[4,256]{1,0:T(4,128)(2,1)S(1)}, u32[]{:S(2)}, u32[]{:S(2)}) collective-permute-start(bf16[4,256]{1,0:T(4,128)(2,1)S(1)} %slice.423), channel_id=1, source_target_pairs={{0,24},{8,0},{16,8},{24,16},{1,25},{9,1},{17,9},{25,17},{2,26},{10... | collective-permute-start | bytes 6152 | tf_op jit(solution)/shard_map/ppermute | solution.py:301
  94.3 6.0 %all-to-all-done = bf16[4,128,1792]{2,1,0:T(8,128)(2,1)S(1)} async-done(((bf16[4,128,1792]{2,1,0:T(8,128)(2,1)}), bf16[4,128,1792]{2,1,0:T(8,128)(2,1)S(1)}, u32[]{:S(2)}, u32[]{:S(2)}) %all-to-all-start) | async-done | bytes 1835040 | tf_op jit(solution)/shard_map/all_to_all | solution.py:374
  104.5 16.1 %collective-permute-done.10 = bf16[512,768]{1,0:T(8,128)(2,1)S(1)} collective-permute-done((bf16[512,768]{1,0:T(8,128)(2,1)}, bf16[512,768]{1,0:T(8,128)(2,1)S(1)}, u32[]{:S(2)}, u32[]{:S(2)}) %collective-permute-start.10) | collective-permute-done | bytes 786464 | tf_op jit(solution)/shard_map/ppermute | solution.py:330
  123.9 6.7 %collective-permute-done.12 = bf16[256,768]{1,0:T(8,128)(2,1)S(1)} collective-permute-done((bf16[256,768]{1,0:T(8,128)(2,1)S(1)}, bf16[256,768]{1,0:T(8,128)(2,1)S(1)}, u32[]{:S(2)}, u32[]{:S(2)}) %collective-permute-start.12) | collective-permute-done | bytes 393248 | tf_op jit(solution)/shard_map/ppermute | solution.py:330
  132.0 3.1 pad_maximum_fusion
  137.0 4.5 convolution_convert_fusion.4.q_in.k_in.v_in
  144.7 15.1 %attend.1 = (bf16[1024,256]{1,0:T(8,128)(2,1)}, f32[2,2,1024]{2,1,0:T(2,128)}) custom-call(s32[1]{0:T(128)} %bitcast.here_ref, bf16[1024,768]{1,0:T(8,128)(2,1)} %convolution_convert_fusion.4.q_in.k_in.v_in, bf16[1024,768]{1,0:T(8,128)(2,1)} %convolution_convert_fusion.4.q_in.k_in.v_in, bf16[1024,768]{1,0:T(8,128)(2,1)} %convolution_convert_fusion.4.q_in.k_in.v_in, ...), custom_call_target="tpu_custom_call" | custom-call | flops 4294967296 | bytes 1048576 | tf_op jit(solution)/shard_map/attend/pallas_call | solution.py:246
  161.8 3.5 all-to-all-start.1
  166.0 2.6 broadcast_in_dim.196
  175.8 2.3 bitcast_dynamic-update-slice_fusion.1
  178.1 2.3 bitcast_dynamic-update-slice_fusion
  180.4 3.5 collective-permute-done.19
  187.3 8.2 %all-to-all-done.1 = bf16[4,256,256]{1,2,0:T(8,128)(2,1)S(1)} async-done(((bf16[4,256,256]{1,2,0:T(8,128)(2,1)}), bf16[4,256,256]{1,2,0:T(8,128)(2,1)S(1)}, u32[]{:S(2)}, u32[]{:S(2)}) %all-to-all-start.1) | async-done | bytes 524320 | tf_op jit(solution)/shard_map/all_to_all | solution.py:374
  195.5 3.7 fusion.97
  204.3 2.4 pad_maximum_fusion.1
  206.9 28.4 %all_to_all.40 = bf16[4,128,2048]{2,1,0:T(8,128)(2,1)S(1)} all-to-all(bf16[4,128,2048]{2,1,0:T(8,128)(2,1)S(1)} %broadcast_in_dim.211), channel_id=1, replica_groups=mesh['dp'=4,'ctx'=4,'tensor'=2] {'dp'}, dimensions={0} | all-to-all | bytes 4194304 | tf_op jit(solution)/shard_map/all_to_all | solution.py:374
  235.4 4.2 collective-permute-done.23
  239.5 2.4 pad_maximum_fusion.2
  243.8 10.6 %fusion.5 = f32[1024,1280]{0,1:T(8,128)} fusion(bf16[1024,2048]{1,0:T(8,128)(2,1)} %bitcast.254, bf16[2048,1920]{1,0:T(8,128)(2,1)} %all-gather.4.cloned.1.call-done), kind=kOutput, calls=%fused_computation.8 | convolution fusion | flops 5368709120 | bytes 14680064 | tf_op jit(solution)/shard_map/dot_general | solution.py:477
  254.4 6.7 %fusion.19 = (bf16[1024,640]{0,1:T(8,128)(2,1)S(1)}, bf16[1024,640]{0,1:T(8,128)(2,1)S(1)}, bf16[1024,640]{0,1:T(8,128)(2,1)S(1)}) fusion(f32[1024,1280]{0,1:T(8,128)} %fusion.5, bf16[1024,2048]{1,0:T(8,128)(2,1)S(1)} %bitcast.256, bf16[2048,1920]{1,0:T(8,128)(2,1)S(1)} %copy-done.51), kind=kOutput, calls=%fused_computation.34 | convolution fusion | flops 2701393920 | bytes 15990784 | tf_op jit(solution)/shard_map/dot_general | solution.py:477
  261.1 5.9 %fusion.10 = bf16[1024,2048]{1,0:T(8,128)(2,1)S(1)} fusion(bf16[2048,1920]{1,0:T(8,128)(2,1)S(1)} %copy-done.51, bf16[1024,640]{0,1:T(8,128)(2,1)S(1)} %get-tuple-element.137, bf16[1024,640]{0,1:T(8,128)(2,1)S(1)} %get-tuple-element.136), kind=kOutput, calls=%fused_computation.22 | convolution fusion | flops 5376049152 | bytes 12058624 | tf_op jit(solution)/shard_map/dot_general | solution.py:44
  267.0 2.5 fusion.95
  269.6 4.9 convolution_convert_fusion.3
  274.5 3.6 pad_maximum_fusion.3
  278.0 4.3 fusion.9
  282.3 4.4 all-to-all-start.3
  287.0 7.8 %convolution_convert_fusion.1 = bf16[1024,2048]{1,0:T(8,128)(2,1)} fusion(bf16[1024,640]{0,1:T(8,128)(2,1)} %copy-done.53, bf16[2048,1920]{1,0:T(8,128)(2,1)} %all-gather.4.cloned.1.call-done), kind=kOutput, calls=%fused_computation.23 | convolution fusion | flops 2686451712 | bytes 8126464 | tf_op jit(solution)/shard_map/dot_general | solution.py:44
  294.8 7.4 %convolution_convert_fusion = bf16[2048,1280]{1,0:T(8,128)(2,1)} fusion(bf16[1024,2048]{1,0:T(8,128)(2,1)S(1)} %bitcast.255, bf16[1024,1280]{0,1:T(8,128)(2,1)S(1)} %copy-done.21), kind=kOutput, calls=%fused_computation.5 | convolution fusion | flops 5371330560 | bytes 12058624 | tf_op jit(solution)/shard_map/dot_general | solution.py:485
  302.2 10.3 %all-to-all-done.3 = bf16[4,128,2048]{2,1,0:T(8,128)(2,1)} async-done(((bf16[4,128,2048]{2,1,0:T(8,128)(2,1)}), bf16[4,128,2048]{2,1,0:T(8,128)(2,1)}, u32[]{:S(2)}, u32[]{:S(2)}) %all-to-all-start.3) | async-done | bytes 2097184 | tf_op jit(solution)/shard_map/all_to_all | solution.py:374
  317.2 2.5 fusion.94
  319.7 3.7 convolution_convert_fusion.11
  324.3 4.1 all-to-all-start.4
  335.8 3.7 fusion.8
  339.5 16.4 %all-to-all-done.4 = bf16[4,256,256]{2,1,0:T(8,128)(2,1)} async-done(((bf16[4,256,256]{2,1,0:T(8,128)(2,1)}), bf16[4,256,256]{2,1,0:T(8,128)(2,1)}, u32[]{:S(2)}, u32[]{:S(2)}) %all-to-all-start.4) | async-done | bytes 524320 | tf_op jit(solution)/shard_map/all_to_all | solution.py:374
  355.9 4.7 all-to-all-start.5
  366.2 17.6 %attend_back.1 = (bf16[1024,768]{1,0:T(8,128)(2,1)}, f32[2,2,1024]{2,1,0:T(2,128)}, f32[2,2,512]{2,1,0:T(2,128)}) custom-call(s32[1]{0:T(128)} %bitcast.here_ref, bf16[1024,768]{1,0:T(8,128)(2,1)} %convolution_convert_fusion.4.q_in.k_in.v_in, bf16[1024,768]{1,0:T(8,128)(2,1)} %convolution_convert_fusion.4.q_in.k_in.v_in, ...), custom_call_target="tpu_custom_call" | custom-call | flops 10737418240 | bytes 2097152 | tf_op jit(solution)/shard_map/attend_back/pallas_call | solution.py:270
  383.8 3.2 all-to-all-done.5
  387.0 5.9 %convolution_convert_fusion.2 = bf16[1024,2048]{1,0:T(8,128)(2,1)S(1)} fusion(bf16[1024,768]{1,0:T(8,128)(2,1)} %get-tuple-element.66, bf16[2048,768]{1,0:T(8,128)(2,1)} %bitcast.259), kind=kOutput, calls=%fused_computation.24 | convolution fusion | flops 3223322624 | bytes 8912896 | tf_op jit(solution)/shard_map/dot_general | solution.py:44
  392.9 2.3 fusion.93
  395.7 2.1 fusion.38
  399.3 10.1 %collective-permute-done.39 = bf16[2,512,512]{2,1,0:T(8,128)(2,1)} collective-permute-done((bf16[2,512,512]{2,1,0:T(8,128)(2,1)}, bf16[2,512,512]{2,1,0:T(8,128)(2,1)}, u32[]{:S(2)}, u32[]{:S(2)}) %collective-permute-start.39) | collective-permute-done | bytes 1048608 | tf_op jit(solution)/shard_map/ppermute | solution.py:330
  409.4 2.1 fusion.39
  413.0 2.7 fusion.58
  418.6 3.1 collective-permute-done.40
  421.7 2.6 fusion.37
  424.3 3.8 fusion.7
  428.1 4.5 all-to-all-start.6
  432.6 2.9 convolution_convert_fusion.8
  442.9 9.7 %collective-permute-done.44 = bf16[2,512,384]{2,1,0:T(8,128)(2,1)S(1)} collective-permute-done((bf16[2,512,384]{2,1,0:T(8,128)(2,1)S(1)}, bf16[2,512,384]{2,1,0:T(8,128)(2,1)S(1)}, u32[]{:S(2)}, u32[]{:S(2)}) %collective-permute-start.44) | collective-permute-done | bytes 786464 | tf_op jit(solution)/shard_map/ppermute | solution.py:330
  453.8 5.1 collective-permute-done.42
  463.1 3.7 collective-permute-done.43
  476.7 2.1 convert_reduce_fusion
  478.9 4.4 all-to-all-start.7
  483.3 2.2 collective-permute-start.31
  490.7 5.1 collective-permute-done.31
  502.7 3.2 collective-permute-start.35
  507.4 2.3 collective-permute-done.34
  511.7 3.5 collective-permute-start.38
  516.5 2.9 convert_bitcast_fusion
  (425 shorter events, 157.1 us)
Async XLA Ops:
  7.2 74.8 %all-gather.6.cloned.1.call-start = ((), (), s32[]{:S(2)}) async-start(), calls=%async_computation.13 | async-start | bytes 2621440 | tf_op jit(solution)/shard_map/all_gather | solution.py:518
  8.7 21.6 %collective-permute-start.3 = (bf16[1,512]{1,0:T(2,128)(2,1)S(1)}, bf16[1,512]{1,0:T(2,128)(2,1)S(1)}, u32[]{:S(2)}, u32[]{:S(2)}) collective-permute-start(bf16[1,512]{1,0:T(2,128)(2,1)S(1)} %reshape.301), channel_id=1, source_target_pairs={{0,6},{2,0},{4,2},{6,4},{1,7},{3,1},{5,3},{7,5},{8,14},{10,8},{12,... | collective-permute-start | bytes 3080 | tf_op jit(solution)/shard_map/ppermute | solution.py:301
  13.8 16.4 %collective-permute-start.2 = (bf16[1,512]{1,0:T(2,128)(2,1)S(1)}, bf16[1,512]{1,0:T(2,128)(2,1)S(1)}, u32[]{:S(2)}, u32[]{:S(2)}) collective-permute-start(bf16[1,512]{1,0:T(2,128)(2,1)S(1)} %reshape.301), channel_id=1, source_target_pairs={{0,4},{2,6},{4,0},{6,2},{1,5},{3,7},{5,1},{7,3},{8,12},{10,14},{12... | collective-permute-start | bytes 3080 | tf_op jit(solution)/shard_map/ppermute | solution.py:301
  13.8 16.4 %collective-permute-start.1 = (bf16[1,512]{1,0:T(2,128)(2,1)S(1)}, bf16[1,512]{1,0:T(2,128)(2,1)S(1)}, u32[]{:S(2)}, u32[]{:S(2)}) collective-permute-start(bf16[1,512]{1,0:T(2,128)(2,1)S(1)} %reshape.301), channel_id=1, source_target_pairs={{0,2},{2,4},{4,6},{6,0},{1,3},{3,5},{5,7},{7,1},{8,10},{10,12},{12... | collective-permute-start | bytes 3080 | tf_op jit(solution)/shard_map/ppermute | solution.py:301
  32.6 15.4 %collective-permute-start.4 = (bf16[128,1920]{1,0:T(8,128)(2,1)}, bf16[128,1920]{1,0:T(8,128)(2,1)}, u32[]{:S(2)}, u32[]{:S(2)}) collective-permute-start(bf16[128,1920]{1,0:T(8,128)(2,1)} %pad_maximum_fusion.12), channel_id=1, source_target_pairs={{0,8},{8,16},{16,24},{24,0},{1,9},{9,17},{17,25},{25,1},{2,10},{10... | collective-permute-start | bytes 1474568 | tf_op jit(solution)/shard_map/ppermute | solution.py:301
  34.1 66.2 %all-to-all-start = ((bf16[4,128,1792]{2,1,0:T(8,128)(2,1)}), bf16[4,128,1792]{2,1,0:T(8,128)(2,1)S(1)}, u32[]{:S(2)}, u32[]{:S(2)}) async-start(bf16[4,128,1792]{2,1,0:T(8,128)(2,1)} %pad_maximum_fusion.5), calls=%async_computation | async-start | bytes 3670016 | tf_op jit(solution)/shard_map/all_to_all | solution.py:374
  38.1 205.7 %all-gather.4.cloned.1.call-start = ((), (), s32[]{:S(2)}) async-start(), calls=%async_computation.10 | async-start | bytes 9830400 | tf_op jit(solution)/shard_map/all_gather | solution.py:545
  39.0 17.5 %collective-permute-start.5 = (bf16[128,1920]{1,0:T(8,128)(2,1)}, bf16[128,1920]{1,0:T(8,128)(2,1)}, u32[]{:S(2)}, u32[]{:S(2)}) collective-permute-start(bf16[128,1920]{1,0:T(8,128)(2,1)} %pad_maximum_fusion.13), channel_id=1, source_target_pairs={{0,16},{8,24},{16,0},{24,8},{1,17},{9,25},{17,1},{25,9},{2,18},{10... | collective-permute-start | bytes 1474568 | tf_op jit(solution)/shard_map/ppermute | solution.py:301
  41.3 15.1 %collective-permute-start.6 = (bf16[128,1920]{1,0:T(8,128)(2,1)}, bf16[128,1920]{1,0:T(8,128)(2,1)S(1)}, u32[]{:S(2)}, u32[]{:S(2)}) collective-permute-start(bf16[128,1920]{1,0:T(8,128)(2,1)} %pad_maximum_fusion.14), channel_id=1, source_target_pairs={{0,24},{8,0},{16,8},{24,16},{1,25},{9,1},{17,9},{25,17},{2,26},{10... | collective-permute-start | bytes 1474568 | tf_op jit(solution)/shard_map/ppermute | solution.py:301
  44.0 27.0 %copy-start.40 = (s32[1,1,4,256]{3,1,2,0:T(1,128)}, s32[1,1,4,256]{3,1,2,0:T(1,128)S(1)}, u32[]{:S(2)}) copy-start(s32[1,1,4,256]{3,1,2,0:T(1,128)S(1)} %copy.170) | copy-start | bytes 12292
  56.4 47.7 %collective-permute-start.15 = (bf16[4,256]{1,0:T(4,128)(2,1)S(1)}, bf16[4,256]{1,0:T(4,128)(2,1)S(1)}, u32[]{:S(2)}, u32[]{:S(2)}) collective-permute-start(bf16[4,256]{1,0:T(4,128)(2,1)S(1)} %slice.423), channel_id=1, source_target_pairs={{0,16},{8,24},{16,0},{24,8},{1,17},{9,25},{17,1},{25,9},{2,18},{10... | collective-permute-start | bytes 6152 | tf_op jit(solution)/shard_map/ppermute | solution.py:301
  58.0 14.9 %collective-permute-start.14 = (bf16[4,256]{1,0:T(4,128)(2,1)S(1)}, bf16[4,256]{1,0:T(4,128)(2,1)S(1)}, u32[]{:S(2)}, u32[]{:S(2)}) collective-permute-start(bf16[4,256]{1,0:T(4,128)(2,1)S(1)} %slice.423), channel_id=1, source_target_pairs={{0,8},{8,16},{16,24},{24,0},{1,9},{9,17},{17,25},{25,1},{2,10},{10... | collective-permute-start | bytes 6152 | tf_op jit(solution)/shard_map/ppermute | solution.py:301
  63.9 18.1 %collective-permute-start.9 = (bf16[128,2048]{1,0:T(8,128)(2,1)}, bf16[128,2048]{1,0:T(8,128)(2,1)S(1)}, u32[]{:S(2)}, u32[]{:S(2)}) collective-permute-start(bf16[128,2048]{1,0:T(8,128)(2,1)} %constant_dynamic-update-slice_fusion), channel_id=1, source_target_pairs={{0,24},{8,0},{16,8},{24,16},{1,25},{9,1},{17,9},{25,17},{2,26},{10... | collective-permute-start | bytes 1572872 | tf_op jit(solution)/shard_map/ppermute | solution.py:301
  64.7 29.5 %collective-permute-start.8 = (bf16[128,2048]{1,0:T(8,128)(2,1)}, bf16[128,2048]{1,0:T(8,128)(2,1)S(1)}, u32[]{:S(2)}, u32[]{:S(2)}) collective-permute-start(bf16[128,2048]{1,0:T(8,128)(2,1)} %constant_dynamic-update-slice_fusion), channel_id=1, source_target_pairs={{0,16},{8,24},{16,0},{24,8},{1,17},{9,25},{17,1},{25,9},{2,18},{10... | collective-permute-start | bytes 1572872 | tf_op jit(solution)/shard_map/ppermute | solution.py:301
  65.4 28.8 %collective-permute-start.7 = (bf16[128,2048]{1,0:T(8,128)(2,1)}, bf16[128,2048]{1,0:T(8,128)(2,1)S(1)}, u32[]{:S(2)}, u32[]{:S(2)}) collective-permute-start(bf16[128,2048]{1,0:T(8,128)(2,1)} %constant_dynamic-update-slice_fusion), channel_id=1, source_target_pairs={{0,8},{8,16},{16,24},{24,0},{1,9},{9,17},{17,25},{25,1},{2,10},{10... | collective-permute-start | bytes 1572872 | tf_op jit(solution)/shard_map/ppermute | solution.py:301
  82.1 49.9 %collective-permute-start = (bf16[4,128,2048]{2,1,0:T(8,128)(2,1)}, bf16[4,128,2048]{2,1,0:T(8,128)(2,1)}, u32[]{:S(2)}, u32[]{:S(2)}) collective-permute-start(bf16[4,128,2048]{2,1,0:T(8,128)(2,1)} %bitcast.265), channel_id=1, source_target_pairs={{0,1},{1,0},{2,3},{3,2},{4,5},{5,4},{6,7},{7,6},{8,9},{9,8},{10,11... | collective-permute-start | bytes 6291464 | tf_op jit(solution)/shard_map/ppermute | solution.py:301
  82.1 18.2 %copy-start.29 = (bf16[128,2048]{1,0:T(8,128)(2,1)}, bf16[128,2048]{1,0:T(8,128)(2,1)S(1)}, u32[]{:S(2)}) copy-start(bf16[128,2048]{1,0:T(8,128)(2,1)S(1)} %collective-permute-done.9) | copy-start | bytes 1572868
  82.1 22.0 %collective-permute-start.16 = (bf16[4,256]{1,0:T(4,128)(2,1)S(1)}, bf16[4,256]{1,0:T(4,128)(2,1)S(1)}, u32[]{:S(2)}, u32[]{:S(2)}) collective-permute-start(bf16[4,256]{1,0:T(4,128)(2,1)S(1)} %slice.423), channel_id=1, source_target_pairs={{0,24},{8,0},{16,8},{24,16},{1,25},{9,1},{17,9},{25,17},{2,26},{10... | collective-permute-start | bytes 6152 | tf_op jit(solution)/shard_map/ppermute | solution.py:301
  101.2 19.4 %collective-permute-start.10 = (bf16[512,768]{1,0:T(8,128)(2,1)}, bf16[512,768]{1,0:T(8,128)(2,1)S(1)}, u32[]{:S(2)}, u32[]{:S(2)}) collective-permute-start(bf16[512,768]{1,0:T(8,128)(2,1)} %slice.420), channel_id=1, source_target_pairs={{0,8},{8,0},{16,24},{24,16},{1,9},{9,1},{17,25},{25,17},{2,10},{10... | collective-permute-start | bytes 2359304 | tf_op jit(solution)/shard_map/ppermute | solution.py:330
  102.6 19.5 %collective-permute-start.11 = (bf16[512,768]{1,0:T(8,128)(2,1)}, bf16[512,768]{1,0:T(8,128)(2,1)S(1)}, u32[]{:S(2)}, u32[]{:S(2)}) collective-permute-start(bf16[512,768]{1,0:T(8,128)(2,1)} %slice.420), channel_id=1, source_target_pairs={{0,16},{8,24},{16,0},{24,8},{1,17},{9,25},{17,1},{25,9},{2,18},{10... | collective-permute-start | bytes 2359304 | tf_op jit(solution)/shard_map/ppermute | solution.py:330
  104.2 31.8 %copy-start.38 = (f32[1,4,4,128]{3,0,2,1:T(1,128)}, f32[1,4,4,128]{3,0,2,1:T(1,128)S(1)}, u32[]{:S(2)}) copy-start(f32[1,4,4,128]{3,0,2,1:T(1,128)S(1)} %get-tuple-element.181) | copy-start | bytes 24580
  120.6 10.0 %collective-permute-start.12 = (bf16[256,768]{1,0:T(8,128)(2,1)S(1)}, bf16[256,768]{1,0:T(8,128)(2,1)S(1)}, u32[]{:S(2)}, u32[]{:S(2)}) collective-permute-start(bf16[256,768]{1,0:T(8,128)(2,1)S(1)} %slice.532), channel_id=1, source_target_pairs={{0,16},{8,24},{16,0},{24,8},{1,17},{9,25},{17,1},{25,9},{2,18},{10... | collective-permute-start | bytes 1179656 | tf_op jit(solution)/shard_map/ppermute | solution.py:330
  122.2 9.7 %collective-permute-start.13 = (bf16[256,768]{1,0:T(8,128)(2,1)S(1)}, bf16[256,768]{1,0:T(8,128)(2,1)S(1)}, u32[]{:S(2)}, u32[]{:S(2)}) collective-permute-start(bf16[256,768]{1,0:T(8,128)(2,1)S(1)} %slice.533), channel_id=1, source_target_pairs={{0,8},{8,0},{16,24},{24,16},{1,9},{9,1},{17,25},{25,17},{2,10},{10... | collective-permute-start | bytes 1179656 | tf_op jit(solution)/shard_map/ppermute | solution.py:330
  142.6 28.5 %collective-permute-start.17 = (bf16[512,1024]{1,0:T(8,128)(2,1)}, bf16[512,1024]{1,0:T(8,128)(2,1)}, u32[]{:S(2)}, u32[]{:S(2)}) collective-permute-start(bf16[512,1024]{1,0:T(8,128)(2,1)} %slice.428), channel_id=1, source_target_pairs={{0,8},{8,0},{16,24},{24,16},{1,9},{9,1},{17,25},{25,17},{2,10},{10... | collective-permute-start | bytes 3145736 | tf_op jit(solution)/shard_map/ppermute | solution.py:330
  144.3 30.1 %collective-permute-start.18 = (bf16[512,1024]{1,0:T(8,128)(2,1)}, bf16[512,1024]{1,0:T(8,128)(2,1)}, u32[]{:S(2)}, u32[]{:S(2)}) collective-permute-start(bf16[512,1024]{1,0:T(8,128)(2,1)} %slice.428), channel_id=1, source_target_pairs={{0,16},{8,24},{16,0},{24,8},{1,17},{9,25},{17,1},{25,9},{2,18},{10... | collective-permute-start | bytes 3145736 | tf_op jit(solution)/shard_map/ppermute | solution.py:330
  161.8 33.7 %all-to-all-start.1 = ((bf16[4,256,256]{1,2,0:T(8,128)(2,1)}), bf16[4,256,256]{1,2,0:T(8,128)(2,1)S(1)}, u32[]{:S(2)}, u32[]{:S(2)}) async-start(bf16[4,256,256]{1,2,0:T(8,128)(2,1)} %copy.142), calls=%async_computation.1 | async-start | bytes 1048576 | tf_op jit(solution)/shard_map/all_to_all | solution.py:374
  165.3 200.9 %reduce-scatter.3.cloned.1.call-start = ((), (), s32[]{:S(2)}) async-start(), calls=%async_computation.11 | async-start | bytes 3276800 | tf_op jit(solution)/shard_map/reduce_scatter | solution.py:590
  172.6 11.4 %collective-permute-start.19 = (bf16[256,1024]{1,0:T(8,128)(2,1)S(1)}, bf16[256,1024]{1,0:T(8,128)(2,1)S(1)}, u32[]{:S(2)}, u32[]{:S(2)}) collective-permute-start(bf16[256,1024]{1,0:T(8,128)(2,1)S(1)} %slice.536), channel_id=1, source_target_pairs={{0,16},{8,24},{16,0},{24,8},{1,17},{9,25},{17,1},{25,9},{2,18},{10... | collective-permute-start | bytes 1572872 | tf_op jit(solution)/shard_map/ppermute | solution.py:330
  175.4 11.0 %collective-permute-start.20 = (bf16[256,1024]{1,0:T(8,128)(2,1)S(1)}, bf16[256,1024]{1,0:T(8,128)(2,1)S(1)}, u32[]{:S(2)}, u32[]{:S(2)}) collective-permute-start(bf16[256,1024]{1,0:T(8,128)(2,1)S(1)} %slice.537), channel_id=1, source_target_pairs={{0,8},{8,0},{16,24},{24,16},{1,9},{9,1},{17,25},{25,17},{2,10},{10... | collective-permute-start | bytes 1572872 | tf_op jit(solution)/shard_map/ppermute | solution.py:330
  199.3 2.0 collective-permute-start.21
  199.5 4.8 collective-permute-start.22
  201.7 113.6 %copy-start.44 = (f32[128]{0:T(128)}, f32[128]{0:T(128)S(1)}, u32[]{:S(2)}) copy-start(f32[128]{0:T(128)S(1)} %add_rsqrt_fusion.2) | copy-start | bytes 1540
  235.4 4.2 collective-permute-start.23
  269.5 8.5 %collective-permute-start.24 = (bf16[4,128,2048]{2,1,0:T(8,128)(2,1)}, bf16[4,128,2048]{2,1,0:T(8,128)(2,1)}, u32[]{:S(2)}, u32[]{:S(2)}) collective-permute-start(bf16[4,128,2048]{2,1,0:T(8,128)(2,1)} %bitcast.45), channel_id=1, source_target_pairs={{0,1},{1,0},{2,3},{3,2},{4,5},{5,4},{6,7},{7,6},{8,9},{9,8},{10,11... | collective-permute-start | bytes 6291464 | tf_op jit(solution)/shard_map/ppermute | solution.py:301
  282.3 30.2 %all-to-all-start.3 = ((bf16[4,128,2048]{2,1,0:T(8,128)(2,1)}), bf16[4,128,2048]{2,1,0:T(8,128)(2,1)}, u32[]{:S(2)}, u32[]{:S(2)}) async-start(bf16[4,128,2048]{2,1,0:T(8,128)(2,1)} %fusion.9), calls=%async_computation.3 | async-start | bytes 4194304 | tf_op jit(solution)/shard_map/all_to_all | solution.py:374
  286.7 181.1 %reduce-scatter.5.cloned.1.call-start = ((), (), s32[]{:S(2)}) async-start(), calls=%async_computation.12 | async-start | bytes 6553600 | tf_op jit(solution)/shard_map/reduce_scatter | solution.py:592
  316.0 3.7 collective-permute-start.25
  319.7 16.1 %collective-permute-start.26 = (bf16[4,128,2048]{2,1,0:T(8,128)(2,1)}, bf16[4,128,2048]{2,1,0:T(8,128)(2,1)}, u32[]{:S(2)}, u32[]{:S(2)}) collective-permute-start(bf16[4,128,2048]{2,1,0:T(8,128)(2,1)} %bitcast.47), channel_id=1, source_target_pairs={{0,1},{1,0},{2,3},{3,2},{4,5},{5,4},{6,7},{7,6},{8,9},{9,8},{10,11... | collective-permute-start | bytes 6291464 | tf_op jit(solution)/shard_map/ppermute | solution.py:301
  324.3 31.7 %all-to-all-start.4 = ((bf16[4,256,256]{2,1,0:T(8,128)(2,1)}), bf16[4,256,256]{2,1,0:T(8,128)(2,1)}, u32[]{:S(2)}, u32[]{:S(2)}) async-start(bf16[4,256,256]{2,1,0:T(8,128)(2,1)} %bitcast.264), calls=%async_computation.4 | async-start | bytes 1048576 | tf_op jit(solution)/shard_map/all_to_all | solution.py:374
  334.3 31.9 %collective-permute-start.27 = (bf16[2,512,512]{2,1,0:T(8,128)(2,1)}, bf16[2,512,512]{2,1,0:T(8,128)(2,1)}, u32[]{:S(2)}, u32[]{:S(2)}) collective-permute-start(bf16[2,512,512]{2,1,0:T(8,128)(2,1)} %pad_maximum_fusion.8), channel_id=1, source_target_pairs={{0,16},{8,24},{16,0},{24,8},{1,17},{9,25},{17,1},{25,9},{2,18},{10... | collective-permute-start | bytes 3145736 | tf_op jit(solution)/shard_map/ppermute | solution.py:330
  355.9 31.0 %all-to-all-start.5 = ((bf16[4,128,2048]{2,1,0:T(8,128)(2,1)}), bf16[4,128,2048]{2,1,0:T(8,128)(2,1)}, u32[]{:S(2)}, u32[]{:S(2)}) async-start(bf16[4,128,2048]{2,1,0:T(8,128)(2,1)} %fusion.8), calls=%async_computation.5 | async-start | bytes 4194304 | tf_op jit(solution)/shard_map/all_to_all | solution.py:374
  364.2 45.2 %collective-permute-start.39 = (bf16[2,512,512]{2,1,0:T(8,128)(2,1)}, bf16[2,512,512]{2,1,0:T(8,128)(2,1)}, u32[]{:S(2)}, u32[]{:S(2)}) collective-permute-start(bf16[2,512,512]{2,1,0:T(8,128)(2,1)} %pad_maximum_fusion.9), channel_id=1, source_target_pairs={{0,8},{8,0},{16,24},{24,16},{1,9},{9,1},{17,25},{25,17},{2,10},{10... | collective-permute-start | bytes 3145736 | tf_op jit(solution)/shard_map/ppermute | solution.py:330
  395.2 29.1 %collective-permute-start.28 = (bf16[4,128,2048]{2,1,0:T(8,128)(2,1)}, bf16[4,128,2048]{2,1,0:T(8,128)(2,1)}, u32[]{:S(2)}, u32[]{:S(2)}) collective-permute-start(bf16[4,128,2048]{2,1,0:T(8,128)(2,1)} %bitcast.54), channel_id=1, source_target_pairs={{0,1},{1,0},{2,3},{3,2},{4,5},{5,4},{6,7},{7,6},{8,9},{9,8},{10,11... | collective-permute-start | bytes 6291464 | tf_op jit(solution)/shard_map/ppermute | solution.py:301
  397.8 17.9 %copy-start.43 = (f32[2,2,512]{2,1,0:T(2,128)S(1)}, f32[2,2,512]{2,1,0:T(2,128)}, u32[]{:S(2)}) copy-start(f32[2,2,512]{2,1,0:T(2,128)} %get-tuple-element.65) | copy-start | bytes 24580
  397.8 17.9 %copy-start.42 = (f32[2,2,1024]{2,1,0:T(2,128)S(1)}, f32[2,2,1024]{2,1,0:T(2,128)}, u32[]{:S(2)}) copy-start(f32[2,2,1024]{2,1,0:T(2,128)} %get-tuple-element.64) | copy-start | bytes 49156
  397.8 20.8 %collective-permute-start.41 = (bf16[512,512]{1,0:T(8,128)(2,1)}, bf16[512,512]{1,0:T(8,128)(2,1)}, u32[]{:S(2)}, u32[]{:S(2)}) collective-permute-start(bf16[512,512]{1,0:T(8,128)(2,1)} %fusion.38), channel_id=1, source_target_pairs={{0,8},{8,0},{16,24},{24,16},{1,9},{9,1},{17,25},{25,17},{2,10},{10... | collective-permute-start | bytes 1572872 | tf_op jit(solution)/shard_map/ppermute | solution.py:330
  411.6 10.2 %collective-permute-start.40 = (bf16[512,512]{1,0:T(8,128)(2,1)}, bf16[512,512]{1,0:T(8,128)(2,1)}, u32[]{:S(2)}, u32[]{:S(2)}) collective-permute-start(bf16[512,512]{1,0:T(8,128)(2,1)} %fusion.39), channel_id=1, source_target_pairs={{0,16},{8,24},{16,0},{24,8},{1,17},{9,25},{17,1},{25,9},{2,18},{10... | collective-permute-start | bytes 1572872 | tf_op jit(solution)/shard_map/ppermute | solution.py:330
  428.1 48.6 %all-to-all-start.6 = ((bf16[4,128,2048]{2,1,0:T(8,128)(2,1)}), bf16[4,128,2048]{2,1,0:T(8,128)(2,1)}, u32[]{:S(2)}, u32[]{:S(2)}) async-start(bf16[4,128,2048]{2,1,0:T(8,128)(2,1)} %fusion.7), calls=%async_computation.7 | async-start | bytes 4194304 | tf_op jit(solution)/shard_map/all_to_all | solution.py:374
  437.3 15.3 %collective-permute-start.44 = (bf16[2,512,384]{2,1,0:T(8,128)(2,1)S(1)}, bf16[2,512,384]{2,1,0:T(8,128)(2,1)S(1)}, u32[]{:S(2)}, u32[]{:S(2)}) collective-permute-start(bf16[2,512,384]{2,1,0:T(8,128)(2,1)S(1)} %pad_maximum_fusion.11), channel_id=1, source_target_pairs={{0,16},{8,24},{16,0},{24,8},{1,17},{9,25},{17,1},{25,9},{2,18},{10... | collective-permute-start | bytes 2359304 | tf_op jit(solution)/shard_map/ppermute | solution.py:330
  440.1 18.8 %collective-permute-start.42 = (bf16[2,512,384]{2,1,0:T(8,128)(2,1)S(1)}, bf16[2,512,384]{2,1,0:T(8,128)(2,1)S(1)}, u32[]{:S(2)}, u32[]{:S(2)}) collective-permute-start(bf16[2,512,384]{2,1,0:T(8,128)(2,1)S(1)} %pad_maximum_fusion.10), channel_id=1, source_target_pairs={{0,8},{8,0},{16,24},{24,16},{1,9},{9,1},{17,25},{25,17},{2,10},{10... | collective-permute-start | bytes 2359304 | tf_op jit(solution)/shard_map/ppermute | solution.py:330
  452.8 10.3 %collective-permute-start.45 = (bf16[512,384]{1,0:T(8,128)(2,1)S(1)}, bf16[512,384]{1,0:T(8,128)(2,1)S(1)}, u32[]{:S(2)}, u32[]{:S(2)}) collective-permute-start(bf16[512,384]{1,0:T(8,128)(2,1)S(1)} %fusion.49), channel_id=1, source_target_pairs={{0,8},{8,0},{16,24},{24,16},{1,9},{9,1},{17,25},{25,17},{2,10},{10... | collective-permute-start | bytes 1179656 | tf_op jit(solution)/shard_map/ppermute | solution.py:330
  459.0 7.8 %collective-permute-start.43 = (bf16[512,384]{1,0:T(8,128)(2,1)S(1)}, bf16[512,384]{1,0:T(8,128)(2,1)S(1)}, u32[]{:S(2)}, u32[]{:S(2)}) collective-permute-start(bf16[512,384]{1,0:T(8,128)(2,1)S(1)} %fusion.50), channel_id=1, source_target_pairs={{0,16},{8,24},{16,0},{24,8},{1,17},{9,25},{17,1},{25,9},{2,18},{10... | collective-permute-start | bytes 1179656 | tf_op jit(solution)/shard_map/ppermute | solution.py:330
  472.1 13.4 %collective-permute-start.29 = (bf16[128,1920]{1,0:T(8,128)(2,1)}, bf16[128,1920]{1,0:T(8,128)(2,1)}, u32[]{:S(2)}, u32[]{:S(2)}) collective-permute-start(bf16[128,1920]{1,0:T(8,128)(2,1)} %get-tuple-element.152), channel_id=1, source_target_pairs={{0,8},{8,16},{16,24},{24,0},{1,9},{9,17},{17,25},{25,1},{2,10},{10... | collective-permute-start | bytes 1474568 | tf_op jit(solution)/shard_map/ppermute | solution.py:301
  474.6 14.2 %collective-permute-start.30 = (bf16[128,1920]{1,0:T(8,128)(2,1)}, bf16[128,1920]{1,0:T(8,128)(2,1)}, u32[]{:S(2)}, u32[]{:S(2)}) collective-permute-start(bf16[128,1920]{1,0:T(8,128)(2,1)} %get-tuple-element.151), channel_id=1, source_target_pairs={{0,16},{8,24},{16,0},{24,8},{1,17},{9,25},{17,1},{25,9},{2,18},{10... | collective-permute-start | bytes 1474568 | tf_op jit(solution)/shard_map/ppermute | solution.py:301
  478.8 17.7 %copy-start.39 = (f32[1,4,4,128]{3,0,2,1:T(1,128)S(1)}, f32[1,4,4,128]{3,0,2,1:T(1,128)}, u32[]{:S(2)}) copy-start(f32[1,4,4,128]{3,0,2,1:T(1,128)} %copy-done.38) | copy-start | bytes 24580
  478.9 52.1 %all-to-all-start.7 = ((bf16[4,128,1792]{2,1,0:T(8,128)(2,1)}), bf16[4,128,1792]{2,1,0:T(8,128)(2,1)}, u32[]{:S(2)}, u32[]{:S(2)}) async-start(bf16[4,128,1792]{2,1,0:T(8,128)(2,1)} %pad_maximum_fusion.6), calls=%async_computation.9 | async-start | bytes 3670016 | tf_op jit(solution)/shard_map/all_to_all | solution.py:374
  483.3 12.4 %collective-permute-start.31 = (bf16[128,1920]{1,0:T(8,128)(2,1)}, bf16[128,1920]{1,0:T(8,128)(2,1)S(1)}, u32[]{:S(2)}, u32[]{:S(2)}) collective-permute-start(bf16[128,1920]{1,0:T(8,128)(2,1)} %get-tuple-element.150), channel_id=1, source_target_pairs={{0,24},{8,0},{16,8},{24,16},{1,25},{9,1},{17,9},{25,17},{2,26},{10... | collective-permute-start | bytes 1474568 | tf_op jit(solution)/shard_map/ppermute | solution.py:301
  501.2 1.3 collective-permute-start.32
  502.7 4.7 collective-permute-start.35
  505.8 3.8 collective-permute-start.34
  506.5 4.7 collective-permute-start.33
  511.7 14.4 %collective-permute-start.38 = (f32[41,128]{1,0:T(8,128)S(1)}, f32[41,128]{1,0:T(8,128)S(1)}, u32[]{:S(2)}, u32[]{:S(2)}) collective-permute-start(f32[41,128]{1,0:T(8,128)S(1)} %reduce_sum.197), channel_id=1, source_target_pairs={{0,6},{2,0},{4,2},{6,4},{1,7},{3,1},{5,3},{7,5},{8,14},{10,8},{12,... | collective-permute-start | bytes 62984 | tf_op jit(solution)/shard_map/ppermute | solution.py:301
  515.2 12.2 %collective-permute-start.37 = (f32[41,128]{1,0:T(8,128)S(1)}, f32[41,128]{1,0:T(8,128)S(1)}, u32[]{:S(2)}, u32[]{:S(2)}) collective-permute-start(f32[41,128]{1,0:T(8,128)S(1)} %reduce_sum.197), channel_id=1, source_target_pairs={{0,4},{2,6},{4,0},{6,2},{1,5},{3,7},{5,1},{7,3},{8,12},{10,14},{12... | collective-permute-start | bytes 62984 | tf_op jit(solution)/shard_map/ppermute | solution.py:301
  515.2 12.2 %collective-permute-start.36 = (f32[41,128]{1,0:T(8,128)S(1)}, f32[41,128]{1,0:T(8,128)S(1)}, u32[]{:S(2)}, u32[]{:S(2)}) collective-permute-start(f32[41,128]{1,0:T(8,128)S(1)} %reduce_sum.197), channel_id=1, source_target_pairs={{0,2},{2,4},{4,6},{6,0},{1,3},{3,5},{5,7},{7,1},{8,10},{10,12},{12... | collective-permute-start | bytes 62984 | tf_op jit(solution)/shard_map/ppermute | solution.py:301
  (47 other events, 287.6 us)
Sparse Core Ops, SparseCore 0:
  15.0 67.0 all-gather.5
  83.6 160.1 all-gather.3
  274.6 50.3 reduce-scatter.2
  327.2 98.6 reduce-scatter.4
